TPU v7x, 512 devices: a whole 4x4x16 slice. The times are simulated.
512 devices in a mesh: ctx: 32 (over z, core), pb: 16 (over y, x).
Axes of the slice: x: 4, y: 4, z: 16, core: 2. Of those that a mesh axis runs over, the one named last changes fastest.
Arguments:
- q_latent: bfloat16 [1024, 73728], P(('ctx', 'pb')), may hold values from -80 to 80
- kv_cache: bfloat16 [16384, 576], P('ctx'), may hold values from -6 to 6
- index_queries: bfloat16 [1024, 8192], P(('ctx', 'pb')), may hold values from -6 to 6
- index_weights: bfloat16 [1024, 64], P(('ctx', 'pb')), may hold values from -0.75 to 0.75
- index_keys: bfloat16 [16384, 128], P(('ctx', 'pb')), may hold values from -6 to 6
- q_blocks: int32 [1024, 32], P(('ctx', 'pb')), may hold values from 0 to 255, as said below
Outputs:
- attention: bfloat16 [1024, 65536], P(('ctx', 'pb'))
- index_scores: bfloat16 [1024, 16384], P(('ctx', 'pb'))
Inputs may be any that keep to these rules, and one draw needn't show every extreme that they name: `q_blocks`: each row names 32 different blocks, none after the block that holds pos of that row, and names both that block and block 0. Over the rows of one device (2 rows in a row of the ctx+pb order) at most 2 different named blocks lie in one context shard of 512 keys; every device names exactly 2 blocks of shard 0.
All inputs are finite; a program needn't handle non-finite values.
Results may differ from a plain program's by a relative error of at most 0.0037.
Values may be sent and summed in bfloat16 or wider, within the bound.
No kernel may reach another device: no remote copies, remote signals or barrier semaphores. Data moves between devices by JAX's collectives and lax.ppermute only.
A program may use at most 64 MiB of HBM per device.

v0:
```python
import jax
import jax.numpy as jnp
from jax import lax
from jax.sharding import PartitionSpec as P

DL = 512
BLK = 64


score_scale = 192.0 ** (-0.5)


def index_rows(query_rows, weight_rows, key_rows):
    row_count = weight_rows.shape[0]
    head_count = weight_rows.shape[1]
    row_width = query_rows.shape[1] // head_count
    group_size = 8
    group_total = head_count // group_size
    grouped_queries = query_rows.reshape(row_count, group_total, group_size, row_width).transpose(
        1, 0, 2, 3
    )
    grouped_weights = weight_rows.reshape(row_count, group_total, group_size).transpose(1, 0, 2)

    def add_group(total, pair):
        group_queries, group_weights = pair
        products = lax.dot_general(
            group_queries.reshape(row_count * group_size, row_width),
            key_rows,
            (((1,), (1,)), ((), ())),
            preferred_element_type=jnp.float32,
        )
        active = jnp.maximum(products * row_width ** (-0.5), 0.0).reshape(
            row_count, group_size, key_rows.shape[0]
        )
        return (
            total + jnp.sum(active * group_weights.astype(jnp.float32)[:, :, None], axis=1),
            None,
        )

    start_total = jnp.zeros((row_count, key_rows.shape[0]), jnp.float32)
    total, unused = lax.scan(add_group, start_total, (grouped_queries, grouped_weights))
    return total.astype(jnp.bfloat16)


def local(q_latent, kv_cache, index_queries, index_weights, index_keys, q_blocks):
    shard_count = lax.axis_size("ctx")
    group_count = lax.axis_size("pb")
    local_rows = q_latent.shape[0]
    shard_keys = kv_cache.shape[0]
    row_width = kv_cache.shape[1]
    head_count = q_latent.shape[1] // row_width
    chosen_count = q_blocks.shape[1]
    context = shard_keys * shard_count
    all_queries = local_rows * shard_count * group_count
    device_rank = lax.axis_index("ctx") * group_count + lax.axis_index("pb")
    positions = (
        context - all_queries + device_rank * local_rows + jnp.arange(local_rows, dtype=jnp.int32)
    )
    index_scores = index_rows(
        index_queries, index_weights, lax.all_gather(index_keys, ("ctx", "pb"), axis=0, tiled=True)
    )
    shard_blocks = shard_keys // BLK
    block_count = shard_blocks * shard_count
    capacity = max(2, (chosen_count + shard_count - 2) // (shard_count - 1))
    block_ids = jnp.arange(block_count, dtype=jnp.int32)
    chosen = q_blocks.reshape(local_rows * chosen_count)
    marked = (
        jnp.any(chosen[:, None] == block_ids[None, :], axis=0)
        .astype(jnp.int32)
        .reshape(shard_count, shard_blocks)
    )
    slot_rank = jnp.cumsum(marked, axis=1) - 1
    slot_match = (marked[:, None, :] == 1) & (
        slot_rank[:, None, :] == jnp.arange(capacity, dtype=jnp.int32)[None, :, None]
    )
    requests = jnp.sum(
        jnp.where(slot_match, jnp.arange(shard_blocks, dtype=jnp.int32)[None, None, :], 0), axis=2
    )
    cache_blocks = kv_cache.reshape(shard_blocks, BLK, row_width)
    block_rows = cache_blocks[
        lax.all_to_all(requests, "ctx", split_axis=0, concat_axis=0, tiled=True)
    ]
    fetched = lax.all_to_all(block_rows, "ctx", split_axis=0, concat_axis=0, tiled=True)
    fetched_rows = fetched.reshape(shard_count * capacity, BLK, row_width)
    block_slots = jnp.sum(
        jnp.where(
            q_blocks[:, :, None] == block_ids[None, None, :],
            slot_rank.reshape(block_count)[None, None, :],
            0,
        ),
        axis=2,
    )
    locations = q_blocks // shard_blocks * capacity + block_slots
    key_positions = (
        q_blocks[:, :, None] * BLK + jnp.arange(BLK, dtype=jnp.int32)[None, None, :]
    ).reshape(local_rows, chosen_count * BLK)
    query_heads = q_latent.reshape(local_rows, head_count, row_width)

    def attend_row(row_items):
        query_row, row_locations, row_positions, position = row_items
        key_rows = fetched_rows[row_locations].reshape(chosen_count * BLK, row_width)
        scores = jnp.dot(query_row, key_rows.T, preferred_element_type=jnp.float32) * score_scale
        masked = jnp.where(row_positions[None, :] <= position, scores, -1e30)
        highest = jnp.max(masked, axis=1, keepdims=True)
        weights = jnp.exp(masked - highest)
        rounded = (weights / jnp.sum(weights, axis=1, keepdims=True)).astype(jnp.bfloat16)
        attended = jnp.dot(rounded, key_rows[:, :DL], preferred_element_type=jnp.float32)
        return attended.astype(jnp.bfloat16).reshape(head_count * DL)

    attention = lax.map(attend_row, (query_heads, locations, key_positions, positions))
    return (attention, index_scores)


def solution(mesh):
    in_specs = (
        P(("ctx", "pb"), None),
        P("ctx", None),
        P(("ctx", "pb"), None),
        P(("ctx", "pb"), None),
        P(("ctx", "pb"), None),
        P(("ctx", "pb"), None),
    )
    out_specs = (P(("ctx", "pb"), None), P(("ctx", "pb"), None))
    return jax.shard_map(local, mesh=mesh, in_specs=in_specs, out_specs=out_specs, check_vma=False)
```

profile of v0, /device:TPU:1, one launch (start us, length us, event | category | flops | bytes accessed | tf_op | source)
XLA Modules:
  0.0 366.8 jit_solution(11005182235766075597)
XLA Ops:
  7.2 0.7 all-gather.2.cloned.1.call-update
  7.9 0.8 eq.55
  9.2 0.7 copy.24
  9.9 16.7 %all-to-all-start = ((s32[32,1,2]{2,1,0:T(1,128)}), s32[32,1,2]{2,1,0:T(1,128)S(1)}, u32[]{:S(2)}, u32[]{:S(2)}) async-start(s32[32,1,2]{2,1,0:T(1,128)} %copy.24), calls=%async_computation | async-start | bytes 32768 | tf_op jit(solution)/shard_map/all_to_all | solution.py:81
  26.8 0.9 select_reduce_fusion
  27.6 0.7 multiply_add_fusion
  28.6 1.4 copy.21
  30.0 1.3 reshape.128
  31.3 0.8 copy.33
  32.0 0.7 reshape.132
  32.8 5.6 %all-to-all-done = s32[32,1,2]{2,1,0:T(1,128)S(1)} async-done(((s32[32,1,2]{2,1,0:T(1,128)}), s32[32,1,2]{2,1,0:T(1,128)S(1)}, u32[]{:S(2)}, u32[]{:S(2)}) %all-to-all-start) | async-done | bytes 288 | tf_op jit(solution)/shard_map/all_to_all | solution.py:81
  38.7 3.5 gather_fusion.1
  42.2 6.6 %all-to-all-start.1 = ((bf16[32,2,64,576]{3,2,1,0:T(8,128)(2,1)}), bf16[32,2,64,576]{3,2,1,0:T(8,128)(2,1)}, u32[]{:S(2)}, u32[]{:S(2)}) async-start(bf16[32,2,64,576]{3,2,1,0:T(8,128)(2,1)} %bitcast.80), calls=%async_computation.1 | async-start | bytes 10485760 | tf_op jit(solution)/shard_map/all_to_all | solution.py:83
  48.8 261.0 %all-gather.2.cloned.1.call-done = bf16[16384,128]{1,0:T(8,128)(2,1)} async-done(((bf16[32,128]{1,0:T(8,128)(2,1)}), bf16[16384,128]{1,0:T(8,128)(2,1)}) %all-gather.2.cloned.1.call-update) | async-done | bytes 4194320 | tf_op jit(solution)/shard_map/all_gather | solution.py:60
  309.8 29.7 %while.22 = (s32[]{:T(128)}, f32[2,16384]{1,0:T(2,128)S(1)}, bf16[8,2,8,128]{3,2,0,1:T(8,128)(2,1)S(1)}, bf16[16384,128]{1,0:T(8,128)(2,1)}, bf16[8,2,8]{2,1,0:T(2,128)(2,1)S(1)}, /*index=5*/s32[]{:T(128)}, s32[]{:T(128)}) while((s32[]{:T(128)}, f32[2,16384]{1,0:T(2,128)S(1)}, bf16[8,2,8,128]{3,2,0,1:T(8,128)(2,1)S(1)}, ...), condition=%wide.region_10.11_spmd.clone, body=%wide.region_8.10_spmd.clone.sunk | while | flops 68190224 | bytes 4723903 | solution.py:41
  309.8 3.5 fusion.46
  313.3 0.2 select_add_fusion.2
  313.5 3.5 fusion.46
  317.0 0.2 select_add_fusion.2
  317.3 3.5 fusion.46
  320.7 0.2 select_add_fusion.2
  321.0 3.5 fusion.46
  324.5 0.2 select_add_fusion.2
  324.7 3.5 fusion.46
  328.4 3.5 fusion.46
  332.1 3.5 fusion.46
  335.6 0.2 select_add_fusion.2
  335.9 3.5 fusion.46
  339.3 0.2 select_add_fusion.2
  339.5 0.7 convert_element_type.33
  340.2 19.0 %while.21 = (s32[]{:T(128)}, bf16[2,65536]{1,0:T(2,128)(2,1)S(1)}, s32[2,2048]{1,0:T(2,128)S(1)}, s32[2]{0:T(128)S(1)}, bf16[2,128,576]{2,1,0:T(8,128)(2,1)S(1)}...) while((s32[]{:T(128)}, bf16[2,65536]{1,0:T(2,128)(2,1)S(1)}, ...), condition=%wide.region_7.8_spmd, body=%wide.region_4.0_spmd.sunk | while | flops 572590976 | bytes 13421693 | solution.py:110
  340.2 0.6 dynamic_slice.54
  340.8 0.7 compare_reduce_fusion.2
  341.5 3.5 gather_fusion
  345.1 1.1 fusion.41
  346.1 0.3 fusion.42
  346.4 0.5 fusion.43
  347.0 0.2 copy.35
  347.2 2.5 dynamic_update_slice.5
  349.7 0.6 dynamic_slice.54
  350.3 0.7 compare_reduce_fusion.2
  351.0 3.5 gather_fusion
  354.6 1.1 fusion.41
  355.6 0.3 fusion.42
  355.9 0.5 fusion.43
  356.5 0.2 copy.35
  356.7 2.5 dynamic_update_slice.5
  359.2 0.7 copy-done
  (41 shorter events, 1.7 us)
Async XLA Ops:
  7.2 302.6 %all-gather.2.cloned.1.call-start = ((), (), s32[]{:S(2)}) async-start(), calls=%async_computation.2 | async-start | bytes 4202496 | tf_op jit(solution)/shard_map/all_gather | solution.py:60
  9.9 28.5 %all-to-all-start = ((s32[32,1,2]{2,1,0:T(1,128)}), s32[32,1,2]{2,1,0:T(1,128)S(1)}, u32[]{:S(2)}, u32[]{:S(2)}) async-start(s32[32,1,2]{2,1,0:T(1,128)} %copy.24), calls=%async_computation | async-start | bytes 32768 | tf_op jit(solution)/shard_map/all_to_all | solution.py:81
  42.2 298.0 %all-to-all-start.1 = ((bf16[32,2,64,576]{3,2,1,0:T(8,128)(2,1)}), bf16[32,2,64,576]{3,2,1,0:T(8,128)(2,1)}, u32[]{:S(2)}, u32[]{:S(2)}) async-start(bf16[32,2,64,576]{3,2,1,0:T(8,128)(2,1)} %bitcast.80), calls=%async_computation.1 | async-start | bytes 10485760 | tf_op jit(solution)/shard_map/all_to_all | solution.py:83
  359.2 0.7 copy-start
Sparse Core Ops, SparseCore 0:
  12.4 297.3 all-gather.1
where the time goes:
time: 368 us; the launch traced here: 367 us
  waiting for transfers between devices  267 us (73%)
  matrix products  31.1 us (8%)
  local copies, waits for them, and re-layouts  24.4 us (7%)
  starting transfers between devices  23.4 us (6%)
  between operations  14.1 us (4%)
  other arithmetic  6.21 us (2%)
    all_gather x1, waiting for transfers between devices, local(): lax.all_gather(index_keys, ('ctx', 'pb'), axis=0, tiled=True)  261 us
    dot_general x8, matrix products, add_group(): lax.dot_general(group_queries.reshape(row_count * group_size, row_width),...  27.9 us
    all_to_all x1, starting transfers between devices, local(): lax.all_to_all(requests, 'ctx', split_axis=0, concat_axis=0, tiled=True)  16.7 us
  transfers between devices with their start and end apart: 3, of which 2 were waited for; matrix products, arithmetic and copies ran while one was open for 11% of the time, Pallas kernels for 0%

commit v1 on v0

v1 whole, which is shorter than its diff:
```python
import jax
import jax.numpy as jnp
from jax import lax
from jax.experimental import pallas as pl
from jax.experimental.pallas import tpu as pltpu
from jax.sharding import PartitionSpec as P

DL = 512
DQK = 576
ROT = DQK - DL
BLK = 64
IH = 64
ID = 128
HEADS = 128
PLANE = 16
LEVELS = 16
PIECE = BLK // PLANE
KV_COLS = PIECE * DQK
Z_COLS = KV_COLS + 4 * ID
SENT_COLS = KV_COLS + 128
VMEM_LIMIT = 40 * 1024 * 1024

score_scale = 192.0 ** (-0.5)
index_scale = 128.0 ** (-0.5)
f32 = jnp.float32
bf16 = jnp.bfloat16

NEAR = (0, 64, 16)
FAR = (64, 192, 48)


def params():
    return pltpu.CompilerParams(vmem_limit_bytes=VMEM_LIMIT)


def whole():
    return pl.BlockSpec(memory_space=pltpu.VMEM)


def anywhere():
    return pl.BlockSpec(memory_space=pl.ANY)


def iota(shape, dim):
    return lax.broadcasted_iota(jnp.int32, shape, dim)


def table_row(block):
    at = lax.axis_index("ctx")
    half = (block // 8 + at) % 2
    turn = (block // 16 - at // 2 + LEVELS) % 4
    order = jnp.where(turn == 3, 2, jnp.where(turn == 2, 3, turn))
    inner = block // 64 * 8 + block % 8
    return jnp.where(
        order == 0, half * 32 + inner, 64 + half * 96 + (order - 1) * 32 + inner
    )


def pack_kernel(kv_ref, ik_ref, iq_ref, iw_ref, qb_ref, z_ref, y_ref, keys, rows):
    piece = lax.axis_index("pb")
    shard_keys = kv_ref.shape[1]
    line = iota((PIECE * 8, shard_keys), 0)
    source = (line % 8) * BLK + piece * PIECE + line // 8
    select = jnp.where(source == iota(source.shape, 1), 1.0, 0.0).astype(bf16)
    part = lax.dot_general(
        select, kv_ref[...], (((1,), (1,)), ((), ())), preferred_element_type=f32
    )
    keys[...] = ik_ref[...].astype(f32)
    columns = [part[r * 8 : (r + 1) * 8, :DL] for r in range(PIECE)]
    columns += [part[r * 8 : (r + 1) * 8, DL:] for r in range(PIECE)]
    columns += [keys[pl.ds(j, 8, stride=4), :] for j in range(4)]
    chunk = jnp.concatenate(columns, axis=1).astype(bf16)
    for n in range(4):
        z_ref[n] = chunk
    for h in range(IH):
        rows[pl.ds(h, 2, stride=IH), :] = iq_ref[:, h * ID : (h + 1) * ID].astype(f32)
    weights = iw_ref[...].astype(f32)
    weights = jnp.concatenate([weights[0:1], weights[1:2]], axis=1)
    ids = qb_ref[...].astype(f32)
    ids = jnp.concatenate([ids[0:1], ids[1:2], jnp.zeros((1, 64), f32)], axis=1)
    at = iota((16, 128), 0)
    tail = jnp.where(at == 0, weights, jnp.where(at == 1, ids, 0.0)).astype(bf16)
    head = rows[...].astype(bf16)
    for p in range(PLANE):
        y_ref[p, 0 : 2 * IH, :] = head
        y_ref[p, 2 * IH : 2 * IH + 16, :] = tail


def pack(kv_turned, index_keys, index_queries, index_weights, q_blocks):
    return pl.pallas_call(
        pack_kernel,
        out_shape=(
            jax.ShapeDtypeStruct((4, 8, Z_COLS), bf16),
            jax.ShapeDtypeStruct((PLANE, 2 * IH + 16, ID), bf16),
        ),
        in_specs=[whole()] * 5,
        out_specs=(whole(), whole()),
        scratch_shapes=[pltpu.VMEM((32, ID), f32), pltpu.VMEM((2 * IH, ID), f32)],
        compiler_params=params(),
        name="pack",
    )(kv_turned, index_keys, index_queries, index_weights, q_blocks)


def named_columns(span, ids):
    first, count, unused = span
    lane = iota((count, 128), 1)
    named = jnp.zeros((count, 128), f32)
    for n, row in enumerate(ids):
        place = table_row(row) - first
        hit = jnp.where(place == iota((count, row.shape[1]), 0), 1.0, 0.0)
        named = jnp.where(lane == n, jnp.max(hit, axis=1, keepdims=True), named)
    return named


def slot_codes(span, named):
    count = span[1]
    t, u = iota((count, count), 0), iota((count, count), 1)
    before = jnp.where((t // 8 == u // 8) & (u < t), 1.0, 0.0).astype(bf16)
    rank = jnp.dot(before, named.astype(bf16), preferred_element_type=f32)
    return jnp.where(named > 0.5, rank, -1.0)


def gather_kernel(span, tables, y_ref, scores_ref, out_ref, onehot):
    first, count, slots = span
    rows = [
        y_ref[p, 2 * IH : 2 * IH + 16, :].astype(f32)[1:2, :64].astype(jnp.int32)
        for p in range(PLANE)
    ]
    named = named_columns(span, rows)
    code = slot_codes(span, named)
    width = PLANE * slots
    line, lane = iota((count, width), 0), iota((count, width), 1)
    wide = jnp.full((count, width), -1.0, f32)
    for p in range(PLANE):
        wide = jnp.where(lane // slots == p, code[:, p : p + 1], wide)
    slot = lane % slots
    turned = jnp.where(
        (line // 8 == slot // 2) & (wide == (slot % 2).astype(f32)), 1.0, 0.0
    )
    pad = -count % 128
    turned = jnp.concatenate([turned, jnp.zeros((pad, width), f32)], axis=0)
    onehot[...] = turned.T[:, :count].astype(bf16)
    for c in range(KV_COLS // 256):
        cols = slice(c * 256, (c + 1) * 256)
        rows = jnp.concatenate([ref[:, cols] for ref in tables], axis=0)
        out_ref[:, cols] = jnp.dot(
            onehot[...], rows, preferred_element_type=f32
        ).astype(bf16)
    if scores_ref is not None:
        for p in range(PLANE):
            at = p * slots
            out_ref[at : at + 16, KV_COLS:] = scores_ref[p]
            out_ref[at + 16 : at + slots, KV_COLS:] = jnp.zeros((slots - 16, 128), bf16)


def gather(name, span, tables, y, scores=None):
    first, count, slots = span

    def body(*refs):
        refs = list(refs)
        held = [refs.pop(0) for table in tables]
        y_ref = refs.pop(0)
        scores_ref = None if scores is None else refs.pop(0)
        gather_kernel(span, held, y_ref, scores_ref, *refs)

    operands = [*tables, y] + ([] if scores is None else [scores])
    columns = KV_COLS if scores is None else SENT_COLS
    return pl.pallas_call(
        body,
        out_shape=jax.ShapeDtypeStruct((PLANE * slots, columns), bf16),
        in_specs=[whole()] * len(operands),
        out_specs=whole(),
        scratch_shapes=[pltpu.VMEM((PLANE * slots, count), bf16)],
        compiler_params=params(),
        cost_estimate=pl.CostEstimate(
            flops=2 * PLANE * slots * count * KV_COLS,
            bytes_accessed=3_000_000,
            transcendentals=0,
        ),
        name=name,
    )(*operands)


def score_kernel(*refs):
    tables, y_ref, out_ref, keys = refs[:8], refs[8], refs[9], refs[10]
    tail = jnp.concatenate(
        [y_ref[p, 2 * IH : 2 * IH + 16, :].astype(f32)[0:1] for p in range(PLANE)], axis=0
    )
    weights = jnp.concatenate(
        [tail * index_scale, jnp.zeros((128 - PLANE, 128), f32)], axis=0
    ).T
    lane = iota((128, 128), 1)
    at = lax.axis_index("ctx")
    for n, ref in enumerate(tables):
        step = (0, 1, 3, 2)[n % 4]
        inner = (at // 2 + step) % 4
        core = (at + n // 4) % 2
        for outer in range(4):
            shard = (outer * 4 + inner) * 2 + core
            for j in range(4):
                cols = slice(KV_COLS + j * ID, KV_COLS + (j + 1) * ID)
                keys[pl.ds(shard * 32 + j, 8, stride=4), :] = ref[
                    outer * 8 : (outer + 1) * 8, cols
                ].astype(f32)
    key_rows = keys[...].astype(bf16)

    def peer(p, carry):
        products = lax.dot_general(
            y_ref[p, 0 : 2 * IH, :],
            key_rows,
            (((1,), (1,)), ((), ())),
            preferred_element_type=f32,
        )
        weight = jnp.sum(jnp.where(lane == p, weights, 0.0), axis=1, keepdims=True)
        active = jnp.maximum(products, 0.0) * weight
        lines = []
        for i in range(2):
            total = jnp.sum(active[i * IH : (i + 1) * IH], axis=0, keepdims=True)
            lines += [total[:, c * 128 : (c + 1) * 128] for c in range(8)]
        out_ref[p] = jnp.concatenate(lines, axis=0).astype(bf16)
        return carry

    lax.fori_loop(0, PLANE, peer, 0)


def score(tables, y):
    return pl.pallas_call(
        score_kernel,
        out_shape=jax.ShapeDtypeStruct((PLANE, 16, 128), bf16),
        in_specs=[whole()] * 9,
        out_specs=whole(),
        scratch_shapes=[pltpu.VMEM((1024, ID), f32)],
        compiler_params=params(),
        cost_estimate=pl.CostEstimate(
            flops=2 * 2048 * 128 * 1024, bytes_accessed=2_000_000, transcendentals=0
        ),
        name="score",
    )(*tables, y)


def attend_kernel(q_ref, ids_ref, near_ref, far_ref, out_ref, scores, total):
    rank = lax.axis_index("ctx") * PLANE + lax.axis_index("pb")
    ids = ids_ref[...]
    own_row = table_row(240 + rank * 2 // BLK)
    query = jnp.concatenate([q_ref[0], q_ref[1]], axis=0)
    latent = query[:, :DL]
    rotary = query[:, DL:]
    nothing = jnp.zeros_like(rotary)
    padded = (
        jnp.concatenate([rotary, nothing], axis=1),
        jnp.concatenate([nothing, rotary], axis=1),
    )
    contract = (((1,), (1,)), ((), ()))
    sets = []
    for span, ref in ((NEAR, near_ref), (FAR, far_ref)):
        first, count, slots = span
        one, two = named_columns(span, [ids[0:1]]), named_columns(span, [ids[1:2]])
        members = (one[:, 0:1], two[:, 0:1])
        code = slot_codes(span, jnp.maximum(one, two))[:, 0:1]
        width = PLANE * slots
        line, slot = iota((count, width), 0), iota((count, width), 1) % slots
        onehot = (line // 8 == slot // 2) & (code == (slot % 2).astype(f32))
        limits = []
        for i in range(2):
            offset = ((rank * 2 + i) % BLK).astype(f32)
            limit = jnp.where(line[:, 0:1] + first == own_row, offset, 63.0) + 1.0
            limit = jnp.where(members[i] > 0.5, limit, 0.0)
            limits.append(jnp.sum(jnp.where(onehot, limit, 0.0), axis=0, keepdims=True))
        place = iota((1, width), 1) // slots * PIECE
        for k in range(width // 256):
            rows = slice(k * 256, (k + 1) * 256)
            for r in range(PIECE):
                turn = PIECE * DL + r // 2 * 128
                block = lax.dot_general(
                    latent, ref[rows, r * DL : (r + 1) * DL], contract,
                    preferred_element_type=f32,
                ) + lax.dot_general(
                    padded[r % 2], ref[rows, turn : turn + 128], contract,
                    preferred_element_type=f32,
                )
                at = len(sets) * 256
                sets.append((ref, rows, slice(r * DL, (r + 1) * DL)))
                here = (place[:, rows] + r).astype(f32)
                for i in range(2):
                    heads = slice(i * HEADS, (i + 1) * HEADS)
                    scores[heads, at : at + 256] = jnp.where(
                        here < limits[i][:, rows], block[heads] * score_scale, -1e30
                    )
    highest = jnp.full((2 * HEADS, 1), -1e30, f32)
    for c in range(16):
        highest = jnp.maximum(
            highest, jnp.max(scores[:, c * 256 : (c + 1) * 256], axis=1, keepdims=True)
        )
    norm = jnp.zeros((2 * HEADS, 1), f32)
    for c in range(16):
        cols = slice(c * 256, (c + 1) * 256)
        weight = jnp.exp(scores[:, cols] - highest)
        scores[:, cols] = weight
        norm = norm + jnp.sum(weight, axis=1, keepdims=True)
    share = 1.0 / norm
    for c, (ref, rows, lanes) in enumerate(sets):
        probs = (scores[:, c * 256 : (c + 1) * 256] * share).astype(bf16)
        term = jnp.dot(probs, ref[rows, lanes], preferred_element_type=f32)
        for k in range(4):
            if c == 0:
                total[k] = term[:, k * 128 : (k + 1) * 128]
            else:
                total[k] += term[:, k * 128 : (k + 1) * 128]
    for h in range(HEADS):
        for k in range(4):
            at = h * DL + k * 128
            out_ref[:, at : at + 128] = total[k, pl.ds(h, 2, stride=HEADS), :].astype(bf16)


def attend(query, ids, near, far):
    return pl.pallas_call(
        attend_kernel,
        out_shape=jax.ShapeDtypeStruct((2, HEADS * DL), bf16),
        in_specs=[whole()] * 4,
        out_specs=whole(),
        scratch_shapes=[
            pltpu.VMEM((2 * HEADS, 4096), f32),
            pltpu.VMEM((4, 2 * HEADS, 128), f32),
        ],
        compiler_params=params(),
        cost_estimate=pl.CostEstimate(
            flops=2 * 256 * 4096 * 1152, bytes_accessed=6_000_000, transcendentals=256 * 4096
        ),
        name="attend",
    )(query, ids, near, far)


def level_from(value, away):
    pairs = [
        ((level + away) % LEVELS * 2 + core, level * 2 + core)
        for level in range(LEVELS)
        for core in range(2)
    ]
    return lax.ppermute(value, "ctx", pairs)


def swap(value):
    return lax.ppermute(value, "ctx", [(at, at ^ 1) for at in range(2 * LEVELS)])


def exchange(rows):
    parts = rows.reshape(PLANE, rows.shape[0] // PLANE, rows.shape[1])
    got = lax.all_to_all(parts, "pb", split_axis=0, concat_axis=0, tiled=True)
    return got.reshape(rows.shape)


def outer_levels(chunks):
    groups = [
        [(outer * 4 + inner) * 2 + core for outer in range(4)]
        for inner in range(4)
        for core in range(2)
    ]
    got = lax.all_to_all(
        chunks, "ctx", split_axis=0, concat_axis=0, axis_index_groups=groups, tiled=True
    )
    return got.reshape(chunks.shape[0] * chunks.shape[1], chunks.shape[2])


def local(q_latent, kv_cache, index_queries, index_weights, index_keys, q_blocks):
    z, y = pack(kv_cache.T, index_keys, index_queries, index_weights, q_blocks)
    held = outer_levels(z)
    y = lax.all_to_all(y, "pb", split_axis=0, concat_axis=0, tiled=True)
    across = swap(held)
    near = exchange(gather("near", NEAR, [held, across], y))
    others = [level_from(held, away) for away in (1, 15, 2)]
    swapped = [swap(other) for other in others]
    scores = score([held] + others + [across] + swapped, y)
    far = exchange(gather("far", FAR, others + swapped, y, scores))
    attention = attend(q_latent.reshape(2, HEADS, DQK), q_blocks, near, far)
    scores = far.reshape(PLANE, FAR[2], SENT_COLS)[:, :16, KV_COLS:]
    scores = scores.reshape(PLANE, 2, 32, 32).transpose(1, 2, 0, 3).reshape(2, 16384)
    return (attention, scores)


def solution(mesh):
    in_specs = (
        P(("ctx", "pb"), None),
        P("ctx", None),
        P(("ctx", "pb"), None),
        P(("ctx", "pb"), None),
        P(("ctx", "pb"), None),
        P(("ctx", "pb"), None),
    )
    out_specs = (P(("ctx", "pb"), None), P(("ctx", "pb"), None))
    return jax.shard_map(local, mesh=mesh, in_specs=in_specs, out_specs=out_specs, check_vma=False)
```

time: 368 us -> 169 us (0.46)
  waiting for transfers between devices: 267 us -> 69 us
  matrix products: 31.1 us -> 0 us
  blocking collectives: 0 us -> 28.3 us
  starting transfers between devices: 23.4 us -> 41.5 us
  Pallas kernels: 0 us -> 17.8 us
  local copies, waits for them, and re-layouts: 24.4 us -> 8.13 us
  between operations: 14.1 us -> 0.85 us
  other arithmetic: 6.21 us -> 0 us
    all_gather x1 -> x0, waiting for transfers between devices: 261 us -> none  [local(): lax.all_gather(index_keys, ('ctx', 'pb'), axis=0, tiled=True)]
    all_to_all x2 -> x3, waiting for transfers between devices: 5.62 us -> 68 us  [the longest x2 68 us: exchange(): got = lax.all_to_all(parts, 'pb', split_axis=0, concat_axis=0, tiled=True)]
    dot_general x12 -> x0, matrix products: 31.1 us -> none  [the longest x8 27.9 us: add_group(): lax.dot_general(group_queries.reshape(row_count * group_size, row_width),...]
    all_to_all x0 -> x1, blocking collectives: none -> 28.3 us  [outer_levels(): lax.all_to_all(chunks, 'ctx', split_axis=0, concat_axis=0, axis_index_gro...]
    ppermute x0 -> x7, starting transfers between devices: none -> 23.3 us  [the longest x3 12.3 us: level_from(): return lax.ppermute(value, 'ctx', pairs)]
    pallas_call x0 -> x5, Pallas kernels: none -> 17.8 us  [the longest x1 7.4 us: attend(): pl.pallas_call(attend_kernel, out_shape=jax.ShapeDtypeStruct((2, HEADS *...]
    gather x3 -> x0, local copies, waits for them, and re-layouts: 10.5 us -> none  [the longest x2 7.01 us: attend_row(): fetched_rows[row_locations].reshape(chosen_count * BLK, row_width)]
    all_to_all x2 -> x3, starting transfers between devices: 23.4 us -> 18.2 us  [the longest x2 11.4 us: exchange(): got = lax.all_to_all(parts, 'pb', split_axis=0, concat_axis=0, tiled=True)]
  transfers between devices with their start and end apart: 3 -> 10, of which waited for: 2 -> 3; matrix products, arithmetic and copies ran while one was open for 11% -> 1% of each run, Pallas kernels for 0% -> 1%
where the time goes in v1:
time: 169 us; the launch traced here: 166 us
  waiting for transfers between devices  69 us (41%)
  starting transfers between devices  41.5 us (25%)
  blocking collectives  28.3 us (17%)
  Pallas kernels  17.8 us (11%)
  local copies, waits for them, and re-layouts  8.13 us (5%)
    all_to_all x2, waiting for transfers between devices, exchange(): got = lax.all_to_all(parts, 'pb', split_axis=0, concat_axis=0, tiled=True)  68 us
    all_to_all x1, blocking collectives, outer_levels(): lax.all_to_all(chunks, 'ctx', split_axis=0, concat_axis=0, axis_index_gro...  28.3 us
    ppermute x3, starting transfers between devices, level_from(): return lax.ppermute(value, 'ctx', pairs)  12.3 us
    all_to_all x2, starting transfers between devices, exchange(): got = lax.all_to_all(parts, 'pb', split_axis=0, concat_axis=0, tiled=True)  11.4 us
    ppermute x4, starting transfers between devices, swap(): lax.ppermute(value, 'ctx', [(at, at ^ 1) for at in range(2 * LEVELS)])  10.9 us
    pallas_call x1, Pallas kernels, attend(): pl.pallas_call(attend_kernel, out_shape=jax.ShapeDtypeStruct((2, HEADS *...  7.4 us
    all_to_all x1, starting transfers between devices, local(): y = lax.all_to_all(y, 'pb', split_axis=0, concat_axis=0, tiled=True)  6.76 us
    unnamed x16, local copies, waits for them, and re-layouts  5.7 us
  transfers between devices with their start and end apart: 10, of which 3 were waited for; matrix products, arithmetic and copies ran while one was open for 1% of the time, Pallas kernels for 1%

profile of v1, /device:TPU:1, one launch (start us, length us, event | category | flops | bytes accessed | tf_op | source)
XLA Modules:
  0.0 165.5 jit_solution(9093223733511510738)
XLA Ops:
  0.6 0.0 copy-start.1
  0.6 1.1 copy-done.1
  1.7 0.0 copy-start.2
  1.7 0.8 copy-done.2
  2.5 0.0 copy-start.3
  2.5 0.7 copy-done.3
  3.2 0.0 copy-start.4
  3.2 0.7 copy-done.4
  3.8 0.0 copy-start.6
  3.8 0.7 copy-done.6
  4.5 1.2 pack.1
  5.7 28.3 %all_to_all.20 = bf16[4,8,2816]{2,1,0:T(8,128)(2,1)S(1)} all-to-all(bf16[4,8,2816]{2,1,0:T(8,128)(2,1)S(1)} %get-tuple-element.4), channel_id=1, replica_groups={{0,128,256,384},{16,144,272,400},{32,160,288,416},{48,176,304,432},{64,..., dimensions={0} | all-to-all | bytes 360448 | tf_op jit(solution)/shard_map/all_to_all | solution.py:358
  33.9 6.8 %all-to-all-start.1 = ((bf16[16,144,128]{2,1,0:T(8,128)(2,1)}), bf16[16,144,128]{2,1,0:T(8,128)(2,1)S(1)}, u32[]{:S(2)}, u32[]{:S(2)}) async-start(bf16[16,144,128]{2,1,0:T(8,128)(2,1)} %get-tuple-element.5), calls=%async_computation.1 | async-start | bytes 1179648 | tf_op jit(solution)/shard_map/all_to_all | solution.py:367
  40.7 1.9 %collective-permute-start.1 = (bf16[32,2816]{1,0:T(8,128)(2,1)S(1)}, bf16[32,2816]{1,0:T(8,128)(2,1)S(1)}, u32[]{:S(2)}, u32[]{:S(2)}) collective-permute-start(bf16[32,2816]{1,0:T(8,128)(2,1)S(1)} %bitcast.12), channel_id=1, source_target_pairs={{32,0},{48,16},{64,32},{80,48},{96,64},{112,80},{128,96},{144,112}... | collective-permute-start | bytes 540680 | tf_op jit(solution)/shard_map/ppermute | solution.py:339
  42.6 5.9 %collective-permute-start.2 = (bf16[32,2816]{1,0:T(8,128)(2,1)S(1)}, bf16[32,2816]{1,0:T(8,128)(2,1)S(1)}, u32[]{:S(2)}, u32[]{:S(2)}) collective-permute-start(bf16[32,2816]{1,0:T(8,128)(2,1)S(1)} %bitcast.13), channel_id=1, source_target_pairs={{480,0},{496,16},{0,32},{16,48},{32,64},{48,80},{64,96},{80,112},{... | collective-permute-start | bytes 540680 | tf_op jit(solution)/shard_map/ppermute | solution.py:339
  48.6 4.5 %collective-permute-start.3 = (bf16[32,2816]{1,0:T(8,128)(2,1)S(1)}, bf16[32,2816]{1,0:T(8,128)(2,1)S(1)}, u32[]{:S(2)}, u32[]{:S(2)}) collective-permute-start(bf16[32,2816]{1,0:T(8,128)(2,1)S(1)} %bitcast.14), channel_id=1, source_target_pairs={{64,0},{80,16},{96,32},{112,48},{128,64},{144,80},{160,96},{176,11... | collective-permute-start | bytes 540680 | tf_op jit(solution)/shard_map/ppermute | solution.py:339
  53.0 3.7 %collective-permute-start = (bf16[32,2816]{1,0:T(8,128)(2,1)S(1)}, bf16[32,2816]{1,0:T(8,128)(2,1)S(1)}, u32[]{:S(2)}, u32[]{:S(2)}) collective-permute-start(bf16[32,2816]{1,0:T(8,128)(2,1)S(1)} %bitcast.15), channel_id=1, source_target_pairs={{0,16},{16,0},{32,48},{48,32},{64,80},{80,64},{96,112},{112,96},{1... | collective-permute-start | bytes 540680 | tf_op jit(solution)/shard_map/ppermute | solution.py:343
  56.8 0.0 collective-permute-done.1.refs_1_.refs_0_
  56.8 1.9 %collective-permute-start.4 = (bf16[32,2816]{1,0:T(8,128)(2,1)S(1)}, bf16[32,2816]{1,0:T(8,128)(2,1)S(1)}, u32[]{:S(2)}, u32[]{:S(2)}) collective-permute-start(bf16[32,2816]{1,0:T(8,128)(2,1)S(1)} %collective-permute-done.1.refs_1_.refs_0_), channel_id=1, source_target_pairs={{0,16},{16,0},{32,48},{48,32},{64,80},{80,64},{96,112},{112,96},{1... | collective-permute-start | bytes 540680 | tf_op jit(solution)/shard_map/ppermute | solution.py:343
  58.7 0.0 collective-permute-done.2.refs_2_.refs_1_
  58.7 2.4 %collective-permute-start.5 = (bf16[32,2816]{1,0:T(8,128)(2,1)S(1)}, bf16[32,2816]{1,0:T(8,128)(2,1)S(1)}, u32[]{:S(2)}, u32[]{:S(2)}) collective-permute-start(bf16[32,2816]{1,0:T(8,128)(2,1)S(1)} %collective-permute-done.2.refs_2_.refs_1_), channel_id=1, source_target_pairs={{0,16},{16,0},{32,48},{48,32},{64,80},{80,64},{96,112},{112,96},{1... | collective-permute-start | bytes 540680 | tf_op jit(solution)/shard_map/ppermute | solution.py:343
  61.1 0.0 collective-permute-done.3.refs_3_.refs_2_
  61.1 2.9 %collective-permute-start.6 = (bf16[32,2816]{1,0:T(8,128)(2,1)S(1)}, bf16[32,2816]{1,0:T(8,128)(2,1)S(1)}, u32[]{:S(2)}, u32[]{:S(2)}) collective-permute-start(bf16[32,2816]{1,0:T(8,128)(2,1)S(1)} %collective-permute-done.3.refs_3_.refs_2_), channel_id=1, source_target_pairs={{0,16},{16,0},{32,48},{48,32},{64,80},{80,64},{96,112},{112,96},{1... | collective-permute-start | bytes 540680 | tf_op jit(solution)/shard_map/ppermute | solution.py:343
  64.1 0.0 all-to-all-done.1.refs_2_.refs_8_.refs_6_
  64.1 0.0 collective-permute-done.refs_1_.refs_4_
  64.1 0.0 collective-permute-done.4.refs_5_.refs_3_
  64.1 0.0 collective-permute-done.5.refs_6_.refs_4_
  64.1 1.0 collective-permute-done.6.refs_7_.refs_5_
  65.1 3.9 %score.1.refs_7_ = bf16[16,16,128]{2,1,0:T(8,128)(2,1)S(1)} custom-call(bf16[32,2816]{1,0:T(8,128)(2,1)S(1)} %bitcast.16, bf16[32,2816]{1,0:T(8,128)(2,1)S(1)} %collective-permute-done.1.refs_1_.refs_0_, bf16[32,2816]{1,0:T(8,128)(2,1)S(1)} %collective-permute-done.2.refs_2_.refs_1_, bf16[32,2816]{1,0:T(8,128)(2,1)S(1)} %collective-permute-done.3.refs_3_.refs_2_, ...), custom_call_target="tpu_custom_call" | custom-call | flops 536870912 | bytes 2000000 | tf_op jit(solution)/shard_map/score/pallas_call | solution.py:227
  69.0 2.9 %far.1 = bf16[768,2432]{1,0:T(8,128)(2,1)S(1)} custom-call(bf16[32,2816]{1,0:T(8,128)(2,1)S(1)} %collective-permute-done.1.refs_1_.refs_0_, bf16[32,2816]{1,0:T(8,128)(2,1)S(1)} %collective-permute-done.2.refs_2_.refs_1_, bf16[32,2816]{1,0:T(8,128)(2,1)S(1)} %collective-permute-done.3.refs_3_.refs_2_, ...), custom_call_target="tpu_custom_call" | custom-call | flops 679477248 | bytes 3000000 | tf_op jit(solution)/shard_map/far/pallas_call | solution.py:168
  71.9 0.0 copy-start
  71.9 1.8 %copy-done = bf16[768,2432]{1,0:T(8,128)(2,1)} copy-done((bf16[768,2432]{1,0:T(8,128)(2,1)}, bf16[768,2432]{1,0:T(8,128)(2,1)S(1)}, u32[]{:S(2)}) %copy-start) | copy-done | bytes 3735576
  73.8 7.0 %all-to-all-start.3 = ((bf16[16,48,2432]{2,1,0:T(8,128)(2,1)}), bf16[16,48,2432]{2,1,0:T(8,128)(2,1)}, u32[]{:S(2)}, u32[]{:S(2)}) async-start(bf16[16,48,2432]{2,1,0:T(8,128)(2,1)} %bitcast.11), calls=%async_computation.3 | async-start | bytes 7471104 | tf_op jit(solution)/shard_map/all_to_all | solution.py:348
  80.8 0.0 copy-start.7
  80.8 0.0 copy-start.5
  80.8 2.4 %near.1 = bf16[256,2304]{1,0:T(8,128)(2,1)} custom-call(bf16[32,2816]{1,0:T(8,128)(2,1)S(1)} %bitcast.17, bf16[32,2816]{1,0:T(8,128)(2,1)S(1)} %collective-permute-done.refs_1_.refs_4_, bf16[16,144,128]{2,1,0:T(8,128)(2,1)S(1)} %all-to-all-done.1.refs_2_.refs_8_.refs_6_), custom_call_target="tpu_custom_call" | custom-call | flops 75497472 | bytes 3000000 | tf_op jit(solution)/shard_map/near/pallas_call | solution.py:168
  83.2 53.9 %all-to-all-done.3 = bf16[16,48,2432]{2,1,0:T(8,128)(2,1)} async-done(((bf16[16,48,2432]{2,1,0:T(8,128)(2,1)}), bf16[16,48,2432]{2,1,0:T(8,128)(2,1)}, u32[]{:S(2)}, u32[]{:S(2)}) %all-to-all-start.3) | async-done | bytes 3735584 | tf_op jit(solution)/shard_map/all_to_all | solution.py:348
  137.1 4.4 %all-to-all-start.2 = ((bf16[16,16,2304]{2,1,0:T(8,128)(2,1)}), bf16[16,16,2304]{2,1,0:T(8,128)(2,1)S(1)}, u32[]{:S(2)}, u32[]{:S(2)}) async-start(bf16[16,16,2304]{2,1,0:T(8,128)(2,1)} %bitcast.2), calls=%async_computation.2 | async-start | bytes 2359296 | tf_op jit(solution)/shard_map/all_to_all | solution.py:348
  141.5 0.0 copy-done.7
  141.5 0.3 reshape.28.q_ref
  141.9 0.9 slice.4
  142.7 0.2 reshape.34
  142.9 0.2 copy.11
  143.1 0.9 reshape.35
  144.0 14.1 %all-to-all-done.2 = bf16[16,16,2304]{2,1,0:T(8,128)(2,1)S(1)} async-done(((bf16[16,16,2304]{2,1,0:T(8,128)(2,1)}), bf16[16,16,2304]{2,1,0:T(8,128)(2,1)S(1)}, u32[]{:S(2)}, u32[]{:S(2)}) %all-to-all-start.2) | async-done | bytes 1179680 | tf_op jit(solution)/shard_map/all_to_all | solution.py:348
  158.1 0.0 copy-done.5
  158.1 7.4 %attend.1 = bf16[2,65536]{1,0:T(2,128)(2,1)} custom-call(bf16[2,128,576]{2,1,0:T(8,128)(2,1)S(1)} %reshape.28.q_ref, s32[2,32]{1,0:T(2,128)S(1)} %copy-done.5, bf16[256,2304]{1,0:T(8,128)(2,1)S(1)} %bitcast.18, bf16[768,2432]{1,0:T(8,128)(2,1)} %bitcast.5.far_ref), custom_call_target="tpu_custom_call" | custom-call | flops 2415919104 | bytes 6000000 | tf_op jit(solution)/shard_map/attend/pallas_call | solution.py:316
Async XLA Ops:
  0.6 1.1 copy-start.1
  1.7 0.8 copy-start.2
  2.5 0.7 copy-start.3
  3.2 0.7 copy-start.4
  3.8 0.7 copy-start.6
  33.9 30.1 %all-to-all-start.1 = ((bf16[16,144,128]{2,1,0:T(8,128)(2,1)}), bf16[16,144,128]{2,1,0:T(8,128)(2,1)S(1)}, u32[]{:S(2)}, u32[]{:S(2)}) async-start(bf16[16,144,128]{2,1,0:T(8,128)(2,1)} %get-tuple-element.5), calls=%async_computation.1 | async-start | bytes 1179648 | tf_op jit(solution)/shard_map/all_to_all | solution.py:367
  40.7 16.1 %collective-permute-start.1 = (bf16[32,2816]{1,0:T(8,128)(2,1)S(1)}, bf16[32,2816]{1,0:T(8,128)(2,1)S(1)}, u32[]{:S(2)}, u32[]{:S(2)}) collective-permute-start(bf16[32,2816]{1,0:T(8,128)(2,1)S(1)} %bitcast.12), channel_id=1, source_target_pairs={{32,0},{48,16},{64,32},{80,48},{96,64},{112,80},{128,96},{144,112}... | collective-permute-start | bytes 540680 | tf_op jit(solution)/shard_map/ppermute | solution.py:339
  42.6 16.1 %collective-permute-start.2 = (bf16[32,2816]{1,0:T(8,128)(2,1)S(1)}, bf16[32,2816]{1,0:T(8,128)(2,1)S(1)}, u32[]{:S(2)}, u32[]{:S(2)}) collective-permute-start(bf16[32,2816]{1,0:T(8,128)(2,1)S(1)} %bitcast.13), channel_id=1, source_target_pairs={{480,0},{496,16},{0,32},{16,48},{32,64},{48,80},{64,96},{80,112},{... | collective-permute-start | bytes 540680 | tf_op jit(solution)/shard_map/ppermute | solution.py:339
  48.6 12.6 %collective-permute-start.3 = (bf16[32,2816]{1,0:T(8,128)(2,1)S(1)}, bf16[32,2816]{1,0:T(8,128)(2,1)S(1)}, u32[]{:S(2)}, u32[]{:S(2)}) collective-permute-start(bf16[32,2816]{1,0:T(8,128)(2,1)S(1)} %bitcast.14), channel_id=1, source_target_pairs={{64,0},{80,16},{96,32},{112,48},{128,64},{144,80},{160,96},{176,11... | collective-permute-start | bytes 540680 | tf_op jit(solution)/shard_map/ppermute | solution.py:339
  53.0 11.0 %collective-permute-start = (bf16[32,2816]{1,0:T(8,128)(2,1)S(1)}, bf16[32,2816]{1,0:T(8,128)(2,1)S(1)}, u32[]{:S(2)}, u32[]{:S(2)}) collective-permute-start(bf16[32,2816]{1,0:T(8,128)(2,1)S(1)} %bitcast.15), channel_id=1, source_target_pairs={{0,16},{16,0},{32,48},{48,32},{64,80},{80,64},{96,112},{112,96},{1... | collective-permute-start | bytes 540680 | tf_op jit(solution)/shard_map/ppermute | solution.py:343
  56.8 7.3 %collective-permute-start.4 = (bf16[32,2816]{1,0:T(8,128)(2,1)S(1)}, bf16[32,2816]{1,0:T(8,128)(2,1)S(1)}, u32[]{:S(2)}, u32[]{:S(2)}) collective-permute-start(bf16[32,2816]{1,0:T(8,128)(2,1)S(1)} %collective-permute-done.1.refs_1_.refs_0_), channel_id=1, source_target_pairs={{0,16},{16,0},{32,48},{48,32},{64,80},{80,64},{96,112},{112,96},{1... | collective-permute-start | bytes 540680 | tf_op jit(solution)/shard_map/ppermute | solution.py:343
  58.7 5.4 %collective-permute-start.5 = (bf16[32,2816]{1,0:T(8,128)(2,1)S(1)}, bf16[32,2816]{1,0:T(8,128)(2,1)S(1)}, u32[]{:S(2)}, u32[]{:S(2)}) collective-permute-start(bf16[32,2816]{1,0:T(8,128)(2,1)S(1)} %collective-permute-done.2.refs_2_.refs_1_), channel_id=1, source_target_pairs={{0,16},{16,0},{32,48},{48,32},{64,80},{80,64},{96,112},{112,96},{1... | collective-permute-start | bytes 540680 | tf_op jit(solution)/shard_map/ppermute | solution.py:343
  61.1 4.0 %collective-permute-start.6 = (bf16[32,2816]{1,0:T(8,128)(2,1)S(1)}, bf16[32,2816]{1,0:T(8,128)(2,1)S(1)}, u32[]{:S(2)}, u32[]{:S(2)}) collective-permute-start(bf16[32,2816]{1,0:T(8,128)(2,1)S(1)} %collective-permute-done.3.refs_3_.refs_2_), channel_id=1, source_target_pairs={{0,16},{16,0},{32,48},{48,32},{64,80},{80,64},{96,112},{112,96},{1... | collective-permute-start | bytes 540680 | tf_op jit(solution)/shard_map/ppermute | solution.py:343
  71.9 1.9 %copy-start = (bf16[768,2432]{1,0:T(8,128)(2,1)}, bf16[768,2432]{1,0:T(8,128)(2,1)S(1)}, u32[]{:S(2)}) copy-start(bf16[768,2432]{1,0:T(8,128)(2,1)S(1)} %far.1) | copy-start | bytes 11206660
  73.8 63.3 %all-to-all-start.3 = ((bf16[16,48,2432]{2,1,0:T(8,128)(2,1)}), bf16[16,48,2432]{2,1,0:T(8,128)(2,1)}, u32[]{:S(2)}, u32[]{:S(2)}) async-start(bf16[16,48,2432]{2,1,0:T(8,128)(2,1)} %bitcast.11), calls=%async_computation.3 | async-start | bytes 7471104 | tf_op jit(solution)/shard_map/all_to_all | solution.py:348
  80.8 60.7 %copy-start.7 = (bf16[2,73728]{1,0:T(2,128)(2,1)S(1)}, bf16[2,73728]{1,0:T(2,128)(2,1)}, u32[]{:S(2)}) copy-start(bf16[2,73728]{1,0:T(2,128)(2,1)} %param.6) | copy-start | bytes 884740
  80.8 77.3 %copy-start.5 = (s32[2,32]{1,0:T(2,128)S(1)}, s32[2,32]{1,0:T(2,128)}, u32[]{:S(2)}) copy-start(s32[2,32]{1,0:T(2,128)} %ids_ref.1) | copy-start | bytes 772
  137.1 21.0 %all-to-all-start.2 = ((bf16[16,16,2304]{2,1,0:T(8,128)(2,1)}), bf16[16,16,2304]{2,1,0:T(8,128)(2,1)S(1)}, u32[]{:S(2)}, u32[]{:S(2)}) async-start(bf16[16,16,2304]{2,1,0:T(8,128)(2,1)} %bitcast.2), calls=%async_computation.2 | async-start | bytes 2359296 | tf_op jit(solution)/shard_map/all_to_all | solution.py:348

commit v2 on v1

--- a/solution.py
+++ b/solution.py
@@ -16,17 +16,20 @@
 LEVELS = 16
 PIECE = BLK // PLANE
 KV_COLS = PIECE * DQK
-Z_COLS = KV_COLS + 4 * ID
-SENT_COLS = KV_COLS + 128
-VMEM_LIMIT = 40 * 1024 * 1024
+WIDTH = KV_COLS // 2
+IDS_AT = KV_COLS + 4 * ID
+Z_COLS = IDS_AT + 128
+SENT_COLS = WIDTH + 128
+AWAYS = (0, 1, 2, 14, 15)
+VMEM_LIMIT = 24 * 1024 * 1024
 
 score_scale = 192.0 ** (-0.5)
 index_scale = 128.0 ** (-0.5)
 f32 = jnp.float32
 bf16 = jnp.bfloat16
 
-NEAR = (0, 64, 16)
-FAR = (64, 192, 48)
+NEAR = (0, 64, 12)
+FAR = (64, 192, 32)
 
 
 def params():
@@ -54,6 +57,18 @@
     return jnp.where(
         order == 0, half * 32 + inner, 64 + half * 96 + (order - 1) * 32 + inner
     )
+
+
+def slot_shard(span, t):
+    level = lax.axis_index("ctx") // 2
+    if span is NEAR:
+        away = (t % 32 // 8 * 4 + level % 4 - level + LEVELS) % LEVELS
+        return jnp.where(away == 0, -1, t // 32 * 3 + away // 4 - 1)
+    order = t % 96 // 32
+    step = jnp.where(order == 0, 1, jnp.where(order == 1, 3, 2))
+    away = (t % 32 // 8 * 4 + (level + step) % 4 - level + LEVELS) % LEVELS
+    which = jnp.where(order == 1, away // 4, away // 4 - 1)
+    return jnp.where((away > 2) & (away < 14), t // 96 * 8 + order * 3 + which, -1)
 
 
 def pack_kernel(kv_ref, ik_ref, iq_ref, iw_ref, qb_ref, z_ref, y_ref, keys, rows):
@@ -66,9 +81,14 @@
         select, kv_ref[...], (((1,), (1,)), ((), ())), preferred_element_type=f32
     )
     keys[...] = ik_ref[...].astype(f32)
-    columns = [part[r * 8 : (r + 1) * 8, :DL] for r in range(PIECE)]
-    columns += [part[r * 8 : (r + 1) * 8, DL:] for r in range(PIECE)]
+    ids = qb_ref[...].astype(f32)
+    ids = jnp.concatenate([ids[0:1], ids[1:2], jnp.zeros((1, 64), f32)], axis=1)
+    columns = []
+    for r in range(0, PIECE, 2):
+        pair = (part[r * 8 : (r + 1) * 8], part[(r + 1) * 8 : (r + 2) * 8])
+        columns += [rows_of[:, :DL] for rows_of in pair] + [rows_of[:, DL:] for rows_of in pair]
     columns += [keys[pl.ds(j, 8, stride=4), :] for j in range(4)]
+    columns.append(jnp.where(iota((8, 128), 0) == 0, ids, 0.0))
     chunk = jnp.concatenate(columns, axis=1).astype(bf16)
     for n in range(4):
         z_ref[n] = chunk
@@ -76,8 +96,6 @@
         rows[pl.ds(h, 2, stride=IH), :] = iq_ref[:, h * ID : (h + 1) * ID].astype(f32)
     weights = iw_ref[...].astype(f32)
     weights = jnp.concatenate([weights[0:1], weights[1:2]], axis=1)
-    ids = qb_ref[...].astype(f32)
-    ids = jnp.concatenate([ids[0:1], ids[1:2], jnp.zeros((1, 64), f32)], axis=1)
     at = iota((16, 128), 0)
     tail = jnp.where(at == 0, weights, jnp.where(at == 1, ids, 0.0)).astype(bf16)
     head = rows[...].astype(bf16)
@@ -120,65 +138,135 @@
     return jnp.where(named > 0.5, rank, -1.0)
 
 
+def slot_keys(span, named):
+    code = slot_codes(span, named)
+    shard = slot_shard(span, iota((span[1], 1), 0)).astype(f32)
+    return jnp.where((code >= 0.0) & (shard >= 0.0), shard * 2.0 + code, -1.0)
+
+
 def gather_kernel(span, tables, y_ref, scores_ref, out_ref, onehot):
     first, count, slots = span
     rows = [
         y_ref[p, 2 * IH : 2 * IH + 16, :].astype(f32)[1:2, :64].astype(jnp.int32)
         for p in range(PLANE)
     ]
-    named = named_columns(span, rows)
-    code = slot_codes(span, named)
-    width = PLANE * slots
-    line, lane = iota((count, width), 0), iota((count, width), 1)
-    wide = jnp.full((count, width), -1.0, f32)
-    for p in range(PLANE):
-        wide = jnp.where(lane // slots == p, code[:, p : p + 1], wide)
-    slot = lane % slots
-    turned = jnp.where(
-        (line // 8 == slot // 2) & (wide == (slot % 2).astype(f32)), 1.0, 0.0
-    )
+    keys = slot_keys(span, named_columns(span, rows))
+    each = 2 * slots
     pad = -count % 128
-    turned = jnp.concatenate([turned, jnp.zeros((pad, width), f32)], axis=0)
-    onehot[...] = turned.T[:, :count].astype(bf16)
-    for c in range(KV_COLS // 256):
-        cols = slice(c * 256, (c + 1) * 256)
-        rows = jnp.concatenate([ref[:, cols] for ref in tables], axis=0)
-        out_ref[:, cols] = jnp.dot(
-            onehot[...], rows, preferred_element_type=f32
+    if pad:
+        keys = jnp.concatenate([keys, jnp.zeros((pad, 128), f32)], axis=0)
+    keys = keys.T[:PLANE, :count]
+    keys = jnp.concatenate([keys, keys], axis=1)
+    line, lane = iota((each, 2 * count), 0), iota((each, 2 * count), 1)
+    half = jnp.where(line >= slots, 1, 0)
+    wanted = jnp.where(
+        half == jnp.where(lane >= count, 1, 0), line - half * slots, -5
+    ).astype(f32)
+    picks = [jnp.where(keys[p : p + 1] == wanted, 1.0, 0.0) for p in range(PLANE)]
+    onehot[...] = jnp.concatenate(picks, axis=0).astype(bf16)
+    for c in range(WIDTH // 384):
+        rows = [
+            ref[:, h * WIDTH + c * 384 : h * WIDTH + (c + 1) * 384]
+            for h in range(2)
+            for ref in tables
+        ]
+        out_ref[:, c * 384 : (c + 1) * 384] = jnp.dot(
+            onehot[...], jnp.concatenate(rows, axis=0), preferred_element_type=f32
         ).astype(bf16)
     if scores_ref is not None:
         for p in range(PLANE):
-            at = p * slots
-            out_ref[at : at + 16, KV_COLS:] = scores_ref[p]
-            out_ref[at + 16 : at + slots, KV_COLS:] = jnp.zeros((slots - 16, 128), bf16)
-
-
-def gather(name, span, tables, y, scores=None):
+            at = p * each
+            out_ref[at : at + 16, WIDTH:] = scores_ref[p]
+            out_ref[at + 16 : at + each, WIDTH:] = jnp.zeros((each - 16, 128), bf16)
+
+
+def gather(name, span, tables, y, afters, scores=None):
     first, count, slots = span
 
     def body(*refs):
         refs = list(refs)
         held = [refs.pop(0) for table in tables]
         y_ref = refs.pop(0)
-        scores_ref = None if scores is None else refs.pop(0)
+        scores_ref = None
+        for after in afters:
+            refs.pop(0)
+        if scores is not None:
+            scores_ref = refs.pop(0)
         gather_kernel(span, held, y_ref, scores_ref, *refs)
 
-    operands = [*tables, y] + ([] if scores is None else [scores])
-    columns = KV_COLS if scores is None else SENT_COLS
+    operands = [*tables, y, *afters]
+    in_specs = [whole()] * (len(tables) + 1) + [anywhere()] * len(afters)
+    columns = WIDTH
+    if scores is not None:
+        operands.append(scores)
+        in_specs.append(whole())
+        columns = SENT_COLS
     return pl.pallas_call(
         body,
-        out_shape=jax.ShapeDtypeStruct((PLANE * slots, columns), bf16),
-        in_specs=[whole()] * len(operands),
+        out_shape=jax.ShapeDtypeStruct((PLANE * 2 * slots, columns), bf16),
+        in_specs=in_specs,
         out_specs=whole(),
-        scratch_shapes=[pltpu.VMEM((PLANE * slots, count), bf16)],
+        scratch_shapes=[pltpu.VMEM((PLANE * 2 * slots, 2 * count), bf16)],
         compiler_params=params(),
         cost_estimate=pl.CostEstimate(
-            flops=2 * PLANE * slots * count * KV_COLS,
+            flops=2 * PLANE * slots * 4 * count * WIDTH,
             bytes_accessed=3_000_000,
             transcendentals=0,
         ),
         name=name,
     )(*operands)
+
+
+def serve_kernel(kv_ref, *refs):
+    tables, outs = refs[:8], refs[9:]
+    at = lax.axis_index("ctx")
+    level = at // 2
+    lines = []
+    line = iota((32, 128), 0)
+    for away in AWAYS:
+        outer = (level + away) % LEVELS // 4
+        for other in range(2):
+            ref = tables[(0, 1, 3, 2)[away % 4] + 4 * other]
+            values = jnp.where(line == outer * 8, ref[:, IDS_AT:].astype(f32), 0.0)
+            lines.append(jnp.sum(values, axis=0, keepdims=True))
+    lines += [jnp.full((6, 128), -1.0, f32)]
+    ids = jnp.concatenate(lines, axis=0)[:, :64]
+    own = (at * 8).astype(f32)
+    lane = iota((16, 512), 1)
+    codes = jnp.full((16, 512), -1.0, f32)
+    taken = jnp.zeros((16, 1), f32)
+    for b in range(8):
+        hit = jnp.max(jnp.where(ids == own + b, 1.0, 0.0), axis=1, keepdims=True)
+        codes = jnp.where((lane // BLK == b) & (hit > 0.5), taken, codes)
+        taken = taken + hit
+    row, lane = iota((128, 512), 0), iota((128, 512), 1)
+    same = row % BLK == lane % BLK
+    kind = (row // BLK).astype(f32)
+    for n in range(len(AWAYS)):
+        select = jnp.concatenate(
+            [
+                jnp.where(same & (codes[m : m + 1, :] == kind), 1.0, 0.0).astype(bf16)
+                for m in (2 * n, 2 * n + 1)
+            ],
+            axis=0,
+        )
+        outs[n][...] = lax.dot_general(
+            select, kv_ref[...], (((1,), (1,)), ((), ())), preferred_element_type=f32
+        ).astype(bf16)
+
+
+def serve(kv_turned, tables, after):
+    return pl.pallas_call(
+        serve_kernel,
+        out_shape=tuple(jax.ShapeDtypeStruct((4 * BLK, DQK), bf16) for away in AWAYS),
+        in_specs=[whole()] * 9 + [anywhere()],
+        out_specs=(whole(),) * len(AWAYS),
+        compiler_params=params(),
+        cost_estimate=pl.CostEstimate(
+            flops=2 * 10 * 128 * 512 * DQK, bytes_accessed=4_000_000, transcendentals=0
+        ),
+        name="serve",
+    )(kv_turned, *tables, after)
 
 
 def score_kernel(*refs):
@@ -238,10 +326,20 @@
     )(*tables, y)
 
 
-def attend_kernel(q_ref, ids_ref, near_ref, far_ref, out_ref, scores, total):
-    rank = lax.axis_index("ctx") * PLANE + lax.axis_index("pb")
+def attend_kernel(q_ref, ids_ref, near_ref, far_ref, *refs):
+    count = len(AWAYS)
+    mine, crossed = refs[:count], refs[count]
+    out_ref, index_ref, scores, total, turned = refs[count + 1 :]
+    direct = []
+    for n in range(count):
+        direct.append((mine[n], slice(0, 128)))
+        direct.append((crossed, slice(n * 128, (n + 1) * 128)))
+    at = lax.axis_index("ctx")
+    rank = at * PLANE + lax.axis_index("pb")
     ids = ids_ref[...]
-    own_row = table_row(240 + rank * 2 // BLK)
+    own_block = 240 + rank * 2 // BLK
+    own_row = table_row(own_block)
+    offsets = [((rank * 2 + i) % BLK).astype(f32) for i in range(2)]
     query = jnp.concatenate([q_ref[0], q_ref[1]], axis=0)
     latent = query[:, :DL]
     rotary = query[:, DL:]
@@ -252,55 +350,110 @@
     )
     contract = (((1,), (1,)), ((), ()))
     sets = []
-    for span, ref in ((NEAR, near_ref), (FAR, far_ref)):
+    filled = [0]
+    tops = [jnp.full((HEADS, 128), -1e30, f32) for i in range(2)]
+
+    def keep(block, place, limits, values):
+        at, width = filled[0], block.shape[1]
+        for i in range(2):
+            heads = slice(i * HEADS, (i + 1) * HEADS)
+            value = jnp.where(place < limits[i], block[heads] * score_scale, -1e30)
+            scores[heads, at : at + width] = value
+            for k in range(0, width, 128):
+                tops[i] = jnp.maximum(tops[i], value[:, k : k + 128])
+        sets.append((at, width, values))
+        filled[0] += width
+
+    def product(left, right):
+        return lax.dot_general(left, right, contract, preferred_element_type=f32)
+
+    count = 8 * len(direct)
+    line = iota((count, 128), 0)
+    lane = iota((count, 128), 1)
+    named = jnp.zeros((count, 128), f32)
+    shard = ids // 8
+    away = (shard // 2 - at // 2 + LEVELS) % LEVELS
+    turn = jnp.where(away < 3, away, jnp.where(away > 13, away - 11, -8))
+    place = (turn * 2 + (shard + at) % 2) * 8 + ids % 8
+    own_away = (own_block // 16 - at // 2 + LEVELS) % LEVELS
+    own_turn = jnp.where(own_away < 3, own_away, jnp.where(own_away > 13, own_away - 11, -8))
+    own_place = (own_turn * 2 + (own_block // 8 + at) % 2) * 8 + own_block % 8
+    for i in range(2):
+        hit = jnp.where(place[i : i + 1] == iota((count, ids.shape[1]), 0), 1.0, 0.0)
+        named = jnp.where(lane == i, jnp.max(hit, axis=1, keepdims=True), named)
+    members = named
+    named = jnp.maximum(named[:, 0:1], named[:, 1:2])
+    code = slot_codes((0, count, 2), jnp.broadcast_to(named, (count, 128)))
+    chosen = code == (lane // BLK).astype(f32)
+    limits = []
+    for i in range(2):
+        limit = jnp.where(line[:, 0:1] == own_place, offsets[i], 63.0) + 1.0
+        limit = jnp.where(members[:, i : i + 1] > 0.5, limit, 0.0)
+        limits.append(jnp.where(chosen, limit, 0.0))
+    here = (iota((1, 128), 1) % BLK).astype(f32)
+    here = jnp.concatenate([here, here], axis=1)
+    for n in range(0, len(direct), 2):
+        pair = direct[n : n + 2]
+        block = product(
+            latent, jnp.concatenate([ref[rows, :DL] for ref, rows in pair], axis=0)
+        ) + product(
+            rotary, jnp.concatenate([ref[rows, DL:] for ref, rows in pair], axis=0)
+        )
+        shown = [
+            jnp.concatenate(
+                [
+                    jnp.sum(limit[m * 8 : (m + 1) * 8], axis=0, keepdims=True)
+                    for m in (n, n + 1)
+                ],
+                axis=1,
+            )
+            for limit in limits
+        ]
+        keep(block, here, shown, [(ref, rows, slice(0, DL)) for ref, rows in pair])
+
+    for span, ref, step in ((NEAR, near_ref, 384), (FAR, far_ref, 256)):
         first, count, slots = span
         one, two = named_columns(span, [ids[0:1]]), named_columns(span, [ids[1:2]])
         members = (one[:, 0:1], two[:, 0:1])
-        code = slot_codes(span, jnp.maximum(one, two))[:, 0:1]
-        width = PLANE * slots
-        line, slot = iota((count, width), 0), iota((count, width), 1) % slots
-        onehot = (line // 8 == slot // 2) & (code == (slot % 2).astype(f32))
+        keys = slot_keys(span, jnp.maximum(one, two))[:, 0:1]
+        width = PLANE * 2 * slots
+        line = iota((count, 128), 0)
+        chosen = keys == (iota((1, width), 1) % slots).astype(f32)
         limits = []
         for i in range(2):
-            offset = ((rank * 2 + i) % BLK).astype(f32)
-            limit = jnp.where(line[:, 0:1] + first == own_row, offset, 63.0) + 1.0
+            limit = jnp.where(line[:, 0:1] + first == own_row, offsets[i], 63.0) + 1.0
             limit = jnp.where(members[i] > 0.5, limit, 0.0)
-            limits.append(jnp.sum(jnp.where(onehot, limit, 0.0), axis=0, keepdims=True))
-        place = iota((1, width), 1) // slots * PIECE
-        for k in range(width // 256):
-            rows = slice(k * 256, (k + 1) * 256)
-            for r in range(PIECE):
-                turn = PIECE * DL + r // 2 * 128
-                block = lax.dot_general(
-                    latent, ref[rows, r * DL : (r + 1) * DL], contract,
-                    preferred_element_type=f32,
-                ) + lax.dot_general(
-                    padded[r % 2], ref[rows, turn : turn + 128], contract,
-                    preferred_element_type=f32,
+            limits.append(jnp.sum(jnp.where(chosen, limit, 0.0), axis=0, keepdims=True))
+        lane = iota((1, width), 1)
+        place = lane // (2 * slots) * PIECE + lane // slots % 2 * 2
+        for k in range(width // step):
+            rows = slice(k * step, (k + 1) * step)
+            for parity in range(2):
+                columns = slice(parity * DL, (parity + 1) * DL)
+                block = product(latent, ref[rows, columns]) + product(
+                    padded[parity], ref[rows, 2 * DL : 2 * DL + 128]
                 )
-                at = len(sets) * 256
-                sets.append((ref, rows, slice(r * DL, (r + 1) * DL)))
-                here = (place[:, rows] + r).astype(f32)
-                for i in range(2):
-                    heads = slice(i * HEADS, (i + 1) * HEADS)
-                    scores[heads, at : at + 256] = jnp.where(
-                        here < limits[i][:, rows], block[heads] * score_scale, -1e30
-                    )
-    highest = jnp.full((2 * HEADS, 1), -1e30, f32)
-    for c in range(16):
-        highest = jnp.maximum(
-            highest, jnp.max(scores[:, c * 256 : (c + 1) * 256], axis=1, keepdims=True)
-        )
-    norm = jnp.zeros((2 * HEADS, 1), f32)
-    for c in range(16):
-        cols = slice(c * 256, (c + 1) * 256)
+                keep(
+                    block,
+                    (place[:, rows] + parity).astype(f32),
+                    [limit[:, rows] for limit in limits],
+                    [(ref, rows, columns)],
+                )
+
+    highest = jnp.max(jnp.concatenate(tops, axis=0), axis=1, keepdims=True)
+    norm = jnp.zeros((2 * HEADS, 128), f32)
+    for c in range(32):
+        cols = slice(c * 128, (c + 1) * 128)
         weight = jnp.exp(scores[:, cols] - highest)
         scores[:, cols] = weight
-        norm = norm + jnp.sum(weight, axis=1, keepdims=True)
+        norm = norm + weight
+    norm = jnp.sum(norm, axis=1, keepdims=True)
     share = 1.0 / norm
-    for c, (ref, rows, lanes) in enumerate(sets):
-        probs = (scores[:, c * 256 : (c + 1) * 256] * share).astype(bf16)
-        term = jnp.dot(probs, ref[rows, lanes], preferred_element_type=f32)
+    for c, (at, width, values) in enumerate(sets):
+        probs = (scores[:, at : at + width] * share).astype(bf16)
+        rows = [ref[rows, columns] for ref, rows, columns in values]
+        rows = rows[0] if len(rows) == 1 else jnp.concatenate(rows, axis=0)
+        term = jnp.dot(probs, rows, preferred_element_type=f32)
         for k in range(4):
             if c == 0:
                 total[k] = term[:, k * 128 : (k + 1) * 128]
@@ -311,23 +464,65 @@
             at = h * DL + k * 128
             out_ref[:, at : at + 128] = total[k, pl.ds(h, 2, stride=HEADS), :].astype(bf16)
 
-
-def attend(query, ids, near, far):
+    tiles = [
+        far_ref[p * 2 * FAR[2] : p * 2 * FAR[2] + 16, WIDTH:].astype(f32)
+        for p in range(PLANE)
+    ]
+    group = iota((16, 128), 1) // 32
+    for c in range(4):
+        for m in range(4):
+            mixed = tiles[4 * m]
+            for k in range(4):
+                tile = tiles[4 * m + k]
+                if k != c:
+                    tile = pltpu.roll(tile, (k - c) * 32 % 128, 1)
+                mixed = tile if k == 0 else jnp.where(group == k, tile, mixed)
+            turned[(c * 4 + m) * 16 : (c * 4 + m + 1) * 16, :] = mixed
+            for t in range(8):
+                at = (t * 4 + c) * 512 + m * 128
+                index_ref[:, at : at + 128] = turned[
+                    pl.ds((c * 4 + m) * 16 + t, 2, stride=8), :
+                ].astype(bf16)
+
+
+def attend(query, ids, near, far, mine, crossed):
     return pl.pallas_call(
         attend_kernel,
-        out_shape=jax.ShapeDtypeStruct((2, HEADS * DL), bf16),
-        in_specs=[whole()] * 4,
-        out_specs=whole(),
+        out_shape=(
+            jax.ShapeDtypeStruct((2, HEADS * DL), bf16),
+            jax.ShapeDtypeStruct((2, 16384), bf16),
+        ),
+        in_specs=[whole()] * (5 + len(mine)),
+        out_specs=(whole(), whole()),
         scratch_shapes=[
             pltpu.VMEM((2 * HEADS, 4096), f32),
             pltpu.VMEM((4, 2 * HEADS, 128), f32),
+            pltpu.VMEM((256, 128), f32),
         ],
         compiler_params=params(),
         cost_estimate=pl.CostEstimate(
             flops=2 * 256 * 4096 * 1152, bytes_accessed=6_000_000, transcendentals=256 * 4096
         ),
         name="attend",
-    )(query, ids, near, far)
+    )(query, ids, near, far, *mine, crossed)
+
+
+def join_kernel(*refs):
+    out_ref = refs[-1]
+    for n, ref in enumerate(refs[:-1]):
+        out_ref[n * 128 : (n + 1) * 128, :] = ref[128:, :]
+
+
+def join(parts):
+    return pl.pallas_call(
+        join_kernel,
+        out_shape=jax.ShapeDtypeStruct((len(parts) * 128, DQK), bf16),
+        in_specs=[whole()] * len(parts),
+        out_specs=whole(),
+        compiler_params=params(),
+        cost_estimate=pl.CostEstimate(flops=0, bytes_accessed=2_000_000, transcendentals=0),
+        name="join",
+    )(*parts)
 
 
 def level_from(value, away):
@@ -362,19 +557,25 @@
 
 
 def local(q_latent, kv_cache, index_queries, index_weights, index_keys, q_blocks):
-    z, y = pack(kv_cache.T, index_keys, index_queries, index_weights, q_blocks)
+    kv_turned = kv_cache.T
+    z, y = pack(kv_turned, index_keys, index_queries, index_weights, q_blocks)
     held = outer_levels(z)
     y = lax.all_to_all(y, "pb", split_axis=0, concat_axis=0, tiled=True)
     across = swap(held)
-    near = exchange(gather("near", NEAR, [held, across], y))
     others = [level_from(held, away) for away in (1, 15, 2)]
+    near = exchange(gather("near", NEAR, [held, across], y, others))
     swapped = [swap(other) for other in others]
-    scores = score([held] + others + [across] + swapped, y)
-    far = exchange(gather("far", FAR, others + swapped, y, scores))
-    attention = attend(q_latent.reshape(2, HEADS, DQK), q_blocks, near, far)
-    scores = far.reshape(PLANE, FAR[2], SENT_COLS)[:, :16, KV_COLS:]
-    scores = scores.reshape(PLANE, 2, 32, 32).transpose(1, 2, 0, 3).reshape(2, 16384)
-    return (attention, scores)
+    tables = [held] + others + [across] + swapped
+    scores = score(tables, y)
+    sent = gather("far", FAR, others + swapped, y, [near], scores)
+    served = serve(kv_turned, tables, sent)
+    far = exchange(sent)
+    mine = [served[0]]
+    for away in AWAYS[1:]:
+        mine.append(level_from(served[AWAYS.index(-away % LEVELS)], away))
+    crossed = swap(join(mine))
+    query = q_latent.reshape(2, HEADS, DQK)
+    return tuple(attend(query, q_blocks, near, far, mine, crossed))
 
 
 def solution(mesh):

time: 169 us -> 146 us (0.86)
  waiting for transfers between devices: 69 us -> 19.8 us
  starting transfers between devices: 41.5 us -> 63.8 us
  local copies, waits for them, and re-layouts: 8.13 us -> 11.2 us
  Pallas kernels: 17.8 us -> 20.1 us
    all_to_all x2, waiting for transfers between devices: 68 us -> 0.01 us  [exchange(): got = lax.all_to_all(parts, 'pb', split_axis=0, concat_axis=0, tiled=True)]
    ppermute x3 -> x7, waiting for transfers between devices: 0.01 us -> 18.8 us  [level_from(): return lax.ppermute(value, 'ctx', pairs)]
    ppermute x3 -> x7, starting transfers between devices: 12.3 us -> 26.1 us  [level_from(): return lax.ppermute(value, 'ctx', pairs)]
    ppermute x4 -> x5, starting transfers between devices: 10.9 us -> 16.7 us  [swap(): lax.ppermute(value, 'ctx', [(at, at ^ 1) for at in range(2 * LEVELS)])]
    all_to_all x2, starting transfers between devices: 11.4 us -> 14.3 us  [exchange(): got = lax.all_to_all(parts, 'pb', split_axis=0, concat_axis=0, tiled=True)]
    pallas_call x3 -> x5, Pallas kernels: 12.7 us -> 15 us  [the longest x1 7.46 us: attend(): pl.pallas_call(attend_kernel, out_shape=(jax.ShapeDtypeStruct((2, HEADS *...]
    unnamed x16 -> x20, local copies, waits for them, and re-layouts: 5.7 us -> 6.52 us
  transfers between devices with their start and end apart: 10 -> 15, of which waited for: 3 -> 4; matrix products, arithmetic and copies ran while one was open for 1% -> 3% of each run, Pallas kernels for 1% -> 4%
where the time goes in v2:
time: 146 us; the launch traced here: 144 us
  starting transfers between devices  63.8 us (44%)
  blocking collectives  28.3 us (19%)
  Pallas kernels  20.1 us (14%)
  waiting for transfers between devices  19.8 us (14%)
  local copies, waits for them, and re-layouts  11.2 us (8%)
    all_to_all x1, blocking collectives, outer_levels(): lax.all_to_all(chunks, 'ctx', split_axis=0, concat_axis=0, axis_index_gro...  28.3 us
    ppermute x7, starting transfers between devices, level_from(): return lax.ppermute(value, 'ctx', pairs)  26.1 us
    ppermute x7, waiting for transfers between devices, level_from(): return lax.ppermute(value, 'ctx', pairs)  18.8 us
    ppermute x5, starting transfers between devices, swap(): lax.ppermute(value, 'ctx', [(at, at ^ 1) for at in range(2 * LEVELS)])  16.7 us
    all_to_all x2, starting transfers between devices, exchange(): got = lax.all_to_all(parts, 'pb', split_axis=0, concat_axis=0, tiled=True)  14.3 us
    pallas_call x1, Pallas kernels, attend(): pl.pallas_call(attend_kernel, out_shape=(jax.ShapeDtypeStruct((2, HEADS *...  7.46 us
    all_to_all x1, starting transfers between devices, local(): y = lax.all_to_all(y, 'pb', split_axis=0, concat_axis=0, tiled=True)  6.76 us
    unnamed x20, local copies, waits for them, and re-layouts  6.52 us
  transfers between devices with their start and end apart: 15, of which 4 were waited for; matrix products, arithmetic and copies ran while one was open for 3% of the time, Pallas kernels for 4%

profile of v2, /device:TPU:1, one launch (start us, length us, event | category | flops | bytes accessed | tf_op | source)
XLA Modules:
  0.0 144.2 jit_solution(16315489990586195076)
XLA Ops:
  0.6 0.0 copy-start
  0.6 1.1 copy-done
  1.7 0.8 copy-done.5
  2.5 0.7 copy-done.6
  3.2 0.7 copy-done.7
  3.8 0.7 copy-done.9
  4.5 1.2 pack.1
  5.7 28.3 %all_to_all.20 = bf16[4,8,2944]{2,1,0:T(8,128)(2,1)S(1)} all-to-all(bf16[4,8,2944]{2,1,0:T(8,128)(2,1)S(1)} %get-tuple-element.9), channel_id=1, replica_groups={{0,128,256,384},{16,144,272,400},{32,160,288,416},{48,176,304,432},{64,..., dimensions={0} | all-to-all | bytes 376832 | tf_op jit(solution)/shard_map/all_to_all | solution.py:553
  34.0 6.8 %all-to-all-start.1 = ((bf16[16,144,128]{2,1,0:T(8,128)(2,1)}), bf16[16,144,128]{2,1,0:T(8,128)(2,1)S(1)}, u32[]{:S(2)}, u32[]{:S(2)}) async-start(bf16[16,144,128]{2,1,0:T(8,128)(2,1)} %get-tuple-element.10), calls=%async_computation.1 | async-start | bytes 1179648 | tf_op jit(solution)/shard_map/all_to_all | solution.py:563
  40.8 1.9 %collective-permute-start.1 = (bf16[32,2944]{1,0:T(8,128)(2,1)S(1)}, bf16[32,2944]{1,0:T(8,128)(2,1)S(1)}, u32[]{:S(2)}, u32[]{:S(2)}) collective-permute-start(bf16[32,2944]{1,0:T(8,128)(2,1)S(1)} %bitcast.8), channel_id=1, source_target_pairs={{32,0},{48,16},{64,32},{80,48},{96,64},{112,80},{128,96},{144,112}... | collective-permute-start | bytes 565256 | tf_op jit(solution)/shard_map/ppermute | solution.py:534
  42.7 6.5 %collective-permute-start.2 = (bf16[32,2944]{1,0:T(8,128)(2,1)S(1)}, bf16[32,2944]{1,0:T(8,128)(2,1)S(1)}, u32[]{:S(2)}, u32[]{:S(2)}) collective-permute-start(bf16[32,2944]{1,0:T(8,128)(2,1)S(1)} %bitcast.9), channel_id=1, source_target_pairs={{480,0},{496,16},{0,32},{16,48},{32,64},{48,80},{64,96},{80,112},{... | collective-permute-start | bytes 565256 | tf_op jit(solution)/shard_map/ppermute | solution.py:534
  49.2 4.1 %collective-permute-start.3 = (bf16[32,2944]{1,0:T(8,128)(2,1)S(1)}, bf16[32,2944]{1,0:T(8,128)(2,1)S(1)}, u32[]{:S(2)}, u32[]{:S(2)}) collective-permute-start(bf16[32,2944]{1,0:T(8,128)(2,1)S(1)} %bitcast.10), channel_id=1, source_target_pairs={{64,0},{80,16},{96,32},{112,48},{128,64},{144,80},{160,96},{176,11... | collective-permute-start | bytes 565256 | tf_op jit(solution)/shard_map/ppermute | solution.py:534
  53.3 3.8 %collective-permute-start = (bf16[32,2944]{1,0:T(8,128)(2,1)S(1)}, bf16[32,2944]{1,0:T(8,128)(2,1)S(1)}, u32[]{:S(2)}, u32[]{:S(2)}) collective-permute-start(bf16[32,2944]{1,0:T(8,128)(2,1)S(1)} %bitcast.11), channel_id=1, source_target_pairs={{0,16},{16,0},{32,48},{48,32},{64,80},{80,64},{96,112},{112,96},{1... | collective-permute-start | bytes 565256 | tf_op jit(solution)/shard_map/ppermute | solution.py:538
  57.1 0.0 all-to-all-done.1.refs_2_.refs_8_.refs_6_
  57.1 0.0 collective-permute-done.1.refs_3_.refs_1_.refs_0_
  57.1 0.0 collective-permute-done.2.refs_4_.refs_2_.refs_1_
  57.1 2.4 %collective-permute-done.3.refs_5_.refs_3_.refs_2_ = bf16[32,2944]{1,0:T(8,128)(2,1)S(1)} collective-permute-done((bf16[32,2944]{1,0:T(8,128)(2,1)S(1)}, bf16[32,2944]{1,0:T(8,128)(2,1)S(1)}, u32[]{:S(2)}, u32[]{:S(2)}) %collective-permute-start.3) | collective-permute-done | bytes 188448 | tf_op jit(solution)/shard_map/ppermute | solution.py:534
  59.6 1.9 %near.1 = bf16[384,1152]{1,0:T(8,128)(2,1)} custom-call(bf16[32,2944]{1,0:T(8,128)(2,1)S(1)} %bitcast.12, bf16[32,2944]{1,0:T(8,128)(2,1)S(1)} %collective-permute-done.refs_1_.refs_4_, bf16[16,144,128]{2,1,0:T(8,128)(2,1)S(1)} %all-to-all-done.1.refs_2_.refs_8_.refs_6_, bf16[32,2944]{1,0:T(8,128)(2,1)S(1)} %collective-permute-done.1.refs_3_.refs_1_.refs_0_, ...), custom_call_target="tpu_custom_call" | custom-call | flops 113246208 | bytes 3000000 | tf_op jit(solution)/shard_map/near/pallas_call | solution.py:204
  61.5 7.2 %all-to-all-start.2 = ((bf16[16,24,1152]{2,1,0:T(8,128)(2,1)}), bf16[16,24,1152]{2,1,0:T(8,128)(2,1)S(1)}, u32[]{:S(2)}, u32[]{:S(2)}) async-start(bf16[16,24,1152]{2,1,0:T(8,128)(2,1)} %bitcast.2), calls=%async_computation.2 | async-start | bytes 1769472 | tf_op jit(solution)/shard_map/all_to_all | solution.py:543
  68.7 4.7 %collective-permute-start.4 = (bf16[32,2944]{1,0:T(8,128)(2,1)S(1)}, bf16[32,2944]{1,0:T(8,128)(2,1)S(1)}, u32[]{:S(2)}, u32[]{:S(2)}) collective-permute-start(bf16[32,2944]{1,0:T(8,128)(2,1)S(1)} %collective-permute-done.1.refs_3_.refs_1_.refs_0_), channel_id=1, source_target_pairs={{0,16},{16,0},{32,48},{48,32},{64,80},{80,64},{96,112},{112,96},{1... | collective-permute-start | bytes 565256 | tf_op jit(solution)/shard_map/ppermute | solution.py:538
  73.4 1.9 %collective-permute-start.5 = (bf16[32,2944]{1,0:T(8,128)(2,1)S(1)}, bf16[32,2944]{1,0:T(8,128)(2,1)S(1)}, u32[]{:S(2)}, u32[]{:S(2)}) collective-permute-start(bf16[32,2944]{1,0:T(8,128)(2,1)S(1)} %collective-permute-done.2.refs_4_.refs_2_.refs_1_), channel_id=1, source_target_pairs={{0,16},{16,0},{32,48},{48,32},{64,80},{80,64},{96,112},{112,96},{1... | collective-permute-start | bytes 565256 | tf_op jit(solution)/shard_map/ppermute | solution.py:538
  75.4 2.4 %collective-permute-start.6 = (bf16[32,2944]{1,0:T(8,128)(2,1)S(1)}, bf16[32,2944]{1,0:T(8,128)(2,1)S(1)}, u32[]{:S(2)}, u32[]{:S(2)}) collective-permute-start(bf16[32,2944]{1,0:T(8,128)(2,1)S(1)} %collective-permute-done.3.refs_5_.refs_3_.refs_2_), channel_id=1, source_target_pairs={{0,16},{16,0},{32,48},{48,32},{64,80},{80,64},{96,112},{112,96},{1... | collective-permute-start | bytes 565256 | tf_op jit(solution)/shard_map/ppermute | solution.py:538
  77.8 0.0 collective-permute-done.4.refs_5_.refs_3_
  77.8 1.0 collective-permute-done.6.refs_7_.refs_5_
  78.8 4.0 %score.1.refs_8_ = bf16[16,16,128]{2,1,0:T(8,128)(2,1)S(1)} custom-call(bf16[32,2944]{1,0:T(8,128)(2,1)S(1)} %bitcast.13, bf16[32,2944]{1,0:T(8,128)(2,1)S(1)} %collective-permute-done.1.refs_3_.refs_1_.refs_0_, bf16[32,2944]{1,0:T(8,128)(2,1)S(1)} %collective-permute-done.2.refs_4_.refs_2_.refs_1_, ...), custom_call_target="tpu_custom_call" | custom-call | flops 536870912 | bytes 2000000 | tf_op jit(solution)/shard_map/score/pallas_call | solution.py:315
  82.8 0.0 all-to-all-done.2
  82.8 4.2 %far.1.refs_8_ = bf16[1024,1280]{1,0:T(8,128)(2,1)} custom-call(bf16[32,2944]{1,0:T(8,128)(2,1)S(1)} %collective-permute-done.1.refs_3_.refs_1_.refs_0_, bf16[32,2944]{1,0:T(8,128)(2,1)S(1)} %collective-permute-done.2.refs_4_.refs_2_.refs_1_, bf16[32,2944]{1,0:T(8,128)(2,1)S(1)} %collective-permute-done.3.refs_5_.refs_3_.refs_2_, ...), custom_call_target="tpu_custom_call" | custom-call | flops 905969664 | bytes 3000000 | tf_op jit(solution)/shard_map/far/pallas_call | solution.py:204
  87.0 7.1 %all-to-all-start.3 = ((bf16[16,64,1280]{2,1,0:T(8,128)(2,1)}), bf16[16,64,1280]{2,1,0:T(8,128)(2,1)}, u32[]{:S(2)}, u32[]{:S(2)}) async-start(bf16[16,64,1280]{2,1,0:T(8,128)(2,1)} %bitcast.4), calls=%async_computation.3 | async-start | bytes 5242880 | tf_op jit(solution)/shard_map/all_to_all | solution.py:543
  94.1 1.3 serve.1
  95.4 4.7 %collective-permute-start.10 = (bf16[256,576]{1,0:T(8,128)(2,1)S(1)}, bf16[256,576]{1,0:T(8,128)(2,1)S(1)}, u32[]{:S(2)}, u32[]{:S(2)}) collective-permute-start(bf16[256,576]{1,0:T(8,128)(2,1)S(1)} %get-tuple-element.15), channel_id=1, source_target_pairs={{480,0},{496,16},{0,32},{16,48},{32,64},{48,80},{64,96},{80,112},{... | collective-permute-start | bytes 884744 | tf_op jit(solution)/shard_map/ppermute | solution.py:534
  100.2 2.7 %collective-permute-start.7 = (bf16[256,576]{1,0:T(8,128)(2,1)S(1)}, bf16[256,576]{1,0:T(8,128)(2,1)S(1)}, u32[]{:S(2)}, u32[]{:S(2)}) collective-permute-start(bf16[256,576]{1,0:T(8,128)(2,1)S(1)} %get-tuple-element.12), channel_id=1, source_target_pairs={{32,0},{48,16},{64,32},{80,48},{96,64},{112,80},{128,96},{144,112}... | collective-permute-start | bytes 884744 | tf_op jit(solution)/shard_map/ppermute | solution.py:534
  102.9 3.1 %collective-permute-start.8 = (bf16[256,576]{1,0:T(8,128)(2,1)S(1)}, bf16[256,576]{1,0:T(8,128)(2,1)S(1)}, u32[]{:S(2)}, u32[]{:S(2)}) collective-permute-start(bf16[256,576]{1,0:T(8,128)(2,1)S(1)} %get-tuple-element.13), channel_id=1, source_target_pairs={{64,0},{80,16},{96,32},{112,48},{128,64},{144,80},{160,96},{176,11... | collective-permute-start | bytes 884744 | tf_op jit(solution)/shard_map/ppermute | solution.py:534
  106.0 3.1 %collective-permute-start.9 = (bf16[256,576]{1,0:T(8,128)(2,1)S(1)}, bf16[256,576]{1,0:T(8,128)(2,1)S(1)}, u32[]{:S(2)}, u32[]{:S(2)}) collective-permute-start(bf16[256,576]{1,0:T(8,128)(2,1)S(1)} %get-tuple-element.14), channel_id=1, source_target_pairs={{448,0},{464,16},{480,32},{496,48},{0,64},{16,80},{32,96},{48,112}... | collective-permute-start | bytes 884744 | tf_op jit(solution)/shard_map/ppermute | solution.py:534
  109.1 0.0 collective-permute-done.10.refs_4_
  109.1 1.4 collective-permute-done.7.refs_1_
  110.5 15.0 %collective-permute-done.8.refs_2_ = bf16[256,576]{1,0:T(8,128)(2,1)S(1)} collective-permute-done((bf16[256,576]{1,0:T(8,128)(2,1)S(1)}, bf16[256,576]{1,0:T(8,128)(2,1)S(1)}, u32[]{:S(2)}, u32[]{:S(2)}) %collective-permute-start.8) | collective-permute-done | bytes 294944 | tf_op jit(solution)/shard_map/ppermute | solution.py:534
  125.4 0.0 collective-permute-done.9.refs_3_
  125.4 0.1 join.1
  125.5 0.7 copy-done.2
  126.2 1.2 copy.8
  127.4 3.8 %collective-permute-start.11 = (bf16[640,576]{0,1:T(8,128)(2,1)}, bf16[640,576]{0,1:T(8,128)(2,1)}, u32[]{:S(2)}, u32[]{:S(2)}) collective-permute-start(bf16[640,576]{0,1:T(8,128)(2,1)} %copy.8), channel_id=1, source_target_pairs={{0,16},{16,0},{32,48},{48,32},{64,80},{80,64},{96,112},{112,96},{1... | collective-permute-start | bytes 2211848 | tf_op jit(solution)/shard_map/ppermute | solution.py:538
  131.2 2.0 %reshape.22.q_ref = bf16[2,128,576]{2,1,0:T(8,128)(2,1)} reshape(bf16[2,73728]{1,0:T(2,128)(2,1)} %param.6) | data formatting | bytes 589824 | tf_op jit(solution)/shard_map/reshape | solution.py:577
  133.2 0.0 collective-permute-done.11
  133.2 1.5 %copy.9.refs_5_ = bf16[640,576]{1,0:T(8,128)(2,1)S(1)} copy(bf16[640,576]{0,1:T(8,128)(2,1)} %collective-permute-done.11) | data formatting | bytes 1474560 | tf_op jit(solution)/shard_map/ppermute | solution.py:538
  134.7 0.0 all-to-all-done.3
  134.8 1.0 copy-done.3
  135.7 1.0 copy-done.4
  136.7 7.5 %attend.1 = (bf16[2,65536]{1,0:T(2,128)(2,1)}, bf16[2,16384]{1,0:T(2,128)(2,1)}) custom-call(bf16[2,128,576]{2,1,0:T(8,128)(2,1)S(1)} %copy-done.4, s32[2,32]{1,0:T(2,128)S(1)} %copy-done.8, bf16[384,1152]{1,0:T(8,128)(2,1)S(1)} %bitcast.7, bf16[1024,1280]{1,0:T(8,128)(2,1)} %bitcast.5.far_ref, bf16[256,576]{1,0:T(8,128)(2,1)S(1)} %get-tuple-element.11.refs_0_, ...), custom_call_target="tpu_custom_call" | custom-call | flops 2415919104 | bytes 6000000 | tf_op jit(solution)/shard_map/attend/pallas_call | solution.py:489
  (13 shorter events, 0.0 us)
Async XLA Ops:
  0.6 1.1 copy-start
  1.7 0.8 copy-start.5
  2.5 0.7 copy-start.6
  3.2 0.7 copy-start.7
  3.8 0.7 copy-start.9
  34.0 23.1 %all-to-all-start.1 = ((bf16[16,144,128]{2,1,0:T(8,128)(2,1)}), bf16[16,144,128]{2,1,0:T(8,128)(2,1)S(1)}, u32[]{:S(2)}, u32[]{:S(2)}) async-start(bf16[16,144,128]{2,1,0:T(8,128)(2,1)} %get-tuple-element.10), calls=%async_computation.1 | async-start | bytes 1179648 | tf_op jit(solution)/shard_map/all_to_all | solution.py:563
  40.8 16.3 %collective-permute-start.1 = (bf16[32,2944]{1,0:T(8,128)(2,1)S(1)}, bf16[32,2944]{1,0:T(8,128)(2,1)S(1)}, u32[]{:S(2)}, u32[]{:S(2)}) collective-permute-start(bf16[32,2944]{1,0:T(8,128)(2,1)S(1)} %bitcast.8), channel_id=1, source_target_pairs={{32,0},{48,16},{64,32},{80,48},{96,64},{112,80},{128,96},{144,112}... | collective-permute-start | bytes 565256 | tf_op jit(solution)/shard_map/ppermute | solution.py:534
  42.7 14.4 %collective-permute-start.2 = (bf16[32,2944]{1,0:T(8,128)(2,1)S(1)}, bf16[32,2944]{1,0:T(8,128)(2,1)S(1)}, u32[]{:S(2)}, u32[]{:S(2)}) collective-permute-start(bf16[32,2944]{1,0:T(8,128)(2,1)S(1)} %bitcast.9), channel_id=1, source_target_pairs={{480,0},{496,16},{0,32},{16,48},{32,64},{48,80},{64,96},{80,112},{... | collective-permute-start | bytes 565256 | tf_op jit(solution)/shard_map/ppermute | solution.py:534
  49.2 10.4 %collective-permute-start.3 = (bf16[32,2944]{1,0:T(8,128)(2,1)S(1)}, bf16[32,2944]{1,0:T(8,128)(2,1)S(1)}, u32[]{:S(2)}, u32[]{:S(2)}) collective-permute-start(bf16[32,2944]{1,0:T(8,128)(2,1)S(1)} %bitcast.10), channel_id=1, source_target_pairs={{64,0},{80,16},{96,32},{112,48},{128,64},{144,80},{160,96},{176,11... | collective-permute-start | bytes 565256 | tf_op jit(solution)/shard_map/ppermute | solution.py:534
  53.3 6.3 %collective-permute-start = (bf16[32,2944]{1,0:T(8,128)(2,1)S(1)}, bf16[32,2944]{1,0:T(8,128)(2,1)S(1)}, u32[]{:S(2)}, u32[]{:S(2)}) collective-permute-start(bf16[32,2944]{1,0:T(8,128)(2,1)S(1)} %bitcast.11), channel_id=1, source_target_pairs={{0,16},{16,0},{32,48},{48,32},{64,80},{80,64},{96,112},{112,96},{1... | collective-permute-start | bytes 565256 | tf_op jit(solution)/shard_map/ppermute | solution.py:538
  61.5 21.3 %all-to-all-start.2 = ((bf16[16,24,1152]{2,1,0:T(8,128)(2,1)}), bf16[16,24,1152]{2,1,0:T(8,128)(2,1)S(1)}, u32[]{:S(2)}, u32[]{:S(2)}) async-start(bf16[16,24,1152]{2,1,0:T(8,128)(2,1)} %bitcast.2), calls=%async_computation.2 | async-start | bytes 1769472 | tf_op jit(solution)/shard_map/all_to_all | solution.py:543
  68.7 9.1 %collective-permute-start.4 = (bf16[32,2944]{1,0:T(8,128)(2,1)S(1)}, bf16[32,2944]{1,0:T(8,128)(2,1)S(1)}, u32[]{:S(2)}, u32[]{:S(2)}) collective-permute-start(bf16[32,2944]{1,0:T(8,128)(2,1)S(1)} %collective-permute-done.1.refs_3_.refs_1_.refs_0_), channel_id=1, source_target_pairs={{0,16},{16,0},{32,48},{48,32},{64,80},{80,64},{96,112},{112,96},{1... | collective-permute-start | bytes 565256 | tf_op jit(solution)/shard_map/ppermute | solution.py:538
  73.4 4.4 %collective-permute-start.5 = (bf16[32,2944]{1,0:T(8,128)(2,1)S(1)}, bf16[32,2944]{1,0:T(8,128)(2,1)S(1)}, u32[]{:S(2)}, u32[]{:S(2)}) collective-permute-start(bf16[32,2944]{1,0:T(8,128)(2,1)S(1)} %collective-permute-done.2.refs_4_.refs_2_.refs_1_), channel_id=1, source_target_pairs={{0,16},{16,0},{32,48},{48,32},{64,80},{80,64},{96,112},{112,96},{1... | collective-permute-start | bytes 565256 | tf_op jit(solution)/shard_map/ppermute | solution.py:538
  75.4 3.5 %collective-permute-start.6 = (bf16[32,2944]{1,0:T(8,128)(2,1)S(1)}, bf16[32,2944]{1,0:T(8,128)(2,1)S(1)}, u32[]{:S(2)}, u32[]{:S(2)}) collective-permute-start(bf16[32,2944]{1,0:T(8,128)(2,1)S(1)} %collective-permute-done.3.refs_5_.refs_3_.refs_2_), channel_id=1, source_target_pairs={{0,16},{16,0},{32,48},{48,32},{64,80},{80,64},{96,112},{112,96},{1... | collective-permute-start | bytes 565256 | tf_op jit(solution)/shard_map/ppermute | solution.py:538
  87.0 7.1 %copy-start.1 = (bf16[512,576]{0,1:T(8,128)(2,1)S(1)}, bf16[512,576]{0,1:T(8,128)(2,1)}, u32[]{:S(2)}) copy-start(bf16[512,576]{0,1:T(8,128)(2,1)} %param.7) | copy-start | bytes 1769476
  87.0 47.7 %all-to-all-start.3 = ((bf16[16,64,1280]{2,1,0:T(8,128)(2,1)}), bf16[16,64,1280]{2,1,0:T(8,128)(2,1)}, u32[]{:S(2)}, u32[]{:S(2)}) async-start(bf16[16,64,1280]{2,1,0:T(8,128)(2,1)} %bitcast.4), calls=%async_computation.3 | async-start | bytes 5242880 | tf_op jit(solution)/shard_map/all_to_all | solution.py:543
  95.4 13.6 %collective-permute-start.10 = (bf16[256,576]{1,0:T(8,128)(2,1)S(1)}, bf16[256,576]{1,0:T(8,128)(2,1)S(1)}, u32[]{:S(2)}, u32[]{:S(2)}) collective-permute-start(bf16[256,576]{1,0:T(8,128)(2,1)S(1)} %get-tuple-element.15), channel_id=1, source_target_pairs={{480,0},{496,16},{0,32},{16,48},{32,64},{48,80},{64,96},{80,112},{... | collective-permute-start | bytes 884744 | tf_op jit(solution)/shard_map/ppermute | solution.py:534
  100.2 10.3 %collective-permute-start.7 = (bf16[256,576]{1,0:T(8,128)(2,1)S(1)}, bf16[256,576]{1,0:T(8,128)(2,1)S(1)}, u32[]{:S(2)}, u32[]{:S(2)}) collective-permute-start(bf16[256,576]{1,0:T(8,128)(2,1)S(1)} %get-tuple-element.12), channel_id=1, source_target_pairs={{32,0},{48,16},{64,32},{80,48},{96,64},{112,80},{128,96},{144,112}... | collective-permute-start | bytes 884744 | tf_op jit(solution)/shard_map/ppermute | solution.py:534
  102.9 22.5 %collective-permute-start.8 = (bf16[256,576]{1,0:T(8,128)(2,1)S(1)}, bf16[256,576]{1,0:T(8,128)(2,1)S(1)}, u32[]{:S(2)}, u32[]{:S(2)}) collective-permute-start(bf16[256,576]{1,0:T(8,128)(2,1)S(1)} %get-tuple-element.13), channel_id=1, source_target_pairs={{64,0},{80,16},{96,32},{112,48},{128,64},{144,80},{160,96},{176,11... | collective-permute-start | bytes 884744 | tf_op jit(solution)/shard_map/ppermute | solution.py:534
  106.0 19.4 %collective-permute-start.9 = (bf16[256,576]{1,0:T(8,128)(2,1)S(1)}, bf16[256,576]{1,0:T(8,128)(2,1)S(1)}, u32[]{:S(2)}, u32[]{:S(2)}) collective-permute-start(bf16[256,576]{1,0:T(8,128)(2,1)S(1)} %get-tuple-element.14), channel_id=1, source_target_pairs={{448,0},{464,16},{480,32},{496,48},{0,64},{16,80},{32,96},{48,112}... | collective-permute-start | bytes 884744 | tf_op jit(solution)/shard_map/ppermute | solution.py:534
  125.4 9.3 %copy-start.8 = (s32[2,32]{1,0:T(2,128)S(1)}, s32[2,32]{1,0:T(2,128)}, u32[]{:S(2)}) copy-start(s32[2,32]{1,0:T(2,128)} %ids_ref.1) | copy-start | bytes 772
  125.5 0.7 copy-start.2
  127.4 5.8 %collective-permute-start.11 = (bf16[640,576]{0,1:T(8,128)(2,1)}, bf16[640,576]{0,1:T(8,128)(2,1)}, u32[]{:S(2)}, u32[]{:S(2)}) collective-permute-start(bf16[640,576]{0,1:T(8,128)(2,1)} %copy.8), channel_id=1, source_target_pairs={{0,16},{16,0},{32,48},{48,32},{64,80},{80,64},{96,112},{112,96},{1... | collective-permute-start | bytes 2211848 | tf_op jit(solution)/shard_map/ppermute | solution.py:538
  134.8 1.0 copy-start.3
  135.7 1.0 copy-start.4

commit v3 on v2

--- a/solution.py
+++ b/solution.py
@@ -19,7 +19,7 @@
 WIDTH = KV_COLS // 2
 IDS_AT = KV_COLS + 4 * ID
 Z_COLS = IDS_AT + 128
-SENT_COLS = WIDTH + 128
+SENT_COLS = KV_COLS + 128
 AWAYS = (0, 1, 2, 14, 15)
 VMEM_LIMIT = 24 * 1024 * 1024
 
@@ -71,7 +71,17 @@
     return jnp.where((away > 2) & (away < 14), t // 96 * 8 + order * 3 + which, -1)
 
 
-def pack_kernel(kv_ref, ik_ref, iq_ref, iw_ref, qb_ref, z_ref, y_ref, keys, rows):
+def pack_kernel(*refs):
+    sources, (z_ref, y_ref, keys, rows), targets, sem = refs[:5], refs[5:9], refs[9:14], refs[14]
+    copies = [
+        pltpu.make_async_copy(source, target, sem.at[n])
+        for n, (source, target) in enumerate(zip(sources, targets))
+    ]
+    for copy in copies:
+        copy.start()
+    for copy in copies:
+        copy.wait()
+    kv_ref, ik_ref, iq_ref, iw_ref, qb_ref = targets
     piece = lax.axis_index("pb")
     shard_keys = kv_ref.shape[1]
     line = iota((PIECE * 8, shard_keys), 0)
@@ -111,9 +121,14 @@
             jax.ShapeDtypeStruct((4, 8, Z_COLS), bf16),
             jax.ShapeDtypeStruct((PLANE, 2 * IH + 16, ID), bf16),
         ),
-        in_specs=[whole()] * 5,
+        in_specs=[anywhere()] * 5,
         out_specs=(whole(), whole()),
-        scratch_shapes=[pltpu.VMEM((32, ID), f32), pltpu.VMEM((2 * IH, ID), f32)],
+        scratch_shapes=[pltpu.VMEM((32, ID), f32), pltpu.VMEM((2 * IH, ID), f32)]
+        + [
+            pltpu.VMEM(value.shape, value.dtype)
+            for value in (kv_turned, index_keys, index_queries, index_weights, q_blocks)
+        ]
+        + [pltpu.SemaphoreType.DMA((5,))],
         compiler_params=params(),
         name="pack",
     )(kv_turned, index_keys, index_queries, index_weights, q_blocks)
@@ -151,23 +166,22 @@
         for p in range(PLANE)
     ]
     keys = slot_keys(span, named_columns(span, rows))
-    each = 2 * slots
+    halves = 2 if span is NEAR else 1
+    each = halves * slots
     pad = -count % 128
-    if pad:
-        keys = jnp.concatenate([keys, jnp.zeros((pad, 128), f32)], axis=0)
-    keys = keys.T[:PLANE, :count]
-    keys = jnp.concatenate([keys, keys], axis=1)
-    line, lane = iota((each, 2 * count), 0), iota((each, 2 * count), 1)
+    keys = jnp.concatenate([keys, jnp.zeros((pad, 128), f32)], axis=0)
+    keys = jnp.concatenate([keys.T[:PLANE, :count]] * halves, axis=1)
+    line, lane = iota((each, halves * count), 0), iota((each, halves * count), 1)
     half = jnp.where(line >= slots, 1, 0)
-    wanted = jnp.where(
-        half == jnp.where(lane >= count, 1, 0), line - half * slots, -5
-    ).astype(f32)
+    there = jnp.where(lane >= count, 1, 0)
+    wanted = jnp.where(half == there, line - half * slots, -5).astype(f32)
     picks = [jnp.where(keys[p : p + 1] == wanted, 1.0, 0.0) for p in range(PLANE)]
     onehot[...] = jnp.concatenate(picks, axis=0).astype(bf16)
-    for c in range(WIDTH // 384):
+    columns = KV_COLS // halves
+    for c in range(columns // 384):
         rows = [
-            ref[:, h * WIDTH + c * 384 : h * WIDTH + (c + 1) * 384]
-            for h in range(2)
+            ref[:, h * columns + c * 384 : h * columns + (c + 1) * 384]
+            for h in range(halves)
             for ref in tables
         ]
         out_ref[:, c * 384 : (c + 1) * 384] = jnp.dot(
@@ -176,8 +190,8 @@
     if scores_ref is not None:
         for p in range(PLANE):
             at = p * each
-            out_ref[at : at + 16, WIDTH:] = scores_ref[p]
-            out_ref[at + 16 : at + each, WIDTH:] = jnp.zeros((each - 16, 128), bf16)
+            out_ref[at : at + 16, columns:] = scores_ref[p]
+            out_ref[at + 16 : at + each, columns:] = jnp.zeros((each - 16, 128), bf16)
 
 
 def gather(name, span, tables, y, afters, scores=None):
@@ -194,6 +208,7 @@
             scores_ref = refs.pop(0)
         gather_kernel(span, held, y_ref, scores_ref, *refs)
 
+    halves = 2 if span is NEAR else 1
     operands = [*tables, y, *afters]
     in_specs = [whole()] * (len(tables) + 1) + [anywhere()] * len(afters)
     columns = WIDTH
@@ -203,10 +218,10 @@
         columns = SENT_COLS
     return pl.pallas_call(
         body,
-        out_shape=jax.ShapeDtypeStruct((PLANE * 2 * slots, columns), bf16),
+        out_shape=jax.ShapeDtypeStruct((PLANE * halves * slots, columns), bf16),
         in_specs=in_specs,
         out_specs=whole(),
-        scratch_shapes=[pltpu.VMEM((PLANE * 2 * slots, 2 * count), bf16)],
+        scratch_shapes=[pltpu.VMEM((PLANE * halves * slots, halves * count), bf16)],
         compiler_params=params(),
         cost_estimate=pl.CostEstimate(
             flops=2 * PLANE * slots * 4 * count * WIDTH,
@@ -239,26 +254,33 @@
         hit = jnp.max(jnp.where(ids == own + b, 1.0, 0.0), axis=1, keepdims=True)
         codes = jnp.where((lane // BLK == b) & (hit > 0.5), taken, codes)
         taken = taken + hit
-    row, lane = iota((128, 512), 0), iota((128, 512), 1)
-    same = row % BLK == lane % BLK
-    kind = (row // BLK).astype(f32)
+    row, lane = iota((64, 512), 0), iota((64, 512), 1)
+    kind = (row // 32).astype(f32)
     for n in range(len(AWAYS)):
         select = jnp.concatenate(
             [
-                jnp.where(same & (codes[m : m + 1, :] == kind), 1.0, 0.0).astype(bf16)
+                jnp.where(
+                    (row % 32 + 32 * half == lane % BLK) & (codes[m : m + 1, :] == kind),
+                    1.0,
+                    0.0,
+                )
+                for half in range(2)
                 for m in (2 * n, 2 * n + 1)
             ],
             axis=0,
+        ).astype(bf16)
+        got = lax.dot_general(
+            select, kv_ref[...], (((1,), (1,)), ((), ())), preferred_element_type=f32
         )
-        outs[n][...] = lax.dot_general(
-            select, kv_ref[...], (((1,), (1,)), ((), ())), preferred_element_type=f32
-        ).astype(bf16)
+        got = (got[:128], got[128:])
+        columns = [part[:, :DL] for part in got] + [part[:, DL:] for part in got]
+        outs[n][...] = jnp.concatenate(columns, axis=1).astype(bf16)
 
 
 def serve(kv_turned, tables, after):
     return pl.pallas_call(
         serve_kernel,
-        out_shape=tuple(jax.ShapeDtypeStruct((4 * BLK, DQK), bf16) for away in AWAYS),
+        out_shape=tuple(jax.ShapeDtypeStruct((2 * BLK, WIDTH), bf16) for away in AWAYS),
         in_specs=[whole()] * 9 + [anywhere()],
         out_specs=(whole(),) * len(AWAYS),
         compiler_params=params(),
@@ -292,23 +314,26 @@
                 ].astype(f32)
     key_rows = keys[...].astype(bf16)
 
-    def peer(p, carry):
+    def peers(g, carry):
         products = lax.dot_general(
-            y_ref[p, 0 : 2 * IH, :],
+            y_ref[pl.ds(g * 4, 4), 0 : 2 * IH, :].reshape(8 * IH, ID),
             key_rows,
             (((1,), (1,)), ((), ())),
             preferred_element_type=f32,
         )
-        weight = jnp.sum(jnp.where(lane == p, weights, 0.0), axis=1, keepdims=True)
-        active = jnp.maximum(products, 0.0) * weight
-        lines = []
-        for i in range(2):
-            total = jnp.sum(active[i * IH : (i + 1) * IH], axis=0, keepdims=True)
-            lines += [total[:, c * 128 : (c + 1) * 128] for c in range(8)]
-        out_ref[p] = jnp.concatenate(lines, axis=0).astype(bf16)
+        for m in range(4):
+            weight = jnp.sum(
+                jnp.where(lane == g * 4 + m, weights, 0.0), axis=1, keepdims=True
+            )
+            active = jnp.maximum(products[m * 2 * IH : (m + 1) * 2 * IH], 0.0) * weight
+            lines = []
+            for i in range(2):
+                total = jnp.sum(active[i * IH : (i + 1) * IH], axis=0, keepdims=True)
+                lines += [total[:, c * 128 : (c + 1) * 128] for c in range(8)]
+            out_ref[g * 4 + m] = jnp.concatenate(lines, axis=0).astype(bf16)
         return carry
 
-    lax.fori_loop(0, PLANE, peer, 0)
+    lax.fori_loop(0, PLANE // 4, peers, 0)
 
 
 def score(tables, y):
@@ -329,13 +354,17 @@
 def attend_kernel(q_ref, ids_ref, near_ref, far_ref, *refs):
     count = len(AWAYS)
     mine, crossed = refs[:count], refs[count]
-    out_ref, index_ref, scores, total, turned = refs[count + 1 :]
-    direct = []
+    out_ref, index_ref, scores, total, turned, direct, sem = refs[count + 1 :]
+    copies = []
     for n in range(count):
-        direct.append((mine[n], slice(0, 128)))
-        direct.append((crossed, slice(n * 128, (n + 1) * 128)))
-    at = lax.axis_index("ctx")
-    rank = at * PLANE + lax.axis_index("pb")
+        for other in range(2):
+            source = crossed.at[pl.ds(n * 64, 64)] if other else mine[n].at[pl.ds(0, 64)]
+            target = direct.at[pl.ds((2 * n + other) * 64, 64)]
+            copies.append(pltpu.make_async_copy(source, target, sem.at[2 * n + other]))
+    for copy in copies:
+        copy.start()
+    ctx = lax.axis_index("ctx")
+    rank = ctx * PLANE + lax.axis_index("pb")
     ids = ids_ref[...]
     own_block = 240 + rank * 2 // BLK
     own_row = table_row(own_block)
@@ -367,56 +396,13 @@
     def product(left, right):
         return lax.dot_general(left, right, contract, preferred_element_type=f32)
 
-    count = 8 * len(direct)
-    line = iota((count, 128), 0)
-    lane = iota((count, 128), 1)
-    named = jnp.zeros((count, 128), f32)
-    shard = ids // 8
-    away = (shard // 2 - at // 2 + LEVELS) % LEVELS
-    turn = jnp.where(away < 3, away, jnp.where(away > 13, away - 11, -8))
-    place = (turn * 2 + (shard + at) % 2) * 8 + ids % 8
-    own_away = (own_block // 16 - at // 2 + LEVELS) % LEVELS
-    own_turn = jnp.where(own_away < 3, own_away, jnp.where(own_away > 13, own_away - 11, -8))
-    own_place = (own_turn * 2 + (own_block // 8 + at) % 2) * 8 + own_block % 8
-    for i in range(2):
-        hit = jnp.where(place[i : i + 1] == iota((count, ids.shape[1]), 0), 1.0, 0.0)
-        named = jnp.where(lane == i, jnp.max(hit, axis=1, keepdims=True), named)
-    members = named
-    named = jnp.maximum(named[:, 0:1], named[:, 1:2])
-    code = slot_codes((0, count, 2), jnp.broadcast_to(named, (count, 128)))
-    chosen = code == (lane // BLK).astype(f32)
-    limits = []
-    for i in range(2):
-        limit = jnp.where(line[:, 0:1] == own_place, offsets[i], 63.0) + 1.0
-        limit = jnp.where(members[:, i : i + 1] > 0.5, limit, 0.0)
-        limits.append(jnp.where(chosen, limit, 0.0))
-    here = (iota((1, 128), 1) % BLK).astype(f32)
-    here = jnp.concatenate([here, here], axis=1)
-    for n in range(0, len(direct), 2):
-        pair = direct[n : n + 2]
-        block = product(
-            latent, jnp.concatenate([ref[rows, :DL] for ref, rows in pair], axis=0)
-        ) + product(
-            rotary, jnp.concatenate([ref[rows, DL:] for ref, rows in pair], axis=0)
-        )
-        shown = [
-            jnp.concatenate(
-                [
-                    jnp.sum(limit[m * 8 : (m + 1) * 8], axis=0, keepdims=True)
-                    for m in (n, n + 1)
-                ],
-                axis=1,
-            )
-            for limit in limits
-        ]
-        keep(block, here, shown, [(ref, rows, slice(0, DL)) for ref, rows in pair])
-
     for span, ref, step in ((NEAR, near_ref, 384), (FAR, far_ref, 256)):
         first, count, slots = span
         one, two = named_columns(span, [ids[0:1]]), named_columns(span, [ids[1:2]])
         members = (one[:, 0:1], two[:, 0:1])
         keys = slot_keys(span, jnp.maximum(one, two))[:, 0:1]
-        width = PLANE * 2 * slots
+        halves = 2 if span is NEAR else 1
+        width = PLANE * halves * slots
         line = iota((count, 128), 0)
         chosen = keys == (iota((1, width), 1) % slots).astype(f32)
         limits = []
@@ -425,20 +411,77 @@
             limit = jnp.where(members[i] > 0.5, limit, 0.0)
             limits.append(jnp.sum(jnp.where(chosen, limit, 0.0), axis=0, keepdims=True))
         lane = iota((1, width), 1)
-        place = lane // (2 * slots) * PIECE + lane // slots % 2 * 2
+        place = lane // (halves * slots) * PIECE
+        if halves == 2:
+            place = place + lane // slots % 2 * 2
         for k in range(width // step):
             rows = slice(k * step, (k + 1) * step)
-            for parity in range(2):
-                columns = slice(parity * DL, (parity + 1) * DL)
+            for r in range(PIECE // halves):
+                half, parity = r // 2, r % 2
+                at = half * WIDTH + parity * DL
+                columns = slice(at, at + DL)
+                turn = half * WIDTH + 2 * DL
                 block = product(latent, ref[rows, columns]) + product(
-                    padded[parity], ref[rows, 2 * DL : 2 * DL + 128]
+                    padded[parity], ref[rows, turn : turn + 128]
                 )
                 keep(
                     block,
-                    (place[:, rows] + parity).astype(f32),
+                    (place[:, rows] + r).astype(f32),
                     [limit[:, rows] for limit in limits],
                     [(ref, rows, columns)],
                 )
+
+    count = 16 * len(AWAYS)
+    line = iota((count, 128), 0)
+    lane = iota((count, 128), 1)
+    named = jnp.zeros((count, 128), f32)
+    shard = ids // 8
+    away = (shard // 2 - ctx // 2 + LEVELS) % LEVELS
+    turn = jnp.where(away < 3, away, jnp.where(away > 13, away - 11, -8))
+    place = (turn * 2 + (shard + ctx) % 2) * 8 + ids % 8
+    own_away = (own_block // 16 - ctx // 2 + LEVELS) % LEVELS
+    own_turn = jnp.where(own_away < 3, own_away, jnp.where(own_away > 13, own_away - 11, -8))
+    own_place = (own_turn * 2 + (own_block // 8 + ctx) % 2) * 8 + own_block % 8
+    for i in range(2):
+        hit = jnp.where(place[i : i + 1] == iota((count, ids.shape[1]), 0), 1.0, 0.0)
+        named = jnp.where(lane == i, jnp.max(hit, axis=1, keepdims=True), named)
+    members = named
+    named = jnp.maximum(named[:, 0:1], named[:, 1:2])
+    code = slot_codes((0, count, 2), jnp.broadcast_to(named, (count, 128)))
+    chosen = code == (lane // 32 % 2).astype(f32)
+    limits = []
+    for i in range(2):
+        limit = jnp.where(line[:, 0:1] == own_place, offsets[i], 63.0) + 1.0
+        limit = jnp.where(members[:, i : i + 1] > 0.5, limit, 0.0)
+        limits.append(jnp.where(chosen, limit, 0.0))
+    low = iota((1, 128), 1) < 64
+    shown = [
+        [
+            jnp.where(
+                low,
+                jnp.sum(limit[n * 8 : (n + 1) * 8], axis=0, keepdims=True),
+                jnp.sum(limit[(n + 1) * 8 : (n + 2) * 8], axis=0, keepdims=True),
+            )
+            for n in range(0, 2 * len(AWAYS), 2)
+        ]
+        for limit in limits
+    ]
+    here = iota((1, 128), 1) % 32
+    for copy in copies:
+        copy.wait()
+    for first, last in ((0, 2), (2, 4), (4, 5)):
+        rows = slice(first * 128, last * 128)
+        for parity in range(2):
+            columns = slice(parity * DL, (parity + 1) * DL)
+            block = product(latent, direct[rows, columns]) + product(
+                padded[parity], direct[rows, 2 * DL : 2 * DL + 128]
+            )
+            keep(
+                block,
+                jnp.concatenate([(here + 32 * parity).astype(f32)] * (last - first), axis=1),
+                [jnp.concatenate(each[first:last], axis=1) for each in shown],
+                [(direct, rows, columns)],
+            )
 
     highest = jnp.max(jnp.concatenate(tops, axis=0), axis=1, keepdims=True)
     norm = jnp.zeros((2 * HEADS, 128), f32)
@@ -465,7 +508,7 @@
             out_ref[:, at : at + 128] = total[k, pl.ds(h, 2, stride=HEADS), :].astype(bf16)
 
     tiles = [
-        far_ref[p * 2 * FAR[2] : p * 2 * FAR[2] + 16, WIDTH:].astype(f32)
+        far_ref[p * FAR[2] : p * FAR[2] + 16, KV_COLS:].astype(f32)
         for p in range(PLANE)
     ]
     group = iota((16, 128), 1) // 32
@@ -492,12 +535,14 @@
             jax.ShapeDtypeStruct((2, HEADS * DL), bf16),
             jax.ShapeDtypeStruct((2, 16384), bf16),
         ),
-        in_specs=[whole()] * (5 + len(mine)),
+        in_specs=[whole()] * 4 + [anywhere()] * (1 + len(mine)),
         out_specs=(whole(), whole()),
         scratch_shapes=[
             pltpu.VMEM((2 * HEADS, 4096), f32),
             pltpu.VMEM((4, 2 * HEADS, 128), f32),
             pltpu.VMEM((256, 128), f32),
+            pltpu.VMEM((128 * len(AWAYS), WIDTH), bf16),
+            pltpu.SemaphoreType.DMA((2 * len(AWAYS),)),
         ],
         compiler_params=params(),
         cost_estimate=pl.CostEstimate(
@@ -507,16 +552,25 @@
     )(query, ids, near, far, *mine, crossed)
 
 
+def two_levels_on(value):
+    pairs = [
+        ((level + (2, -2)[core]) % LEVELS * 2 + core, level * 2 + core)
+        for level in range(LEVELS)
+        for core in range(2)
+    ]
+    return lax.ppermute(value, "ctx", pairs)
+
+
 def join_kernel(*refs):
     out_ref = refs[-1]
     for n, ref in enumerate(refs[:-1]):
-        out_ref[n * 128 : (n + 1) * 128, :] = ref[128:, :]
+        out_ref[n * 64 : (n + 1) * 64, :] = ref[64:, :]
 
 
 def join(parts):
     return pl.pallas_call(
         join_kernel,
-        out_shape=jax.ShapeDtypeStruct((len(parts) * 128, DQK), bf16),
+        out_shape=jax.ShapeDtypeStruct((len(parts) * 64, WIDTH), bf16),
         in_specs=[whole()] * len(parts),
         out_specs=whole(),
         compiler_params=params(),
@@ -562,7 +616,7 @@
     held = outer_levels(z)
     y = lax.all_to_all(y, "pb", split_axis=0, concat_axis=0, tiled=True)
     across = swap(held)
-    others = [level_from(held, away) for away in (1, 15, 2)]
+    others = [level_from(held, 1), level_from(held, 15), two_levels_on(held)]
     near = exchange(gather("near", NEAR, [held, across], y, others))
     swapped = [swap(other) for other in others]
     tables = [held] + others + [across] + swapped

time: 146 us -> 140 us (0.959)
  starting transfers between devices: 63.8 us -> 59.9 us
  waiting for transfers between devices: 19.8 us -> 23.5 us
  local copies, waits for them, and re-layouts: 11.2 us -> 7.71 us
  Pallas kernels: 20.1 us -> 18.5 us
    ppermute x7 -> x6, starting transfers between devices: 26.1 us -> 18.7 us  [level_from(): return lax.ppermute(value, 'ctx', pairs)]
    ppermute x0 -> x1, starting transfers between devices: none -> 6.95 us  [two_levels_on(): return lax.ppermute(value, 'ctx', pairs)]
    all_to_all x2, waiting for transfers between devices: 0.01 us -> 3.18 us  [exchange(): got = lax.all_to_all(parts, 'pb', split_axis=0, concat_axis=0, tiled=True)]
    all_to_all x2, starting transfers between devices: 14.3 us -> 11.6 us  [exchange(): got = lax.all_to_all(parts, 'pb', split_axis=0, concat_axis=0, tiled=True)]
    pallas_call x1, Pallas kernels: 3.98 us -> 1.94 us  [score(): pl.pallas_call(score_kernel, out_shape=jax.ShapeDtypeStruct((PLANE, 16, 1...]
    ppermute x5, waiting for transfers between devices: 1.03 us -> 2.68 us  [swap(): lax.ppermute(value, 'ctx', [(at, at ^ 1) for at in range(2 * LEVELS)])]
    ppermute x1 -> x0, local copies, waits for them, and re-layouts: 1.49 us -> none  [swap(): lax.ppermute(value, 'ctx', [(at, at ^ 1) for at in range(2 * LEVELS)])]
    ppermute x7 -> x6, waiting for transfers between devices: 18.8 us -> 17.6 us  [level_from(): return lax.ppermute(value, 'ctx', pairs)]
  transfers between devices with their start and end apart: 15 -> 15, of which waited for: 4 -> 7; matrix products, arithmetic and copies ran while one was open for 3% -> 1% of each run, Pallas kernels for 4% -> 2%
where the time goes in v3:
time: 140 us; the launch traced here: 139 us
  starting transfers between devices  59.9 us (43%)
  blocking collectives  28.3 us (20%)
  waiting for transfers between devices  23.5 us (17%)
  Pallas kernels  18.5 us (13%)
  local copies, waits for them, and re-layouts  7.71 us (6%)
    all_to_all x1, blocking collectives, outer_levels(): lax.all_to_all(chunks, 'ctx', split_axis=0, concat_axis=0, axis_index_gro...  28.3 us
    ppermute x6, starting transfers between devices, level_from(): return lax.ppermute(value, 'ctx', pairs)  18.7 us
    ppermute x6, waiting for transfers between devices, level_from(): return lax.ppermute(value, 'ctx', pairs)  17.6 us
    ppermute x5, starting transfers between devices, swap(): lax.ppermute(value, 'ctx', [(at, at ^ 1) for at in range(2 * LEVELS)])  15.8 us
    all_to_all x2, starting transfers between devices, exchange(): got = lax.all_to_all(parts, 'pb', split_axis=0, concat_axis=0, tiled=True)  11.6 us
    pallas_call x1, Pallas kernels, attend(): pl.pallas_call(attend_kernel, out_shape=(jax.ShapeDtypeStruct((2, HEADS *...  8.37 us
    ppermute x1, starting transfers between devices, two_levels_on(): return lax.ppermute(value, 'ctx', pairs)  6.95 us
    all_to_all x1, starting transfers between devices, local(): y = lax.all_to_all(y, 'pb', split_axis=0, concat_axis=0, tiled=True)  6.76 us
  transfers between devices with their start and end apart: 15, of which 7 were waited for; matrix products, arithmetic and copies ran while one was open for 1% of the time, Pallas kernels for 2%

profile of v3, /device:TPU:1, one launch (start us, length us, event | category | flops | bytes accessed | tf_op | source)
XLA Modules:
  0.0 138.8 jit_solution(2396436998127601997)
XLA Ops:
  0.6 0.0 copy-start
  0.6 1.1 copy-done
  1.7 0.8 copy-done.6
  2.5 0.7 copy-done.7
  3.2 0.7 copy-done.8
  3.8 0.7 copy-done.10
  4.5 1.4 %pack.1 = (bf16[4,8,2944]{2,1,0:T(8,128)(2,1)S(1)}, bf16[16,144,128]{2,1,0:T(8,128)(2,1)}) custom-call(bf16[576,512]{1,0:T(8,128)(2,1)S(1)} %bitcast.15, bf16[32,128]{1,0:T(8,128)(2,1)S(1)} %copy-done.7, bf16[2,8192]{1,0:T(2,128)(2,1)S(1)} %copy-done.6, bf16[2,64]{1,0:T(2,128)(2,1)S(1)} %copy-done.10, s32[2,32]{1,0:T(2,128)S(1)} %copy-done.8), custom_call_target="tpu_custom_call" | custom-call | tf_op jit(solution)/shard_map/pack/pallas_call | solution.py:118
  5.9 28.3 %all_to_all.20 = bf16[4,8,2944]{2,1,0:T(8,128)(2,1)S(1)} all-to-all(bf16[4,8,2944]{2,1,0:T(8,128)(2,1)S(1)} %get-tuple-element.9), channel_id=1, replica_groups={{0,128,256,384},{16,144,272,400},{32,160,288,416},{48,176,304,432},{64,..., dimensions={0} | all-to-all | bytes 376832 | tf_op jit(solution)/shard_map/all_to_all | solution.py:607
  34.2 6.8 %all-to-all-start.1 = ((bf16[16,144,128]{2,1,0:T(8,128)(2,1)}), bf16[16,144,128]{2,1,0:T(8,128)(2,1)S(1)}, u32[]{:S(2)}, u32[]{:S(2)}) async-start(bf16[16,144,128]{2,1,0:T(8,128)(2,1)} %get-tuple-element.10), calls=%async_computation.1 | async-start | bytes 1179648 | tf_op jit(solution)/shard_map/all_to_all | solution.py:617
  41.0 7.0 %collective-permute-start.3 = (bf16[32,2944]{1,0:T(8,128)(2,1)S(1)}, bf16[32,2944]{1,0:T(8,128)(2,1)S(1)}, u32[]{:S(2)}, u32[]{:S(2)}) collective-permute-start(bf16[32,2944]{1,0:T(8,128)(2,1)S(1)} %bitcast.8), channel_id=1, source_target_pairs={{64,0},{464,16},{96,32},{496,48},{128,64},{16,80},{160,96},{48,112... | collective-permute-start | bytes 565256 | tf_op jit(solution)/shard_map/ppermute | solution.py:561
  48.0 1.9 %collective-permute-start.2 = (bf16[32,2944]{1,0:T(8,128)(2,1)S(1)}, bf16[32,2944]{1,0:T(8,128)(2,1)S(1)}, u32[]{:S(2)}, u32[]{:S(2)}) collective-permute-start(bf16[32,2944]{1,0:T(8,128)(2,1)S(1)} %bitcast.9), channel_id=1, source_target_pairs={{480,0},{496,16},{0,32},{16,48},{32,64},{48,80},{64,96},{80,112},{... | collective-permute-start | bytes 565256 | tf_op jit(solution)/shard_map/ppermute | solution.py:588
  49.9 4.6 %collective-permute-start.1 = (bf16[32,2944]{1,0:T(8,128)(2,1)S(1)}, bf16[32,2944]{1,0:T(8,128)(2,1)S(1)}, u32[]{:S(2)}, u32[]{:S(2)}) collective-permute-start(bf16[32,2944]{1,0:T(8,128)(2,1)S(1)} %bitcast.10), channel_id=1, source_target_pairs={{32,0},{48,16},{64,32},{80,48},{96,64},{112,80},{128,96},{144,112}... | collective-permute-start | bytes 565256 | tf_op jit(solution)/shard_map/ppermute | solution.py:588
  54.5 4.1 %collective-permute-start = (bf16[32,2944]{1,0:T(8,128)(2,1)S(1)}, bf16[32,2944]{1,0:T(8,128)(2,1)S(1)}, u32[]{:S(2)}, u32[]{:S(2)}) collective-permute-start(bf16[32,2944]{1,0:T(8,128)(2,1)S(1)} %bitcast.11), channel_id=1, source_target_pairs={{0,16},{16,0},{32,48},{48,32},{64,80},{80,64},{96,112},{112,96},{1... | collective-permute-start | bytes 565256 | tf_op jit(solution)/shard_map/ppermute | solution.py:592
  58.5 0.0 all-to-all-done.1.refs_2_.refs_8_.refs_6_
  58.6 0.0 collective-permute-done.3.refs_5_.refs_3_.refs_2_
  58.6 0.0 collective-permute-done.2.refs_4_.refs_2_.refs_1_
  58.6 0.0 collective-permute-done.1.refs_3_.refs_1_.refs_0_
  58.6 1.0 collective-permute-done.refs_1_.refs_4_
  59.6 1.9 %near.1 = bf16[384,1152]{1,0:T(8,128)(2,1)} custom-call(bf16[32,2944]{1,0:T(8,128)(2,1)S(1)} %bitcast.12, bf16[32,2944]{1,0:T(8,128)(2,1)S(1)} %collective-permute-done.refs_1_.refs_4_, bf16[16,144,128]{2,1,0:T(8,128)(2,1)S(1)} %all-to-all-done.1.refs_2_.refs_8_.refs_6_, bf16[32,2944]{1,0:T(8,128)(2,1)S(1)} %collective-permute-done.1.refs_3_.refs_1_.refs_0_, ...), custom_call_target="tpu_custom_call" | custom-call | flops 113246208 | bytes 3000000 | tf_op jit(solution)/shard_map/near/pallas_call | solution.py:219
  61.5 6.9 %all-to-all-start.2 = ((bf16[16,24,1152]{2,1,0:T(8,128)(2,1)}), bf16[16,24,1152]{2,1,0:T(8,128)(2,1)S(1)}, u32[]{:S(2)}, u32[]{:S(2)}) async-start(bf16[16,24,1152]{2,1,0:T(8,128)(2,1)} %bitcast.2), calls=%async_computation.2 | async-start | bytes 1769472 | tf_op jit(solution)/shard_map/all_to_all | solution.py:597
  68.4 3.3 %collective-permute-start.6 = (bf16[32,2944]{1,0:T(8,128)(2,1)S(1)}, bf16[32,2944]{1,0:T(8,128)(2,1)S(1)}, u32[]{:S(2)}, u32[]{:S(2)}) collective-permute-start(bf16[32,2944]{1,0:T(8,128)(2,1)S(1)} %collective-permute-done.3.refs_5_.refs_3_.refs_2_), channel_id=1, source_target_pairs={{0,16},{16,0},{32,48},{48,32},{64,80},{80,64},{96,112},{112,96},{1... | collective-permute-start | bytes 565256 | tf_op jit(solution)/shard_map/ppermute | solution.py:592
  71.7 1.9 %collective-permute-start.5 = (bf16[32,2944]{1,0:T(8,128)(2,1)S(1)}, bf16[32,2944]{1,0:T(8,128)(2,1)S(1)}, u32[]{:S(2)}, u32[]{:S(2)}) collective-permute-start(bf16[32,2944]{1,0:T(8,128)(2,1)S(1)} %collective-permute-done.2.refs_4_.refs_2_.refs_1_), channel_id=1, source_target_pairs={{0,16},{16,0},{32,48},{48,32},{64,80},{80,64},{96,112},{112,96},{1... | collective-permute-start | bytes 565256 | tf_op jit(solution)/shard_map/ppermute | solution.py:592
  73.7 2.4 %collective-permute-start.4 = (bf16[32,2944]{1,0:T(8,128)(2,1)S(1)}, bf16[32,2944]{1,0:T(8,128)(2,1)S(1)}, u32[]{:S(2)}, u32[]{:S(2)}) collective-permute-start(bf16[32,2944]{1,0:T(8,128)(2,1)S(1)} %collective-permute-done.1.refs_3_.refs_1_.refs_0_), channel_id=1, source_target_pairs={{0,16},{16,0},{32,48},{48,32},{64,80},{80,64},{96,112},{112,96},{1... | collective-permute-start | bytes 565256 | tf_op jit(solution)/shard_map/ppermute | solution.py:592
  76.1 0.0 collective-permute-done.6.refs_7_.refs_5_
  76.1 0.0 collective-permute-done.5.refs_6_.refs_4_
  76.1 1.0 collective-permute-done.4.refs_5_.refs_3_
  77.1 1.9 %score.1.refs_8_ = bf16[16,16,128]{2,1,0:T(8,128)(2,1)S(1)} custom-call(bf16[32,2944]{1,0:T(8,128)(2,1)S(1)} %bitcast.13, bf16[32,2944]{1,0:T(8,128)(2,1)S(1)} %collective-permute-done.1.refs_3_.refs_1_.refs_0_, bf16[32,2944]{1,0:T(8,128)(2,1)S(1)} %collective-permute-done.2.refs_4_.refs_2_.refs_1_, ...), custom_call_target="tpu_custom_call" | custom-call | flops 536870912 | bytes 2000000 | tf_op jit(solution)/shard_map/score/pallas_call | solution.py:340
  79.1 3.2 %all-to-all-done.2 = bf16[16,24,1152]{2,1,0:T(8,128)(2,1)S(1)} async-done(((bf16[16,24,1152]{2,1,0:T(8,128)(2,1)}), bf16[16,24,1152]{2,1,0:T(8,128)(2,1)S(1)}, u32[]{:S(2)}, u32[]{:S(2)}) %all-to-all-start.2) | async-done | bytes 884768 | tf_op jit(solution)/shard_map/all_to_all | solution.py:597
  82.2 3.5 %far.1.refs_8_ = bf16[512,2432]{1,0:T(8,128)(2,1)} custom-call(bf16[32,2944]{1,0:T(8,128)(2,1)S(1)} %collective-permute-done.1.refs_3_.refs_1_.refs_0_, bf16[32,2944]{1,0:T(8,128)(2,1)S(1)} %collective-permute-done.2.refs_4_.refs_2_.refs_1_, bf16[32,2944]{1,0:T(8,128)(2,1)S(1)} %collective-permute-done.3.refs_5_.refs_3_.refs_2_, ...), custom_call_target="tpu_custom_call" | custom-call | flops 905969664 | bytes 3000000 | tf_op jit(solution)/shard_map/far/pallas_call | solution.py:219
  85.7 4.7 %all-to-all-start.3 = ((bf16[16,32,2432]{2,1,0:T(8,128)(2,1)}), bf16[16,32,2432]{2,1,0:T(8,128)(2,1)}, u32[]{:S(2)}, u32[]{:S(2)}) async-start(bf16[16,32,2432]{2,1,0:T(8,128)(2,1)} %bitcast.4), calls=%async_computation.3 | async-start | bytes 4980736 | tf_op jit(solution)/shard_map/all_to_all | solution.py:597
  90.4 1.4 serve.1
  91.8 0.0 copy-start.9
  91.8 4.1 %collective-permute-start.7 = (bf16[128,1152]{1,0:T(8,128)(2,1)S(1)}, bf16[128,1152]{1,0:T(8,128)(2,1)S(1)}, u32[]{:S(2)}, u32[]{:S(2)}) collective-permute-start(bf16[128,1152]{1,0:T(8,128)(2,1)S(1)} %get-tuple-element.12), channel_id=1, source_target_pairs={{32,0},{48,16},{64,32},{80,48},{96,64},{112,80},{128,96},{144,112}... | collective-permute-start | bytes 884744 | tf_op jit(solution)/shard_map/ppermute | solution.py:588
  95.9 1.9 %collective-permute-start.8 = (bf16[128,1152]{1,0:T(8,128)(2,1)S(1)}, bf16[128,1152]{1,0:T(8,128)(2,1)S(1)}, u32[]{:S(2)}, u32[]{:S(2)}) collective-permute-start(bf16[128,1152]{1,0:T(8,128)(2,1)S(1)} %get-tuple-element.13), channel_id=1, source_target_pairs={{64,0},{80,16},{96,32},{112,48},{128,64},{144,80},{160,96},{176,11... | collective-permute-start | bytes 884744 | tf_op jit(solution)/shard_map/ppermute | solution.py:588
  97.9 4.3 %collective-permute-start.9 = (bf16[128,1152]{1,0:T(8,128)(2,1)S(1)}, bf16[128,1152]{1,0:T(8,128)(2,1)S(1)}, u32[]{:S(2)}, u32[]{:S(2)}) collective-permute-start(bf16[128,1152]{1,0:T(8,128)(2,1)S(1)} %get-tuple-element.14), channel_id=1, source_target_pairs={{448,0},{464,16},{480,32},{496,48},{0,64},{16,80},{32,96},{48,112}... | collective-permute-start | bytes 884744 | tf_op jit(solution)/shard_map/ppermute | solution.py:588
  102.1 1.9 %collective-permute-start.10 = (bf16[128,1152]{1,0:T(8,128)(2,1)S(1)}, bf16[128,1152]{1,0:T(8,128)(2,1)S(1)}, u32[]{:S(2)}, u32[]{:S(2)}) collective-permute-start(bf16[128,1152]{1,0:T(8,128)(2,1)S(1)} %get-tuple-element.15), channel_id=1, source_target_pairs={{480,0},{496,16},{0,32},{16,48},{32,64},{48,80},{64,96},{80,112},{... | collective-permute-start | bytes 884744 | tf_op jit(solution)/shard_map/ppermute | solution.py:588
  104.1 7.9 %collective-permute-done.8.refs_2_ = bf16[128,1152]{1,0:T(8,128)(2,1)S(1)} collective-permute-done((bf16[128,1152]{1,0:T(8,128)(2,1)S(1)}, bf16[128,1152]{1,0:T(8,128)(2,1)S(1)}, u32[]{:S(2)}, u32[]{:S(2)}) %collective-permute-start.8) | collective-permute-done | bytes 294944 | tf_op jit(solution)/shard_map/ppermute | solution.py:588
  112.0 1.3 collective-permute-done.9.refs_3_
  113.3 8.4 %collective-permute-done.10.refs_4_ = bf16[128,1152]{1,0:T(8,128)(2,1)S(1)} collective-permute-done((bf16[128,1152]{1,0:T(8,128)(2,1)S(1)}, bf16[128,1152]{1,0:T(8,128)(2,1)S(1)}, u32[]{:S(2)}, u32[]{:S(2)}) %collective-permute-start.10) | collective-permute-done | bytes 294944 | tf_op jit(solution)/shard_map/ppermute | solution.py:588
  121.7 0.1 join.1
  121.7 0.6 copy-done.4
  122.4 4.2 %collective-permute-start.11 = (bf16[320,1152]{1,0:T(8,128)(2,1)S(1)}, bf16[320,1152]{1,0:T(8,128)(2,1)}, u32[]{:S(2)}, u32[]{:S(2)}) collective-permute-start(bf16[320,1152]{1,0:T(8,128)(2,1)S(1)} %join.1), channel_id=1, source_target_pairs={{0,16},{16,0},{32,48},{48,32},{64,80},{80,64},{96,112},{112,96},{1... | collective-permute-start | bytes 2211848 | tf_op jit(solution)/shard_map/ppermute | solution.py:592
  126.6 1.3 reshape.22.q_ref
  127.9 0.7 collective-permute-done.11.refs_5_
  128.5 0.0 all-to-all-done.3
  128.5 1.0 copy-done.3
  129.5 1.0 copy-done.5
  130.4 8.4 %attend.1 = (bf16[2,65536]{1,0:T(2,128)(2,1)}, bf16[2,16384]{1,0:T(2,128)(2,1)}) custom-call(bf16[2,128,576]{2,1,0:T(8,128)(2,1)S(1)} %reshape.22.q_ref, s32[2,32]{1,0:T(2,128)S(1)} %copy-done.9, bf16[384,1152]{1,0:T(8,128)(2,1)S(1)} %bitcast.7, bf16[512,2432]{1,0:T(8,128)(2,1)} %bitcast.5.far_ref, bf16[128,1152]{1,0:T(8,128)(2,1)S(1)} %get-tuple-element.11.refs_0_, ...), custom_call_target="tpu_custom_call" | custom-call | flops 2415919104 | bytes 6000000 | tf_op jit(solution)/shard_map/attend/pallas_call | solution.py:532
  (13 shorter events, 0.0 us)
Async XLA Ops:
  0.6 1.1 copy-start
  1.7 0.8 copy-start.6
  2.5 0.7 copy-start.7
  3.2 0.7 copy-start.8
  3.8 0.7 copy-start.10
  34.2 24.3 %all-to-all-start.1 = ((bf16[16,144,128]{2,1,0:T(8,128)(2,1)}), bf16[16,144,128]{2,1,0:T(8,128)(2,1)S(1)}, u32[]{:S(2)}, u32[]{:S(2)}) async-start(bf16[16,144,128]{2,1,0:T(8,128)(2,1)} %get-tuple-element.10), calls=%async_computation.1 | async-start | bytes 1179648 | tf_op jit(solution)/shard_map/all_to_all | solution.py:617
  41.0 17.6 %collective-permute-start.3 = (bf16[32,2944]{1,0:T(8,128)(2,1)S(1)}, bf16[32,2944]{1,0:T(8,128)(2,1)S(1)}, u32[]{:S(2)}, u32[]{:S(2)}) collective-permute-start(bf16[32,2944]{1,0:T(8,128)(2,1)S(1)} %bitcast.8), channel_id=1, source_target_pairs={{64,0},{464,16},{96,32},{496,48},{128,64},{16,80},{160,96},{48,112... | collective-permute-start | bytes 565256 | tf_op jit(solution)/shard_map/ppermute | solution.py:561
  48.0 10.6 %collective-permute-start.2 = (bf16[32,2944]{1,0:T(8,128)(2,1)S(1)}, bf16[32,2944]{1,0:T(8,128)(2,1)S(1)}, u32[]{:S(2)}, u32[]{:S(2)}) collective-permute-start(bf16[32,2944]{1,0:T(8,128)(2,1)S(1)} %bitcast.9), channel_id=1, source_target_pairs={{480,0},{496,16},{0,32},{16,48},{32,64},{48,80},{64,96},{80,112},{... | collective-permute-start | bytes 565256 | tf_op jit(solution)/shard_map/ppermute | solution.py:588
  49.9 8.7 %collective-permute-start.1 = (bf16[32,2944]{1,0:T(8,128)(2,1)S(1)}, bf16[32,2944]{1,0:T(8,128)(2,1)S(1)}, u32[]{:S(2)}, u32[]{:S(2)}) collective-permute-start(bf16[32,2944]{1,0:T(8,128)(2,1)S(1)} %bitcast.10), channel_id=1, source_target_pairs={{32,0},{48,16},{64,32},{80,48},{96,64},{112,80},{128,96},{144,112}... | collective-permute-start | bytes 565256 | tf_op jit(solution)/shard_map/ppermute | solution.py:588
  54.5 5.1 %collective-permute-start = (bf16[32,2944]{1,0:T(8,128)(2,1)S(1)}, bf16[32,2944]{1,0:T(8,128)(2,1)S(1)}, u32[]{:S(2)}, u32[]{:S(2)}) collective-permute-start(bf16[32,2944]{1,0:T(8,128)(2,1)S(1)} %bitcast.11), channel_id=1, source_target_pairs={{0,16},{16,0},{32,48},{48,32},{64,80},{80,64},{96,112},{112,96},{1... | collective-permute-start | bytes 565256 | tf_op jit(solution)/shard_map/ppermute | solution.py:592
  61.5 20.7 %all-to-all-start.2 = ((bf16[16,24,1152]{2,1,0:T(8,128)(2,1)}), bf16[16,24,1152]{2,1,0:T(8,128)(2,1)S(1)}, u32[]{:S(2)}, u32[]{:S(2)}) async-start(bf16[16,24,1152]{2,1,0:T(8,128)(2,1)} %bitcast.2), calls=%async_computation.2 | async-start | bytes 1769472 | tf_op jit(solution)/shard_map/all_to_all | solution.py:597
  68.4 7.6 %collective-permute-start.6 = (bf16[32,2944]{1,0:T(8,128)(2,1)S(1)}, bf16[32,2944]{1,0:T(8,128)(2,1)S(1)}, u32[]{:S(2)}, u32[]{:S(2)}) collective-permute-start(bf16[32,2944]{1,0:T(8,128)(2,1)S(1)} %collective-permute-done.3.refs_5_.refs_3_.refs_2_), channel_id=1, source_target_pairs={{0,16},{16,0},{32,48},{48,32},{64,80},{80,64},{96,112},{112,96},{1... | collective-permute-start | bytes 565256 | tf_op jit(solution)/shard_map/ppermute | solution.py:592
  71.7 4.4 %collective-permute-start.5 = (bf16[32,2944]{1,0:T(8,128)(2,1)S(1)}, bf16[32,2944]{1,0:T(8,128)(2,1)S(1)}, u32[]{:S(2)}, u32[]{:S(2)}) collective-permute-start(bf16[32,2944]{1,0:T(8,128)(2,1)S(1)} %collective-permute-done.2.refs_4_.refs_2_.refs_1_), channel_id=1, source_target_pairs={{0,16},{16,0},{32,48},{48,32},{64,80},{80,64},{96,112},{112,96},{1... | collective-permute-start | bytes 565256 | tf_op jit(solution)/shard_map/ppermute | solution.py:592
  73.7 3.5 %collective-permute-start.4 = (bf16[32,2944]{1,0:T(8,128)(2,1)S(1)}, bf16[32,2944]{1,0:T(8,128)(2,1)S(1)}, u32[]{:S(2)}, u32[]{:S(2)}) collective-permute-start(bf16[32,2944]{1,0:T(8,128)(2,1)S(1)} %collective-permute-done.1.refs_3_.refs_1_.refs_0_), channel_id=1, source_target_pairs={{0,16},{16,0},{32,48},{48,32},{64,80},{80,64},{96,112},{112,96},{1... | collective-permute-start | bytes 565256 | tf_op jit(solution)/shard_map/ppermute | solution.py:592
  85.7 4.7 %copy-start.1 = (bf16[512,576]{0,1:T(8,128)(2,1)S(1)}, bf16[512,576]{0,1:T(8,128)(2,1)}, u32[]{:S(2)}) copy-start(bf16[512,576]{0,1:T(8,128)(2,1)} %param.7) | copy-start | bytes 1769476
  85.7 42.8 %all-to-all-start.3 = ((bf16[16,32,2432]{2,1,0:T(8,128)(2,1)}), bf16[16,32,2432]{2,1,0:T(8,128)(2,1)}, u32[]{:S(2)}, u32[]{:S(2)}) async-start(bf16[16,32,2432]{2,1,0:T(8,128)(2,1)} %bitcast.4), calls=%async_computation.3 | async-start | bytes 4980736 | tf_op jit(solution)/shard_map/all_to_all | solution.py:597
  91.8 36.7 %copy-start.9 = (s32[2,32]{1,0:T(2,128)S(1)}, s32[2,32]{1,0:T(2,128)}, u32[]{:S(2)}) copy-start(s32[2,32]{1,0:T(2,128)} %ids_ref.1) | copy-start | bytes 772
  91.8 12.2 %collective-permute-start.7 = (bf16[128,1152]{1,0:T(8,128)(2,1)S(1)}, bf16[128,1152]{1,0:T(8,128)(2,1)S(1)}, u32[]{:S(2)}, u32[]{:S(2)}) collective-permute-start(bf16[128,1152]{1,0:T(8,128)(2,1)S(1)} %get-tuple-element.12), channel_id=1, source_target_pairs={{32,0},{48,16},{64,32},{80,48},{96,64},{112,80},{128,96},{144,112}... | collective-permute-start | bytes 884744 | tf_op jit(solution)/shard_map/ppermute | solution.py:588
  95.9 16.1 %collective-permute-start.8 = (bf16[128,1152]{1,0:T(8,128)(2,1)S(1)}, bf16[128,1152]{1,0:T(8,128)(2,1)S(1)}, u32[]{:S(2)}, u32[]{:S(2)}) collective-permute-start(bf16[128,1152]{1,0:T(8,128)(2,1)S(1)} %get-tuple-element.13), channel_id=1, source_target_pairs={{64,0},{80,16},{96,32},{112,48},{128,64},{144,80},{160,96},{176,11... | collective-permute-start | bytes 884744 | tf_op jit(solution)/shard_map/ppermute | solution.py:588
  97.9 15.4 %collective-permute-start.9 = (bf16[128,1152]{1,0:T(8,128)(2,1)S(1)}, bf16[128,1152]{1,0:T(8,128)(2,1)S(1)}, u32[]{:S(2)}, u32[]{:S(2)}) collective-permute-start(bf16[128,1152]{1,0:T(8,128)(2,1)S(1)} %get-tuple-element.14), channel_id=1, source_target_pairs={{448,0},{464,16},{480,32},{496,48},{0,64},{16,80},{32,96},{48,112}... | collective-permute-start | bytes 884744 | tf_op jit(solution)/shard_map/ppermute | solution.py:588
  102.1 19.5 %collective-permute-start.10 = (bf16[128,1152]{1,0:T(8,128)(2,1)S(1)}, bf16[128,1152]{1,0:T(8,128)(2,1)S(1)}, u32[]{:S(2)}, u32[]{:S(2)}) collective-permute-start(bf16[128,1152]{1,0:T(8,128)(2,1)S(1)} %get-tuple-element.15), channel_id=1, source_target_pairs={{480,0},{496,16},{0,32},{16,48},{32,64},{48,80},{64,96},{80,112},{... | collective-permute-start | bytes 884744 | tf_op jit(solution)/shard_map/ppermute | solution.py:588
  113.3 8.4 %copy-start.2 = (bf16[128,1152]{1,0:T(8,128)(2,1)}, bf16[128,1152]{1,0:T(8,128)(2,1)S(1)}, u32[]{:S(2)}) copy-start(bf16[128,1152]{1,0:T(8,128)(2,1)S(1)} %collective-permute-done.9.refs_3_) | copy-start | bytes 884740
  121.7 0.7 copy-start.4
  122.4 6.1 %collective-permute-start.11 = (bf16[320,1152]{1,0:T(8,128)(2,1)S(1)}, bf16[320,1152]{1,0:T(8,128)(2,1)}, u32[]{:S(2)}, u32[]{:S(2)}) collective-permute-start(bf16[320,1152]{1,0:T(8,128)(2,1)S(1)} %join.1), channel_id=1, source_target_pairs={{0,16},{16,0},{32,48},{48,32},{64,80},{80,64},{96,112},{112,96},{1... | collective-permute-start | bytes 2211848 | tf_op jit(solution)/shard_map/ppermute | solution.py:592
  128.5 1.0 copy-start.3
  129.5 1.0 copy-start.5

commit v4 on v3

--- a/solution.py
+++ b/solution.py
@@ -32,8 +32,8 @@
 FAR = (64, 192, 32)
 
 
-def params():
-    return pltpu.CompilerParams(vmem_limit_bytes=VMEM_LIMIT)
+def params(limit=VMEM_LIMIT):
+    return pltpu.CompilerParams(vmem_limit_bytes=limit)
 
 
 def whole():
@@ -42,6 +42,10 @@
 
 def anywhere():
     return pl.BlockSpec(memory_space=pl.ANY)
+
+
+def main_memory():
+    return pl.BlockSpec(memory_space=pltpu.HBM)
 
 
 def iota(shape, dim):
@@ -121,7 +125,7 @@
             jax.ShapeDtypeStruct((4, 8, Z_COLS), bf16),
             jax.ShapeDtypeStruct((PLANE, 2 * IH + 16, ID), bf16),
         ),
-        in_specs=[anywhere()] * 5,
+        in_specs=[main_memory()] * 5,
         out_specs=(whole(), whole()),
         scratch_shapes=[pltpu.VMEM((32, ID), f32), pltpu.VMEM((2 * IH, ID), f32)]
         + [
@@ -129,7 +133,7 @@
             for value in (kv_turned, index_keys, index_queries, index_weights, q_blocks)
         ]
         + [pltpu.SemaphoreType.DMA((5,))],
-        compiler_params=params(),
+        compiler_params=params(60 * 1024 * 1024),
         name="pack",
     )(kv_turned, index_keys, index_queries, index_weights, q_blocks)
 
@@ -374,8 +378,8 @@
     rotary = query[:, DL:]
     nothing = jnp.zeros_like(rotary)
     padded = (
-        jnp.concatenate([rotary, nothing], axis=1),
-        jnp.concatenate([nothing, rotary], axis=1),
+        jnp.concatenate([latent, rotary, nothing], axis=1),
+        jnp.concatenate([latent, nothing, rotary], axis=1),
     )
     contract = (((1,), (1,)), ((), ()))
     sets = []
@@ -386,7 +390,7 @@
         at, width = filled[0], block.shape[1]
         for i in range(2):
             heads = slice(i * HEADS, (i + 1) * HEADS)
-            value = jnp.where(place < limits[i], block[heads] * score_scale, -1e30)
+            value = jnp.where(place < limits[i], block[heads], -1e30)
             scores[heads, at : at + width] = value
             for k in range(0, width, 128):
                 tops[i] = jnp.maximum(tops[i], value[:, k : k + 128])
@@ -421,8 +425,9 @@
                 at = half * WIDTH + parity * DL
                 columns = slice(at, at + DL)
                 turn = half * WIDTH + 2 * DL
-                block = product(latent, ref[rows, columns]) + product(
-                    padded[parity], ref[rows, turn : turn + 128]
+                block = product(
+                    padded[parity],
+                    jnp.concatenate([ref[rows, columns], ref[rows, turn : turn + 128]], axis=1),
                 )
                 keep(
                     block,
@@ -473,8 +478,11 @@
         rows = slice(first * 128, last * 128)
         for parity in range(2):
             columns = slice(parity * DL, (parity + 1) * DL)
-            block = product(latent, direct[rows, columns]) + product(
-                padded[parity], direct[rows, 2 * DL : 2 * DL + 128]
+            block = product(
+                padded[parity],
+                jnp.concatenate(
+                    [direct[rows, columns], direct[rows, 2 * DL : 2 * DL + 128]], axis=1
+                ),
             )
             keep(
                 block,
@@ -487,7 +495,7 @@
     norm = jnp.zeros((2 * HEADS, 128), f32)
     for c in range(32):
         cols = slice(c * 128, (c + 1) * 128)
-        weight = jnp.exp(scores[:, cols] - highest)
+        weight = jnp.exp((scores[:, cols] - highest) * score_scale)
         scores[:, cols] = weight
         norm = norm + weight
     norm = jnp.sum(norm, axis=1, keepdims=True)
@@ -535,7 +543,7 @@
             jax.ShapeDtypeStruct((2, HEADS * DL), bf16),
             jax.ShapeDtypeStruct((2, 16384), bf16),
         ),
-        in_specs=[whole()] * 4 + [anywhere()] * (1 + len(mine)),
+        in_specs=[whole()] * 4 + [main_memory()] * (1 + len(mine)),
         out_specs=(whole(), whole()),
         scratch_shapes=[
             pltpu.VMEM((2 * HEADS, 4096), f32),
@@ -561,6 +569,21 @@
     return lax.ppermute(value, "ctx", pairs)
 
 
+def tie_kernel(value_ref, after_ref, out_ref):
+    pass
+
+
+def tie(value, after):
+    return pl.pallas_call(
+        tie_kernel,
+        out_shape=jax.ShapeDtypeStruct(value.shape, value.dtype),
+        in_specs=[anywhere(), anywhere()],
+        out_specs=anywhere(),
+        input_output_aliases={0: 0},
+        name="tie",
+    )(value, after)
+
+
 def join_kernel(*refs):
     out_ref = refs[-1]
     for n, ref in enumerate(refs[:-1]):
@@ -621,9 +644,9 @@
     swapped = [swap(other) for other in others]
     tables = [held] + others + [across] + swapped
     scores = score(tables, y)
-    sent = gather("far", FAR, others + swapped, y, [near], scores)
+    sent = gather("far", FAR, others + swapped, y, [], scores)
     served = serve(kv_turned, tables, sent)
-    far = exchange(sent)
+    far = exchange(tie(sent, near))
     mine = [served[0]]
     for away in AWAYS[1:]:
         mine.append(level_from(served[AWAYS.index(-away % LEVELS)], away))

time: 140 us -> 142 us (1.014)
  starting transfers between devices: 59.9 us -> 61.5 us
  waiting for transfers between devices: 23.5 us -> 21.9 us
    all_to_all x2, waiting for transfers between devices: 3.18 us -> 0.01 us  [exchange(): got = lax.all_to_all(parts, 'pb', split_axis=0, concat_axis=0, tiled=True)]
    all_to_all x2, starting transfers between devices: 11.6 us -> 14.1 us  [exchange(): got = lax.all_to_all(parts, 'pb', split_axis=0, concat_axis=0, tiled=True)]
    ppermute x6, waiting for transfers between devices: 17.6 us -> 19.4 us  [level_from(): return lax.ppermute(value, 'ctx', pairs)]
    ppermute x5, starting transfers between devices: 15.8 us -> 14.1 us  [swap(): lax.ppermute(value, 'ctx', [(at, at ^ 1) for at in range(2 * LEVELS)])]
    pallas_call x2, Pallas kernels: 5.42 us -> 3.92 us  [gather(): pl.pallas_call(body, out_shape=jax.ShapeDtypeStruct((PLANE * halves * slo...]
    pallas_call x1, Pallas kernels: 8.37 us -> 9.79 us  [attend(): pl.pallas_call(attend_kernel, out_shape=(jax.ShapeDtypeStruct((2, HEADS *...]
    unnamed x22 -> x35, local copies, waits for them, and re-layouts: 6.43 us -> 7.24 us
  transfers between devices with their start and end apart: 15 -> 15, of which waited for: 7 -> 5; matrix products, arithmetic and copies ran while one was open for 1% -> 2% of each run, Pallas kernels for 2% -> 4%
where the time goes in v4:
time: 142 us; the launch traced here: 141 us
  starting transfers between devices  61.5 us (43%)
  blocking collectives  28.5 us (20%)
  waiting for transfers between devices  21.9 us (15%)
  Pallas kernels  19.4 us (14%)
  local copies, waits for them, and re-layouts  8.52 us (6%)
    all_to_all x1, blocking collectives, outer_levels(): lax.all_to_all(chunks, 'ctx', split_axis=0, concat_axis=0, axis_index_gro...  28.5 us
    ppermute x6, starting transfers between devices, level_from(): return lax.ppermute(value, 'ctx', pairs)  19.6 us
    ppermute x6, waiting for transfers between devices, level_from(): return lax.ppermute(value, 'ctx', pairs)  19.4 us
    ppermute x5, starting transfers between devices, swap(): lax.ppermute(value, 'ctx', [(at, at ^ 1) for at in range(2 * LEVELS)])  14.1 us
    all_to_all x2, starting transfers between devices, exchange(): got = lax.all_to_all(parts, 'pb', split_axis=0, concat_axis=0, tiled=True)  14.1 us
    pallas_call x1, Pallas kernels, attend(): pl.pallas_call(attend_kernel, out_shape=(jax.ShapeDtypeStruct((2, HEADS *...  9.79 us
    unnamed x35, local copies, waits for them, and re-layouts  7.24 us
    ppermute x1, starting transfers between devices, two_levels_on(): return lax.ppermute(value, 'ctx', pairs)  6.95 us
  transfers between devices with their start and end apart: 15, of which 5 were waited for; matrix products, arithmetic and copies ran while one was open for 2% of the time, Pallas kernels for 4%

profile of v4, /device:TPU:1, one launch (start us, length us, event | category | flops | bytes accessed | tf_op | source)
XLA Modules:
  0.0 140.9 jit_solution(13024995812522810440)
XLA Ops:
  0.6 2.3 %pack.1 = (bf16[4,8,2944]{2,1,0:T(8,128)(2,1)}, bf16[16,144,128]{2,1,0:T(8,128)(2,1)}) custom-call(bf16[576,512]{1,0:T(8,128)(2,1)} %bitcast.13, bf16[32,128]{1,0:T(8,128)(2,1)} %refs_1_.1, bf16[2,8192]{1,0:T(2,128)(2,1)} %refs_2_.1, bf16[2,64]{1,0:T(2,128)(2,1)} %refs_3_.1, s32[2,32]{1,0:T(2,128)} %ids_ref.1), custom_call_target="tpu_custom_call" | custom-call | tf_op jit(solution)/shard_map/pack/pallas_call | solution.py:122
  3.0 28.5 %all_to_all.20 = bf16[4,8,2944]{2,1,0:T(8,128)(2,1)S(1)} all-to-all(bf16[4,8,2944]{2,1,0:T(8,128)(2,1)} %get-tuple-element.9), channel_id=1, replica_groups={{0,128,256,384},{16,144,272,400},{32,160,288,416},{48,176,304,432},{64,..., dimensions={0} | all-to-all | bytes 376832 | tf_op jit(solution)/shard_map/all_to_all | solution.py:630
  31.5 6.8 %all-to-all-start.1 = ((bf16[16,144,128]{2,1,0:T(8,128)(2,1)}), bf16[16,144,128]{2,1,0:T(8,128)(2,1)S(1)}, u32[]{:S(2)}, u32[]{:S(2)}) async-start(bf16[16,144,128]{2,1,0:T(8,128)(2,1)} %get-tuple-element.10), calls=%async_computation.1 | async-start | bytes 1179648 | tf_op jit(solution)/shard_map/all_to_all | solution.py:640
  38.3 7.0 %collective-permute-start.3 = (bf16[32,2944]{1,0:T(8,128)(2,1)S(1)}, bf16[32,2944]{1,0:T(8,128)(2,1)S(1)}, u32[]{:S(2)}, u32[]{:S(2)}) collective-permute-start(bf16[32,2944]{1,0:T(8,128)(2,1)S(1)} %bitcast.6), channel_id=1, source_target_pairs={{64,0},{464,16},{96,32},{496,48},{128,64},{16,80},{160,96},{48,112... | collective-permute-start | bytes 565256 | tf_op jit(solution)/shard_map/ppermute | solution.py:569
  45.3 1.9 %collective-permute-start.2 = (bf16[32,2944]{1,0:T(8,128)(2,1)S(1)}, bf16[32,2944]{1,0:T(8,128)(2,1)S(1)}, u32[]{:S(2)}, u32[]{:S(2)}) collective-permute-start(bf16[32,2944]{1,0:T(8,128)(2,1)S(1)} %bitcast.7), channel_id=1, source_target_pairs={{480,0},{496,16},{0,32},{16,48},{32,64},{48,80},{64,96},{80,112},{... | collective-permute-start | bytes 565256 | tf_op jit(solution)/shard_map/ppermute | solution.py:611
  47.2 4.6 %collective-permute-start.1 = (bf16[32,2944]{1,0:T(8,128)(2,1)S(1)}, bf16[32,2944]{1,0:T(8,128)(2,1)S(1)}, u32[]{:S(2)}, u32[]{:S(2)}) collective-permute-start(bf16[32,2944]{1,0:T(8,128)(2,1)S(1)} %bitcast.8), channel_id=1, source_target_pairs={{32,0},{48,16},{64,32},{80,48},{96,64},{112,80},{128,96},{144,112}... | collective-permute-start | bytes 565256 | tf_op jit(solution)/shard_map/ppermute | solution.py:611
  51.8 4.1 %collective-permute-start = (bf16[32,2944]{1,0:T(8,128)(2,1)S(1)}, bf16[32,2944]{1,0:T(8,128)(2,1)S(1)}, u32[]{:S(2)}, u32[]{:S(2)}) collective-permute-start(bf16[32,2944]{1,0:T(8,128)(2,1)S(1)} %bitcast.9), channel_id=1, source_target_pairs={{0,16},{16,0},{32,48},{48,32},{64,80},{80,64},{96,112},{112,96},{1... | collective-permute-start | bytes 565256 | tf_op jit(solution)/shard_map/ppermute | solution.py:615
  55.8 0.0 all-to-all-done.1.refs_2_.refs_8_.refs_6_
  55.9 0.0 collective-permute-done.3.refs_5_.refs_3_.refs_2_
  55.9 0.0 collective-permute-done.2.refs_4_.refs_2_.refs_1_
  55.9 0.0 collective-permute-done.1.refs_3_.refs_1_.refs_0_
  55.9 0.0 copy-start
  55.9 1.0 collective-permute-done.refs_1_.refs_4_
  56.9 1.9 %near.1 = bf16[384,1152]{1,0:T(8,128)(2,1)} custom-call(bf16[32,2944]{1,0:T(8,128)(2,1)S(1)} %bitcast.10, bf16[32,2944]{1,0:T(8,128)(2,1)S(1)} %collective-permute-done.refs_1_.refs_4_, bf16[16,144,128]{2,1,0:T(8,128)(2,1)S(1)} %all-to-all-done.1.refs_2_.refs_8_.refs_6_, bf16[32,2944]{1,0:T(8,128)(2,1)S(1)} %collective-permute-done.1.refs_3_.refs_1_.refs_0_, ...), custom_call_target="tpu_custom_call" | custom-call | flops 113246208 | bytes 3000000 | tf_op jit(solution)/shard_map/near/pallas_call | solution.py:223
  58.8 7.0 %all-to-all-start.2 = ((bf16[16,24,1152]{2,1,0:T(8,128)(2,1)}), bf16[16,24,1152]{2,1,0:T(8,128)(2,1)}, u32[]{:S(2)}, u32[]{:S(2)}) async-start(bf16[16,24,1152]{2,1,0:T(8,128)(2,1)} %bitcast.2), calls=%async_computation.2 | async-start | bytes 1769472 | tf_op jit(solution)/shard_map/all_to_all | solution.py:620
  65.8 3.3 %collective-permute-start.6 = (bf16[32,2944]{1,0:T(8,128)(2,1)S(1)}, bf16[32,2944]{1,0:T(8,128)(2,1)S(1)}, u32[]{:S(2)}, u32[]{:S(2)}) collective-permute-start(bf16[32,2944]{1,0:T(8,128)(2,1)S(1)} %collective-permute-done.3.refs_5_.refs_3_.refs_2_), channel_id=1, source_target_pairs={{0,16},{16,0},{32,48},{48,32},{64,80},{80,64},{96,112},{112,96},{1... | collective-permute-start | bytes 565256 | tf_op jit(solution)/shard_map/ppermute | solution.py:615
  69.1 1.9 %collective-permute-start.5 = (bf16[32,2944]{1,0:T(8,128)(2,1)S(1)}, bf16[32,2944]{1,0:T(8,128)(2,1)S(1)}, u32[]{:S(2)}, u32[]{:S(2)}) collective-permute-start(bf16[32,2944]{1,0:T(8,128)(2,1)S(1)} %collective-permute-done.2.refs_4_.refs_2_.refs_1_), channel_id=1, source_target_pairs={{0,16},{16,0},{32,48},{48,32},{64,80},{80,64},{96,112},{112,96},{1... | collective-permute-start | bytes 565256 | tf_op jit(solution)/shard_map/ppermute | solution.py:615
  71.0 2.4 %collective-permute-start.4 = (bf16[32,2944]{1,0:T(8,128)(2,1)S(1)}, bf16[32,2944]{1,0:T(8,128)(2,1)S(1)}, u32[]{:S(2)}, u32[]{:S(2)}) collective-permute-start(bf16[32,2944]{1,0:T(8,128)(2,1)S(1)} %collective-permute-done.1.refs_3_.refs_1_.refs_0_), channel_id=1, source_target_pairs={{0,16},{16,0},{32,48},{48,32},{64,80},{80,64},{96,112},{112,96},{1... | collective-permute-start | bytes 565256 | tf_op jit(solution)/shard_map/ppermute | solution.py:615
  73.4 0.0 collective-permute-done.6.refs_7_.refs_5_
  73.5 0.0 collective-permute-done.5.refs_6_.refs_4_
  73.5 1.0 collective-permute-done.4.refs_5_.refs_3_
  74.5 1.9 %score.1.refs_7_ = bf16[16,16,128]{2,1,0:T(8,128)(2,1)S(1)} custom-call(bf16[32,2944]{1,0:T(8,128)(2,1)S(1)} %bitcast.11, bf16[32,2944]{1,0:T(8,128)(2,1)S(1)} %collective-permute-done.1.refs_3_.refs_1_.refs_0_, bf16[32,2944]{1,0:T(8,128)(2,1)S(1)} %collective-permute-done.2.refs_4_.refs_2_.refs_1_, ...), custom_call_target="tpu_custom_call" | custom-call | flops 536870912 | bytes 2000000 | tf_op jit(solution)/shard_map/score/pallas_call | solution.py:344
  76.4 0.0 copy-start.1
  76.4 0.9 copy-done.1
  77.3 2.0 %far.1.refs_8_ = bf16[512,2432]{1,0:T(8,128)(2,1)S(1)} custom-call(bf16[32,2944]{1,0:T(8,128)(2,1)S(1)} %copy-done.1, bf16[32,2944]{1,0:T(8,128)(2,1)S(1)} %collective-permute-done.2.refs_4_.refs_2_.refs_1_, bf16[32,2944]{1,0:T(8,128)(2,1)S(1)} %collective-permute-done.3.refs_5_.refs_3_.refs_2_, bf16[32,2944]{1,0:T(8,128)(2,1)S(1)} %collective-permute-done.4.refs_5_.refs_3_, ...), custom_call_target="tpu_custom_call" | custom-call | flops 905969664 | bytes 3000000 | tf_op jit(solution)/shard_map/far/pallas_call | solution.py:223
  79.4 1.5 %copy.9.value_ref = bf16[512,2432]{1,0:T(8,128)(2,1)} copy(bf16[512,2432]{1,0:T(8,128)(2,1)S(1)} %far.1.refs_8_) | data formatting | bytes 4980736
  80.9 0.0 all-to-all-done.2
  80.9 7.1 %all-to-all-start.3 = ((bf16[16,32,2432]{2,1,0:T(8,128)(2,1)}), bf16[16,32,2432]{2,1,0:T(8,128)(2,1)}, u32[]{:S(2)}, u32[]{:S(2)}) async-start(bf16[16,32,2432]{2,1,0:T(8,128)(2,1)} %bitcast.15), calls=%async_computation.3 | async-start | bytes 4980736 | tf_op jit(solution)/shard_map/all_to_all | solution.py:620
  88.0 0.0 copy-start.5
  88.0 1.1 copy-done.5
  89.1 0.9 copy-done.9
  90.0 0.9 copy-done.11
  90.9 0.9 copy-done.13
  91.8 1.4 serve.1
  93.2 0.0 copy-start.16
  93.2 5.0 %collective-permute-start.7 = (bf16[128,1152]{1,0:T(8,128)(2,1)S(1)}, bf16[128,1152]{1,0:T(8,128)(2,1)S(1)}, u32[]{:S(2)}, u32[]{:S(2)}) collective-permute-start(bf16[128,1152]{1,0:T(8,128)(2,1)S(1)} %get-tuple-element.12), channel_id=1, source_target_pairs={{32,0},{48,16},{64,32},{80,48},{96,64},{112,80},{128,96},{144,112}... | collective-permute-start | bytes 884744 | tf_op jit(solution)/shard_map/ppermute | solution.py:611
  98.2 1.9 %collective-permute-start.8 = (bf16[128,1152]{1,0:T(8,128)(2,1)S(1)}, bf16[128,1152]{1,0:T(8,128)(2,1)S(1)}, u32[]{:S(2)}, u32[]{:S(2)}) collective-permute-start(bf16[128,1152]{1,0:T(8,128)(2,1)S(1)} %get-tuple-element.13), channel_id=1, source_target_pairs={{64,0},{80,16},{96,32},{112,48},{128,64},{144,80},{160,96},{176,11... | collective-permute-start | bytes 884744 | tf_op jit(solution)/shard_map/ppermute | solution.py:611
  100.2 4.3 %collective-permute-start.9 = (bf16[128,1152]{1,0:T(8,128)(2,1)S(1)}, bf16[128,1152]{1,0:T(8,128)(2,1)S(1)}, u32[]{:S(2)}, u32[]{:S(2)}) collective-permute-start(bf16[128,1152]{1,0:T(8,128)(2,1)S(1)} %get-tuple-element.14), channel_id=1, source_target_pairs={{448,0},{464,16},{480,32},{496,48},{0,64},{16,80},{32,96},{48,112}... | collective-permute-start | bytes 884744 | tf_op jit(solution)/shard_map/ppermute | solution.py:611
  104.4 1.9 %collective-permute-start.10 = (bf16[128,1152]{1,0:T(8,128)(2,1)S(1)}, bf16[128,1152]{1,0:T(8,128)(2,1)S(1)}, u32[]{:S(2)}, u32[]{:S(2)}) collective-permute-start(bf16[128,1152]{1,0:T(8,128)(2,1)S(1)} %get-tuple-element.15), channel_id=1, source_target_pairs={{480,0},{496,16},{0,32},{16,48},{32,64},{48,80},{64,96},{80,112},{... | collective-permute-start | bytes 884744 | tf_op jit(solution)/shard_map/ppermute | solution.py:611
  106.4 10.8 %collective-permute-done.8.refs_2_ = bf16[128,1152]{1,0:T(8,128)(2,1)S(1)} collective-permute-done((bf16[128,1152]{1,0:T(8,128)(2,1)S(1)}, bf16[128,1152]{1,0:T(8,128)(2,1)S(1)}, u32[]{:S(2)}, u32[]{:S(2)}) %collective-permute-start.8) | collective-permute-done | bytes 294944 | tf_op jit(solution)/shard_map/ppermute | solution.py:611
  117.2 0.0 collective-permute-done.9.refs_3_
  117.2 8.6 %collective-permute-done.10.refs_4_ = bf16[128,1152]{1,0:T(8,128)(2,1)S(1)} collective-permute-done((bf16[128,1152]{1,0:T(8,128)(2,1)S(1)}, bf16[128,1152]{1,0:T(8,128)(2,1)S(1)}, u32[]{:S(2)}, u32[]{:S(2)}) %collective-permute-start.10) | collective-permute-done | bytes 294944 | tf_op jit(solution)/shard_map/ppermute | solution.py:611
  125.7 0.1 join.1
  125.8 2.5 %collective-permute-start.11 = (bf16[320,1152]{1,0:T(8,128)(2,1)S(1)}, bf16[320,1152]{1,0:T(8,128)(2,1)S(1)}, u32[]{:S(2)}, u32[]{:S(2)}) collective-permute-start(bf16[320,1152]{1,0:T(8,128)(2,1)S(1)} %join.1), channel_id=1, source_target_pairs={{0,16},{16,0},{32,48},{48,32},{64,80},{80,64},{96,112},{112,96},{1... | collective-permute-start | bytes 2211848 | tf_op jit(solution)/shard_map/ppermute | solution.py:615
  128.3 1.3 reshape.22.q_ref
  129.6 0.5 collective-permute-done.11.refs_5_
  130.1 1.0 copy-done.15
  131.1 9.8 %attend.1 = (bf16[2,65536]{1,0:T(2,128)(2,1)}, bf16[2,16384]{1,0:T(2,128)(2,1)}) custom-call(bf16[2,128,576]{2,1,0:T(8,128)(2,1)S(1)} %reshape.22.q_ref, s32[2,32]{1,0:T(2,128)S(1)} %copy-done.16, bf16[384,1152]{1,0:T(8,128)(2,1)} %bitcast.3.after_ref.near_ref, bf16[512,2432]{1,0:T(8,128)(2,1)} %bitcast.5.far_ref, bf16[128,1152]{1,0:T(8,128)(2,1)S(1)} %copy-done.15, ...), custom_call_target="tpu_custom_call" | custom-call | flops 2415919104 | bytes 6000000 | tf_op jit(solution)/shard_map/attend/pallas_call | solution.py:540
  (27 shorter events, 0.1 us)
Async XLA Ops:
  31.5 42.9 %copy-start.3 = (bf16[4,8,2944]{2,1,0:T(8,128)(2,1)}, bf16[4,8,2944]{2,1,0:T(8,128)(2,1)S(1)}, u32[]{:S(2)}) copy-start(bf16[4,8,2944]{2,1,0:T(8,128)(2,1)S(1)} %all_to_all.20) | copy-start | bytes 565252
  31.5 24.3 %all-to-all-start.1 = ((bf16[16,144,128]{2,1,0:T(8,128)(2,1)}), bf16[16,144,128]{2,1,0:T(8,128)(2,1)S(1)}, u32[]{:S(2)}, u32[]{:S(2)}) async-start(bf16[16,144,128]{2,1,0:T(8,128)(2,1)} %get-tuple-element.10), calls=%async_computation.1 | async-start | bytes 1179648 | tf_op jit(solution)/shard_map/all_to_all | solution.py:640
  38.3 17.6 %collective-permute-start.3 = (bf16[32,2944]{1,0:T(8,128)(2,1)S(1)}, bf16[32,2944]{1,0:T(8,128)(2,1)S(1)}, u32[]{:S(2)}, u32[]{:S(2)}) collective-permute-start(bf16[32,2944]{1,0:T(8,128)(2,1)S(1)} %bitcast.6), channel_id=1, source_target_pairs={{64,0},{464,16},{96,32},{496,48},{128,64},{16,80},{160,96},{48,112... | collective-permute-start | bytes 565256 | tf_op jit(solution)/shard_map/ppermute | solution.py:569
  45.3 10.6 %collective-permute-start.2 = (bf16[32,2944]{1,0:T(8,128)(2,1)S(1)}, bf16[32,2944]{1,0:T(8,128)(2,1)S(1)}, u32[]{:S(2)}, u32[]{:S(2)}) collective-permute-start(bf16[32,2944]{1,0:T(8,128)(2,1)S(1)} %bitcast.7), channel_id=1, source_target_pairs={{480,0},{496,16},{0,32},{16,48},{32,64},{48,80},{64,96},{80,112},{... | collective-permute-start | bytes 565256 | tf_op jit(solution)/shard_map/ppermute | solution.py:611
  47.2 8.7 %collective-permute-start.1 = (bf16[32,2944]{1,0:T(8,128)(2,1)S(1)}, bf16[32,2944]{1,0:T(8,128)(2,1)S(1)}, u32[]{:S(2)}, u32[]{:S(2)}) collective-permute-start(bf16[32,2944]{1,0:T(8,128)(2,1)S(1)} %bitcast.8), channel_id=1, source_target_pairs={{32,0},{48,16},{64,32},{80,48},{96,64},{112,80},{128,96},{144,112}... | collective-permute-start | bytes 565256 | tf_op jit(solution)/shard_map/ppermute | solution.py:611
  51.8 5.1 %collective-permute-start = (bf16[32,2944]{1,0:T(8,128)(2,1)S(1)}, bf16[32,2944]{1,0:T(8,128)(2,1)S(1)}, u32[]{:S(2)}, u32[]{:S(2)}) collective-permute-start(bf16[32,2944]{1,0:T(8,128)(2,1)S(1)} %bitcast.9), channel_id=1, source_target_pairs={{0,16},{16,0},{32,48},{48,32},{64,80},{80,64},{96,112},{112,96},{1... | collective-permute-start | bytes 565256 | tf_op jit(solution)/shard_map/ppermute | solution.py:615
  55.9 18.6 %copy-start = (bf16[32,2944]{1,0:T(8,128)(2,1)}, bf16[32,2944]{1,0:T(8,128)(2,1)S(1)}, u32[]{:S(2)}) copy-start(bf16[32,2944]{1,0:T(8,128)(2,1)S(1)} %collective-permute-done.1.refs_3_.refs_1_.refs_0_) | copy-start | bytes 565252
  56.9 17.6 %copy-start.12 = (bf16[32,2944]{1,0:T(8,128)(2,1)}, bf16[32,2944]{1,0:T(8,128)(2,1)S(1)}, u32[]{:S(2)}) copy-start(bf16[32,2944]{1,0:T(8,128)(2,1)S(1)} %collective-permute-done.refs_1_.refs_4_) | copy-start | bytes 565252
  58.8 22.0 %all-to-all-start.2 = ((bf16[16,24,1152]{2,1,0:T(8,128)(2,1)}), bf16[16,24,1152]{2,1,0:T(8,128)(2,1)}, u32[]{:S(2)}, u32[]{:S(2)}) async-start(bf16[16,24,1152]{2,1,0:T(8,128)(2,1)} %bitcast.2), calls=%async_computation.2 | async-start | bytes 1769472 | tf_op jit(solution)/shard_map/all_to_all | solution.py:620
  65.8 7.6 %collective-permute-start.6 = (bf16[32,2944]{1,0:T(8,128)(2,1)S(1)}, bf16[32,2944]{1,0:T(8,128)(2,1)S(1)}, u32[]{:S(2)}, u32[]{:S(2)}) collective-permute-start(bf16[32,2944]{1,0:T(8,128)(2,1)S(1)} %collective-permute-done.3.refs_5_.refs_3_.refs_2_), channel_id=1, source_target_pairs={{0,16},{16,0},{32,48},{48,32},{64,80},{80,64},{96,112},{112,96},{1... | collective-permute-start | bytes 565256 | tf_op jit(solution)/shard_map/ppermute | solution.py:615
  69.1 4.4 %collective-permute-start.5 = (bf16[32,2944]{1,0:T(8,128)(2,1)S(1)}, bf16[32,2944]{1,0:T(8,128)(2,1)S(1)}, u32[]{:S(2)}, u32[]{:S(2)}) collective-permute-start(bf16[32,2944]{1,0:T(8,128)(2,1)S(1)} %collective-permute-done.2.refs_4_.refs_2_.refs_1_), channel_id=1, source_target_pairs={{0,16},{16,0},{32,48},{48,32},{64,80},{80,64},{96,112},{112,96},{1... | collective-permute-start | bytes 565256 | tf_op jit(solution)/shard_map/ppermute | solution.py:615
  71.0 3.5 %collective-permute-start.4 = (bf16[32,2944]{1,0:T(8,128)(2,1)S(1)}, bf16[32,2944]{1,0:T(8,128)(2,1)S(1)}, u32[]{:S(2)}, u32[]{:S(2)}) collective-permute-start(bf16[32,2944]{1,0:T(8,128)(2,1)S(1)} %collective-permute-done.1.refs_3_.refs_1_.refs_0_), channel_id=1, source_target_pairs={{0,16},{16,0},{32,48},{48,32},{64,80},{80,64},{96,112},{112,96},{1... | collective-permute-start | bytes 565256 | tf_op jit(solution)/shard_map/ppermute | solution.py:615
  73.4 5.9 %copy-start.6 = (bf16[32,2944]{1,0:T(8,128)(2,1)}, bf16[32,2944]{1,0:T(8,128)(2,1)S(1)}, u32[]{:S(2)}) copy-start(bf16[32,2944]{1,0:T(8,128)(2,1)S(1)} %collective-permute-done.6.refs_7_.refs_5_) | copy-start | bytes 565252
  73.5 5.9 %copy-start.8 = (bf16[32,2944]{1,0:T(8,128)(2,1)}, bf16[32,2944]{1,0:T(8,128)(2,1)S(1)}, u32[]{:S(2)}) copy-start(bf16[32,2944]{1,0:T(8,128)(2,1)S(1)} %collective-permute-done.5.refs_6_.refs_4_) | copy-start | bytes 565252
  74.5 4.9 %copy-start.10 = (bf16[32,2944]{1,0:T(8,128)(2,1)}, bf16[32,2944]{1,0:T(8,128)(2,1)S(1)}, u32[]{:S(2)}) copy-start(bf16[32,2944]{1,0:T(8,128)(2,1)S(1)} %collective-permute-done.4.refs_5_.refs_3_) | copy-start | bytes 565252
  76.4 0.9 copy-start.1
  80.9 7.1 %copy-start.2 = (bf16[32,2944]{1,0:T(8,128)(2,1)S(1)}, bf16[32,2944]{1,0:T(8,128)(2,1)}, u32[]{:S(2)}) copy-start(bf16[32,2944]{1,0:T(8,128)(2,1)} %copy-done) | copy-start | bytes 565252
  80.9 7.1 %copy-start.4 = (bf16[4,8,2944]{2,1,0:T(8,128)(2,1)S(1)}, bf16[4,8,2944]{2,1,0:T(8,128)(2,1)}, u32[]{:S(2)}) copy-start(bf16[4,8,2944]{2,1,0:T(8,128)(2,1)} %copy-done.3) | copy-start | bytes 565252
  80.9 7.1 %copy-start.7 = (bf16[32,2944]{1,0:T(8,128)(2,1)S(1)}, bf16[32,2944]{1,0:T(8,128)(2,1)}, u32[]{:S(2)}) copy-start(bf16[32,2944]{1,0:T(8,128)(2,1)} %copy-done.6) | copy-start | bytes 565252
  80.9 49.2 %all-to-all-start.3 = ((bf16[16,32,2432]{2,1,0:T(8,128)(2,1)}), bf16[16,32,2432]{2,1,0:T(8,128)(2,1)}, u32[]{:S(2)}, u32[]{:S(2)}) async-start(bf16[16,32,2432]{2,1,0:T(8,128)(2,1)} %bitcast.15), calls=%async_computation.3 | async-start | bytes 4980736 | tf_op jit(solution)/shard_map/all_to_all | solution.py:620
  88.0 1.1 copy-start.5
  89.1 0.9 copy-start.9
  90.0 0.9 copy-start.11
  90.9 0.9 copy-start.13
  93.2 32.6 %copy-start.14 = (bf16[128,1152]{1,0:T(8,128)(2,1)}, bf16[128,1152]{1,0:T(8,128)(2,1)S(1)}, u32[]{:S(2)}) copy-start(bf16[128,1152]{1,0:T(8,128)(2,1)S(1)} %get-tuple-element.11.refs_0_) | copy-start | bytes 884740
  93.2 36.9 %copy-start.16 = (s32[2,32]{1,0:T(2,128)S(1)}, s32[2,32]{1,0:T(2,128)}, u32[]{:S(2)}) copy-start(s32[2,32]{1,0:T(2,128)} %ids_ref.1) | copy-start | bytes 772
  93.2 13.1 %collective-permute-start.7 = (bf16[128,1152]{1,0:T(8,128)(2,1)S(1)}, bf16[128,1152]{1,0:T(8,128)(2,1)S(1)}, u32[]{:S(2)}, u32[]{:S(2)}) collective-permute-start(bf16[128,1152]{1,0:T(8,128)(2,1)S(1)} %get-tuple-element.12), channel_id=1, source_target_pairs={{32,0},{48,16},{64,32},{80,48},{96,64},{112,80},{128,96},{144,112}... | collective-permute-start | bytes 884744 | tf_op jit(solution)/shard_map/ppermute | solution.py:611
  98.2 18.9 %collective-permute-start.8 = (bf16[128,1152]{1,0:T(8,128)(2,1)S(1)}, bf16[128,1152]{1,0:T(8,128)(2,1)S(1)}, u32[]{:S(2)}, u32[]{:S(2)}) collective-permute-start(bf16[128,1152]{1,0:T(8,128)(2,1)S(1)} %get-tuple-element.13), channel_id=1, source_target_pairs={{64,0},{80,16},{96,32},{112,48},{128,64},{144,80},{160,96},{176,11... | collective-permute-start | bytes 884744 | tf_op jit(solution)/shard_map/ppermute | solution.py:611
  100.2 17.0 %collective-permute-start.9 = (bf16[128,1152]{1,0:T(8,128)(2,1)S(1)}, bf16[128,1152]{1,0:T(8,128)(2,1)S(1)}, u32[]{:S(2)}, u32[]{:S(2)}) collective-permute-start(bf16[128,1152]{1,0:T(8,128)(2,1)S(1)} %get-tuple-element.14), channel_id=1, source_target_pairs={{448,0},{464,16},{480,32},{496,48},{0,64},{16,80},{32,96},{48,112}... | collective-permute-start | bytes 884744 | tf_op jit(solution)/shard_map/ppermute | solution.py:611
  104.4 21.3 %collective-permute-start.10 = (bf16[128,1152]{1,0:T(8,128)(2,1)S(1)}, bf16[128,1152]{1,0:T(8,128)(2,1)S(1)}, u32[]{:S(2)}, u32[]{:S(2)}) collective-permute-start(bf16[128,1152]{1,0:T(8,128)(2,1)S(1)} %get-tuple-element.15), channel_id=1, source_target_pairs={{480,0},{496,16},{0,32},{16,48},{32,64},{48,80},{64,96},{80,112},{... | collective-permute-start | bytes 884744 | tf_op jit(solution)/shard_map/ppermute | solution.py:611
  125.8 4.3 %collective-permute-start.11 = (bf16[320,1152]{1,0:T(8,128)(2,1)S(1)}, bf16[320,1152]{1,0:T(8,128)(2,1)S(1)}, u32[]{:S(2)}, u32[]{:S(2)}) collective-permute-start(bf16[320,1152]{1,0:T(8,128)(2,1)S(1)} %join.1), channel_id=1, source_target_pairs={{0,16},{16,0},{32,48},{48,32},{64,80},{80,64},{96,112},{112,96},{1... | collective-permute-start | bytes 2211848 | tf_op jit(solution)/shard_map/ppermute | solution.py:615
  130.1 1.0 copy-start.15

commit v5 on v4

--- a/solution.py
+++ b/solution.py
@@ -236,20 +236,9 @@
     )(*operands)
 
 
-def serve_kernel(kv_ref, *refs):
-    tables, outs = refs[:8], refs[9:]
+def serve_kernel(kv_ref, ids_ref, after_ref, *outs):
     at = lax.axis_index("ctx")
-    level = at // 2
-    lines = []
-    line = iota((32, 128), 0)
-    for away in AWAYS:
-        outer = (level + away) % LEVELS // 4
-        for other in range(2):
-            ref = tables[(0, 1, 3, 2)[away % 4] + 4 * other]
-            values = jnp.where(line == outer * 8, ref[:, IDS_AT:].astype(f32), 0.0)
-            lines.append(jnp.sum(values, axis=0, keepdims=True))
-    lines += [jnp.full((6, 128), -1.0, f32)]
-    ids = jnp.concatenate(lines, axis=0)[:, :64]
+    ids = ids_ref[:, :64]
     own = (at * 8).astype(f32)
     lane = iota((16, 512), 1)
     codes = jnp.full((16, 512), -1.0, f32)
@@ -281,30 +270,41 @@
         outs[n][...] = jnp.concatenate(columns, axis=1).astype(bf16)
 
 
-def serve(kv_turned, tables, after):
+def serve(kv_turned, ids, after):
     return pl.pallas_call(
         serve_kernel,
         out_shape=tuple(jax.ShapeDtypeStruct((2 * BLK, WIDTH), bf16) for away in AWAYS),
-        in_specs=[whole()] * 9 + [anywhere()],
+        in_specs=[whole()] * 2 + [anywhere()],
         out_specs=(whole(),) * len(AWAYS),
         compiler_params=params(),
         cost_estimate=pl.CostEstimate(
             flops=2 * 10 * 128 * 512 * DQK, bytes_accessed=4_000_000, transcendentals=0
         ),
         name="serve",
-    )(kv_turned, *tables, after)
+    )(kv_turned, ids, after)
 
 
 def score_kernel(*refs):
-    tables, y_ref, out_ref, keys = refs[:8], refs[8], refs[9], refs[10]
+    tables, (y_ref, out_ref, ids_ref, keys) = refs[:8], refs[8:]
     tail = jnp.concatenate(
         [y_ref[p, 2 * IH : 2 * IH + 16, :].astype(f32)[0:1] for p in range(PLANE)], axis=0
     )
     weights = jnp.concatenate(
         [tail * index_scale, jnp.zeros((128 - PLANE, 128), f32)], axis=0
     ).T
+    at = lax.axis_index("ctx")
+    level = at // 2
+    lines = []
+    line = iota((32, 128), 0)
+    for away in AWAYS:
+        outer = (level + away) % LEVELS // 4
+        for other in range(2):
+            ref = tables[(0, 1, 3, 2)[away % 4] + 4 * other]
+            values = jnp.where(line == outer * 8, ref[:, IDS_AT:].astype(f32), 0.0)
+            lines.append(jnp.sum(values, axis=0, keepdims=True))
+    lines += [jnp.full((6, 128), -1.0, f32)]
+    ids_ref[...] = jnp.concatenate(lines, axis=0)
     lane = iota((128, 128), 1)
-    at = lax.axis_index("ctx")
     for n, ref in enumerate(tables):
         step = (0, 1, 3, 2)[n % 4]
         inner = (at // 2 + step) % 4
@@ -343,9 +343,12 @@
 def score(tables, y):
     return pl.pallas_call(
         score_kernel,
-        out_shape=jax.ShapeDtypeStruct((PLANE, 16, 128), bf16),
+        out_shape=(
+            jax.ShapeDtypeStruct((PLANE, 16, 128), bf16),
+            jax.ShapeDtypeStruct((16, 128), f32),
+        ),
         in_specs=[whole()] * 9,
-        out_specs=whole(),
+        out_specs=(whole(), whole()),
         scratch_shapes=[pltpu.VMEM((1024, ID), f32)],
         compiler_params=params(),
         cost_estimate=pl.CostEstimate(
@@ -355,33 +358,24 @@
     )(*tables, y)
 
 
-def attend_kernel(q_ref, ids_ref, near_ref, far_ref, *refs):
-    count = len(AWAYS)
-    mine, crossed = refs[:count], refs[count]
-    out_ref, index_ref, scores, total, turned, direct, sem = refs[count + 1 :]
-    copies = []
-    for n in range(count):
-        for other in range(2):
-            source = crossed.at[pl.ds(n * 64, 64)] if other else mine[n].at[pl.ds(0, 64)]
-            target = direct.at[pl.ds((2 * n + other) * 64, 64)]
-            copies.append(pltpu.make_async_copy(source, target, sem.at[2 * n + other]))
-    for copy in copies:
-        copy.start()
+def product(left, right):
+    return lax.dot_general(
+        left, right, (((1,), (1,)), ((), ())), preferred_element_type=f32
+    )
+
+
+def attend_start(q_ref, scores):
     ctx = lax.axis_index("ctx")
     rank = ctx * PLANE + lax.axis_index("pb")
-    ids = ids_ref[...]
     own_block = 240 + rank * 2 // BLK
-    own_row = table_row(own_block)
     offsets = [((rank * 2 + i) % BLK).astype(f32) for i in range(2)]
     query = jnp.concatenate([q_ref[0], q_ref[1]], axis=0)
-    latent = query[:, :DL]
-    rotary = query[:, DL:]
+    latent, rotary = query[:, :DL], query[:, DL:]
     nothing = jnp.zeros_like(rotary)
     padded = (
         jnp.concatenate([latent, rotary, nothing], axis=1),
         jnp.concatenate([latent, nothing, rotary], axis=1),
     )
-    contract = (((1,), (1,)), ((), ()))
     sets = []
     filled = [0]
     tops = [jnp.full((HEADS, 128), -1e30, f32) for i in range(2)]
@@ -397,9 +391,30 @@
         sets.append((at, width, values))
         filled[0] += width
 
-    def product(left, right):
-        return lax.dot_general(left, right, contract, preferred_element_type=f32)
-
+    return ctx, own_block, offsets, padded, sets, tops, keep
+
+
+def attend_sum(scores, sets, highest, norm, total, fresh):
+    for at, width, values in sets:
+        weight = jnp.exp((scores[:, at : at + width] - highest) * score_scale)
+        for k in range(0, width, 128):
+            norm = norm + weight[:, k : k + 128]
+        rows = [ref[rows, columns] for ref, rows, columns in values]
+        rows = rows[0] if len(rows) == 1 else jnp.concatenate(rows, axis=0)
+        term = jnp.dot(weight.astype(bf16), rows, preferred_element_type=f32)
+        for k in range(4):
+            if fresh:
+                total[k] = term[:, k * 128 : (k + 1) * 128]
+            else:
+                total[k] += term[:, k * 128 : (k + 1) * 128]
+        fresh = False
+    return norm
+
+
+def plane_kernel(q_ref, ids_ref, near_ref, far_ref, total, state, index_ref, scores, turned):
+    ctx, own_block, offsets, padded, sets, tops, keep = attend_start(q_ref, scores)
+    ids = ids_ref[...]
+    own_row = table_row(own_block)
     for span, ref, step in ((NEAR, near_ref, 384), (FAR, far_ref, 256)):
         first, count, slots = span
         one, two = named_columns(span, [ids[0:1]]), named_columns(span, [ids[1:2]])
@@ -436,6 +451,37 @@
                     [(ref, rows, columns)],
                 )
 
+    highest = jnp.max(jnp.concatenate(tops, axis=0), axis=1, keepdims=True)
+    norm = jnp.zeros((2 * HEADS, 128), f32)
+    state[0] = jnp.broadcast_to(highest, (2 * HEADS, 128))
+    state[1] = attend_sum(scores, sets, highest, norm, total, True)
+
+    tiles = [
+        far_ref[p * FAR[2] : p * FAR[2] + 16, KV_COLS:].astype(f32)
+        for p in range(PLANE)
+    ]
+    group = iota((16, 128), 1) // 32
+    for c in range(4):
+        for m in range(4):
+            mixed = tiles[4 * m]
+            for k in range(4):
+                tile = tiles[4 * m + k]
+                if k != c:
+                    tile = pltpu.roll(tile, (k - c) * 32 % 128, 1)
+                mixed = tile if k == 0 else jnp.where(group == k, tile, mixed)
+            turned[(c * 4 + m) * 16 : (c * 4 + m + 1) * 16, :] = mixed
+            for t in range(8):
+                at = (t * 4 + c) * 512 + m * 128
+                index_ref[:, at : at + 128] = turned[
+                    pl.ds((c * 4 + m) * 16 + t, 2, stride=8), :
+                ].astype(bf16)
+
+
+def column_kernel(q_ref, ids_ref, before, state, *refs):
+    count = len(AWAYS)
+    mine, crossed, (out_ref, scores, total) = refs[:count], refs[count], refs[count + 1 :]
+    ctx, own_block, offsets, padded, sets, tops, keep = attend_start(q_ref, scores)
+    ids = ids_ref[...]
     count = 16 * len(AWAYS)
     line = iota((count, 128), 0)
     lane = iota((count, 128), 1)
@@ -472,92 +518,76 @@
         for limit in limits
     ]
     here = iota((1, 128), 1) % 32
-    for copy in copies:
-        copy.wait()
+    direct = []
+    for n in range(len(AWAYS)):
+        direct += [(mine[n], slice(0, 64)), (crossed, slice(n * 64, (n + 1) * 64))]
     for first, last in ((0, 2), (2, 4), (4, 5)):
-        rows = slice(first * 128, last * 128)
+        parts = direct[2 * first : 2 * last]
+        turns = [ref[rows, 2 * DL : 2 * DL + 128] for ref, rows in parts]
         for parity in range(2):
             columns = slice(parity * DL, (parity + 1) * DL)
-            block = product(
-                padded[parity],
-                jnp.concatenate(
-                    [direct[rows, columns], direct[rows, 2 * DL : 2 * DL + 128]], axis=1
-                ),
-            )
+            values = [ref[rows, columns] for ref, rows in parts]
+            both = [jnp.concatenate(pair, axis=1) for pair in zip(values, turns)]
             keep(
-                block,
+                product(padded[parity], jnp.concatenate(both, axis=0)),
                 jnp.concatenate([(here + 32 * parity).astype(f32)] * (last - first), axis=1),
                 [jnp.concatenate(each[first:last], axis=1) for each in shown],
-                [(direct, rows, columns)],
+                [(ref, rows, columns) for ref, rows in parts],
             )
 
     highest = jnp.max(jnp.concatenate(tops, axis=0), axis=1, keepdims=True)
-    norm = jnp.zeros((2 * HEADS, 128), f32)
-    for c in range(32):
-        cols = slice(c * 128, (c + 1) * 128)
-        weight = jnp.exp((scores[:, cols] - highest) * score_scale)
-        scores[:, cols] = weight
-        norm = norm + weight
-    norm = jnp.sum(norm, axis=1, keepdims=True)
-    share = 1.0 / norm
-    for c, (at, width, values) in enumerate(sets):
-        probs = (scores[:, at : at + width] * share).astype(bf16)
-        rows = [ref[rows, columns] for ref, rows, columns in values]
-        rows = rows[0] if len(rows) == 1 else jnp.concatenate(rows, axis=0)
-        term = jnp.dot(probs, rows, preferred_element_type=f32)
-        for k in range(4):
-            if c == 0:
-                total[k] = term[:, k * 128 : (k + 1) * 128]
-            else:
-                total[k] += term[:, k * 128 : (k + 1) * 128]
+    highest = jnp.maximum(highest, state[0][:, 0:1])
+    fade = jnp.exp((state[0] - highest) * score_scale)
+    for k in range(4):
+        total[k] = before[k] * fade
+    norm = attend_sum(scores, sets, highest, state[1] * fade, total, False)
+    share = 1.0 / jnp.sum(norm, axis=1, keepdims=True)
+    for k in range(4):
+        total[k] = total[k] * share
     for h in range(HEADS):
         for k in range(4):
             at = h * DL + k * 128
             out_ref[:, at : at + 128] = total[k, pl.ds(h, 2, stride=HEADS), :].astype(bf16)
 
-    tiles = [
-        far_ref[p * FAR[2] : p * FAR[2] + 16, KV_COLS:].astype(f32)
-        for p in range(PLANE)
-    ]
-    group = iota((16, 128), 1) // 32
-    for c in range(4):
-        for m in range(4):
-            mixed = tiles[4 * m]
-            for k in range(4):
-                tile = tiles[4 * m + k]
-                if k != c:
-                    tile = pltpu.roll(tile, (k - c) * 32 % 128, 1)
-                mixed = tile if k == 0 else jnp.where(group == k, tile, mixed)
-            turned[(c * 4 + m) * 16 : (c * 4 + m + 1) * 16, :] = mixed
-            for t in range(8):
-                at = (t * 4 + c) * 512 + m * 128
-                index_ref[:, at : at + 128] = turned[
-                    pl.ds((c * 4 + m) * 16 + t, 2, stride=8), :
-                ].astype(bf16)
-
-
-def attend(query, ids, near, far, mine, crossed):
-    return pl.pallas_call(
-        attend_kernel,
+
+def attend_plane(query, ids, near, far):
+    return pl.pallas_call(
+        plane_kernel,
         out_shape=(
-            jax.ShapeDtypeStruct((2, HEADS * DL), bf16),
+            jax.ShapeDtypeStruct((4, 2 * HEADS, 128), f32),
+            jax.ShapeDtypeStruct((2, 2 * HEADS, 128), f32),
             jax.ShapeDtypeStruct((2, 16384), bf16),
         ),
-        in_specs=[whole()] * 4 + [main_memory()] * (1 + len(mine)),
-        out_specs=(whole(), whole()),
+        in_specs=[whole()] * 4,
+        out_specs=(whole(),) * 3,
         scratch_shapes=[
-            pltpu.VMEM((2 * HEADS, 4096), f32),
-            pltpu.VMEM((4, 2 * HEADS, 128), f32),
+            pltpu.VMEM((2 * HEADS, 2816), f32),
             pltpu.VMEM((256, 128), f32),
-            pltpu.VMEM((128 * len(AWAYS), WIDTH), bf16),
-            pltpu.SemaphoreType.DMA((2 * len(AWAYS),)),
         ],
         compiler_params=params(),
         cost_estimate=pl.CostEstimate(
-            flops=2 * 256 * 4096 * 1152, bytes_accessed=6_000_000, transcendentals=256 * 4096
-        ),
-        name="attend",
-    )(query, ids, near, far, *mine, crossed)
+            flops=2 * 256 * 2816 * 1152, bytes_accessed=4_000_000, transcendentals=256 * 2816
+        ),
+        name="attend_plane",
+    )(query, ids, near, far)
+
+
+def attend_column(query, ids, before, state, mine, crossed):
+    return pl.pallas_call(
+        column_kernel,
+        out_shape=jax.ShapeDtypeStruct((2, HEADS * DL), bf16),
+        in_specs=[whole()] * (5 + len(mine)),
+        out_specs=whole(),
+        scratch_shapes=[
+            pltpu.VMEM((2 * HEADS, 1280), f32),
+            pltpu.VMEM((4, 2 * HEADS, 128), f32),
+        ],
+        compiler_params=params(),
+        cost_estimate=pl.CostEstimate(
+            flops=2 * 256 * 1280 * 1152, bytes_accessed=3_000_000, transcendentals=256 * 1280
+        ),
+        name="attend_column",
+    )(query, ids, before, state, *mine, crossed)
 
 
 def two_levels_on(value):
@@ -643,16 +673,17 @@
     near = exchange(gather("near", NEAR, [held, across], y, others))
     swapped = [swap(other) for other in others]
     tables = [held] + others + [across] + swapped
-    scores = score(tables, y)
+    scores, asked = score(tables, y)
     sent = gather("far", FAR, others + swapped, y, [], scores)
-    served = serve(kv_turned, tables, sent)
+    served = serve(kv_turned, asked, sent)
     far = exchange(tie(sent, near))
     mine = [served[0]]
     for away in AWAYS[1:]:
         mine.append(level_from(served[AWAYS.index(-away % LEVELS)], away))
     crossed = swap(join(mine))
     query = q_latent.reshape(2, HEADS, DQK)
-    return tuple(attend(query, q_blocks, near, far, mine, crossed))
+    before, state, scores = attend_plane(query, q_blocks, near, far)
+    return (attend_column(query, q_blocks, before, state, mine, crossed), scores)
 
 
 def solution(mesh):

time: 142 us -> 136 us (0.958)
  local copies, waits for them, and re-layouts: 8.52 us -> 3.67 us
    unnamed x35 -> x9, local copies, waits for them, and re-layouts: 7.24 us -> 2.4 us
    pallas_call x2 -> x3, Pallas kernels: 11.7 us -> 10.4 us  [the longest x1 5.45 us: attend_plane(): pl.pallas_call(plane_kernel, out_shape=(jax.ShapeDtypeStruct((4, 2 * HEAD...]
  transfers between devices with their start and end apart: 15 -> 15, of which waited for: 5 -> 5; matrix products, arithmetic and copies ran while one was open for 2% -> 2% of each run, Pallas kernels for 4% -> 8%
where the time goes in v5:
time: 136 us; the launch traced here: 134 us
  starting transfers between devices  61.5 us (45%)
  blocking collectives  28.5 us (21%)
  waiting for transfers between devices  21.7 us (16%)
  Pallas kernels  18 us (13%)
  local copies, waits for them, and re-layouts  3.67 us (3%)
    all_to_all x1, blocking collectives, outer_levels(): lax.all_to_all(chunks, 'ctx', split_axis=0, concat_axis=0, axis_index_gro...  28.5 us
    ppermute x6, starting transfers between devices, level_from(): return lax.ppermute(value, 'ctx', pairs)  19.5 us
    ppermute x6, waiting for transfers between devices, level_from(): return lax.ppermute(value, 'ctx', pairs)  19.3 us
    ppermute x5, starting transfers between devices, swap(): lax.ppermute(value, 'ctx', [(at, at ^ 1) for at in range(2 * LEVELS)])  14.2 us
    all_to_all x2, starting transfers between devices, exchange(): got = lax.all_to_all(parts, 'pb', split_axis=0, concat_axis=0, tiled=True)  14 us
    ppermute x1, starting transfers between devices, two_levels_on(): return lax.ppermute(value, 'ctx', pairs)  6.95 us
    all_to_all x1, starting transfers between devices, local(): y = lax.all_to_all(y, 'pb', split_axis=0, concat_axis=0, tiled=True)  6.77 us
    pallas_call x1, Pallas kernels, attend_plane(): pl.pallas_call(plane_kernel, out_shape=(jax.ShapeDtypeStruct((4, 2 * HEAD...  5.45 us
  transfers between devices with their start and end apart: 15, of which 5 were waited for; matrix products, arithmetic and copies ran while one was open for 2% of the time, Pallas kernels for 8%

profile of v5, /device:TPU:1, one launch (start us, length us, event | category | flops | bytes accessed | tf_op | source)
XLA Modules:
  0.0 134.3 jit_solution(2143159255665716087)
XLA Ops:
  0.6 2.3 %pack.1 = (bf16[4,8,2944]{2,1,0:T(8,128)(2,1)}, bf16[16,144,128]{2,1,0:T(8,128)(2,1)}) custom-call(bf16[576,512]{1,0:T(8,128)(2,1)} %bitcast.6, bf16[32,128]{1,0:T(8,128)(2,1)} %refs_1_.1, bf16[2,8192]{1,0:T(2,128)(2,1)} %refs_2_.1, bf16[2,64]{1,0:T(2,128)(2,1)} %refs_3_.1, s32[2,32]{1,0:T(2,128)} %ids_ref.3), custom_call_target="tpu_custom_call" | custom-call | tf_op jit(solution)/shard_map/pack/pallas_call | solution.py:122
  3.0 28.5 %all_to_all.20 = bf16[4,8,2944]{2,1,0:T(8,128)(2,1)S(1)} all-to-all(bf16[4,8,2944]{2,1,0:T(8,128)(2,1)} %get-tuple-element.14), channel_id=1, replica_groups={{0,128,256,384},{16,144,272,400},{32,160,288,416},{48,176,304,432},{64,..., dimensions={0} | all-to-all | bytes 376832 | tf_op jit(solution)/shard_map/all_to_all | solution.py:660
  31.5 6.8 %all-to-all-start.1 = ((bf16[16,144,128]{2,1,0:T(8,128)(2,1)}), bf16[16,144,128]{2,1,0:T(8,128)(2,1)S(1)}, u32[]{:S(2)}, u32[]{:S(2)}) async-start(bf16[16,144,128]{2,1,0:T(8,128)(2,1)} %get-tuple-element.15), calls=%async_computation.1 | async-start | bytes 1179648 | tf_op jit(solution)/shard_map/all_to_all | solution.py:670
  38.3 7.0 %collective-permute-start.3 = (bf16[32,2944]{1,0:T(8,128)(2,1)S(1)}, bf16[32,2944]{1,0:T(8,128)(2,1)S(1)}, u32[]{:S(2)}, u32[]{:S(2)}) collective-permute-start(bf16[32,2944]{1,0:T(8,128)(2,1)S(1)} %bitcast.8), channel_id=1, source_target_pairs={{64,0},{464,16},{96,32},{496,48},{128,64},{16,80},{160,96},{48,112... | collective-permute-start | bytes 565256 | tf_op jit(solution)/shard_map/ppermute | solution.py:599
  45.3 1.9 %collective-permute-start.2 = (bf16[32,2944]{1,0:T(8,128)(2,1)S(1)}, bf16[32,2944]{1,0:T(8,128)(2,1)S(1)}, u32[]{:S(2)}, u32[]{:S(2)}) collective-permute-start(bf16[32,2944]{1,0:T(8,128)(2,1)S(1)} %bitcast.9), channel_id=1, source_target_pairs={{480,0},{496,16},{0,32},{16,48},{32,64},{48,80},{64,96},{80,112},{... | collective-permute-start | bytes 565256 | tf_op jit(solution)/shard_map/ppermute | solution.py:641
  47.2 4.6 %collective-permute-start.1 = (bf16[32,2944]{1,0:T(8,128)(2,1)S(1)}, bf16[32,2944]{1,0:T(8,128)(2,1)S(1)}, u32[]{:S(2)}, u32[]{:S(2)}) collective-permute-start(bf16[32,2944]{1,0:T(8,128)(2,1)S(1)} %bitcast.10), channel_id=1, source_target_pairs={{32,0},{48,16},{64,32},{80,48},{96,64},{112,80},{128,96},{144,112}... | collective-permute-start | bytes 565256 | tf_op jit(solution)/shard_map/ppermute | solution.py:641
  51.8 4.1 %collective-permute-start = (bf16[32,2944]{1,0:T(8,128)(2,1)S(1)}, bf16[32,2944]{1,0:T(8,128)(2,1)S(1)}, u32[]{:S(2)}, u32[]{:S(2)}) collective-permute-start(bf16[32,2944]{1,0:T(8,128)(2,1)S(1)} %bitcast.11), channel_id=1, source_target_pairs={{0,16},{16,0},{32,48},{48,32},{64,80},{80,64},{96,112},{112,96},{1... | collective-permute-start | bytes 565256 | tf_op jit(solution)/shard_map/ppermute | solution.py:645
  55.8 0.0 all-to-all-done.1.refs_2_.refs_8_.refs_6_
  55.9 0.0 collective-permute-done.3.refs_5_.refs_3_.refs_2_
  55.9 0.0 collective-permute-done.2.refs_4_.refs_2_.refs_1_
  55.9 0.0 collective-permute-done.1.refs_3_.refs_1_.refs_0_
  55.9 0.0 copy-start.1
  55.9 1.0 collective-permute-done.refs_1_.refs_4_
  56.9 1.9 %near.1 = bf16[384,1152]{1,0:T(8,128)(2,1)} custom-call(bf16[32,2944]{1,0:T(8,128)(2,1)S(1)} %bitcast.12, bf16[32,2944]{1,0:T(8,128)(2,1)S(1)} %collective-permute-done.refs_1_.refs_4_, bf16[16,144,128]{2,1,0:T(8,128)(2,1)S(1)} %all-to-all-done.1.refs_2_.refs_8_.refs_6_, bf16[32,2944]{1,0:T(8,128)(2,1)S(1)} %collective-permute-done.1.refs_3_.refs_1_.refs_0_, ...), custom_call_target="tpu_custom_call" | custom-call | flops 113246208 | bytes 3000000 | tf_op jit(solution)/shard_map/near/pallas_call | solution.py:223
  58.8 7.0 %all-to-all-start.2 = ((bf16[16,24,1152]{2,1,0:T(8,128)(2,1)}), bf16[16,24,1152]{2,1,0:T(8,128)(2,1)}, u32[]{:S(2)}, u32[]{:S(2)}) async-start(bf16[16,24,1152]{2,1,0:T(8,128)(2,1)} %bitcast.2), calls=%async_computation.2 | async-start | bytes 1769472 | tf_op jit(solution)/shard_map/all_to_all | solution.py:650
  65.8 3.3 %collective-permute-start.6 = (bf16[32,2944]{1,0:T(8,128)(2,1)S(1)}, bf16[32,2944]{1,0:T(8,128)(2,1)S(1)}, u32[]{:S(2)}, u32[]{:S(2)}) collective-permute-start(bf16[32,2944]{1,0:T(8,128)(2,1)S(1)} %collective-permute-done.3.refs_5_.refs_3_.refs_2_), channel_id=1, source_target_pairs={{0,16},{16,0},{32,48},{48,32},{64,80},{80,64},{96,112},{112,96},{1... | collective-permute-start | bytes 565256 | tf_op jit(solution)/shard_map/ppermute | solution.py:645
  69.1 1.9 %collective-permute-start.5 = (bf16[32,2944]{1,0:T(8,128)(2,1)S(1)}, bf16[32,2944]{1,0:T(8,128)(2,1)S(1)}, u32[]{:S(2)}, u32[]{:S(2)}) collective-permute-start(bf16[32,2944]{1,0:T(8,128)(2,1)S(1)} %collective-permute-done.2.refs_4_.refs_2_.refs_1_), channel_id=1, source_target_pairs={{0,16},{16,0},{32,48},{48,32},{64,80},{80,64},{96,112},{112,96},{1... | collective-permute-start | bytes 565256 | tf_op jit(solution)/shard_map/ppermute | solution.py:645
  71.0 2.4 %collective-permute-start.4 = (bf16[32,2944]{1,0:T(8,128)(2,1)S(1)}, bf16[32,2944]{1,0:T(8,128)(2,1)S(1)}, u32[]{:S(2)}, u32[]{:S(2)}) collective-permute-start(bf16[32,2944]{1,0:T(8,128)(2,1)S(1)} %collective-permute-done.1.refs_3_.refs_1_.refs_0_), channel_id=1, source_target_pairs={{0,16},{16,0},{32,48},{48,32},{64,80},{80,64},{96,112},{112,96},{1... | collective-permute-start | bytes 565256 | tf_op jit(solution)/shard_map/ppermute | solution.py:645
  73.4 0.0 collective-permute-done.6.refs_7_.refs_5_
  73.4 0.0 collective-permute-done.5.refs_6_.refs_4_
  73.4 1.0 collective-permute-done.4.refs_5_.refs_3_
  74.5 1.9 %score.1 = (bf16[16,16,128]{2,1,0:T(8,128)(2,1)S(1)}, f32[16,128]{1,0:T(8,128)S(1)}) custom-call(bf16[32,2944]{1,0:T(8,128)(2,1)S(1)} %bitcast.13, bf16[32,2944]{1,0:T(8,128)(2,1)S(1)} %collective-permute-done.1.refs_3_.refs_1_.refs_0_, bf16[32,2944]{1,0:T(8,128)(2,1)S(1)} %collective-permute-done.2.refs_4_.refs_2_.refs_1_, ...), custom_call_target="tpu_custom_call" | custom-call | flops 536870912 | bytes 2000000 | tf_op jit(solution)/shard_map/score/pallas_call | solution.py:344
  76.4 0.0 copy-done.1
  76.4 0.0 copy-start.2
  76.4 0.9 copy-done.2
  77.4 2.0 %far.1.after_ref = bf16[512,2432]{1,0:T(8,128)(2,1)S(1)} custom-call(bf16[32,2944]{1,0:T(8,128)(2,1)S(1)} %copy-done.2, bf16[32,2944]{1,0:T(8,128)(2,1)S(1)} %collective-permute-done.2.refs_4_.refs_2_.refs_1_, bf16[32,2944]{1,0:T(8,128)(2,1)S(1)} %collective-permute-done.3.refs_5_.refs_3_.refs_2_, ...), custom_call_target="tpu_custom_call" | custom-call | flops 905969664 | bytes 3000000 | tf_op jit(solution)/shard_map/far/pallas_call | solution.py:223
  79.3 1.5 %copy.9.value_ref = bf16[512,2432]{1,0:T(8,128)(2,1)} copy(bf16[512,2432]{1,0:T(8,128)(2,1)S(1)} %far.1.after_ref) | data formatting | bytes 4980736
  80.8 0.0 all-to-all-done.2
  80.8 7.1 %all-to-all-start.3 = ((bf16[16,32,2432]{2,1,0:T(8,128)(2,1)}), bf16[16,32,2432]{2,1,0:T(8,128)(2,1)}, u32[]{:S(2)}, u32[]{:S(2)}) async-start(bf16[16,32,2432]{2,1,0:T(8,128)(2,1)} %bitcast.14), calls=%async_computation.3 | async-start | bytes 4980736 | tf_op jit(solution)/shard_map/all_to_all | solution.py:650
  87.9 0.0 copy-done
  87.9 0.0 copy-start.3
  87.9 1.3 serve.1
  89.2 4.9 %collective-permute-start.7 = (bf16[128,1152]{1,0:T(8,128)(2,1)S(1)}, bf16[128,1152]{1,0:T(8,128)(2,1)S(1)}, u32[]{:S(2)}, u32[]{:S(2)}) collective-permute-start(bf16[128,1152]{1,0:T(8,128)(2,1)S(1)} %get-tuple-element.21), channel_id=1, source_target_pairs={{32,0},{48,16},{64,32},{80,48},{96,64},{112,80},{128,96},{144,112}... | collective-permute-start | bytes 884744 | tf_op jit(solution)/shard_map/ppermute | solution.py:641
  94.1 1.9 %collective-permute-start.8 = (bf16[128,1152]{1,0:T(8,128)(2,1)S(1)}, bf16[128,1152]{1,0:T(8,128)(2,1)S(1)}, u32[]{:S(2)}, u32[]{:S(2)}) collective-permute-start(bf16[128,1152]{1,0:T(8,128)(2,1)S(1)} %get-tuple-element.22), channel_id=1, source_target_pairs={{64,0},{80,16},{96,32},{112,48},{128,64},{144,80},{160,96},{176,11... | collective-permute-start | bytes 884744 | tf_op jit(solution)/shard_map/ppermute | solution.py:641
  96.1 4.3 %collective-permute-start.9 = (bf16[128,1152]{1,0:T(8,128)(2,1)S(1)}, bf16[128,1152]{1,0:T(8,128)(2,1)S(1)}, u32[]{:S(2)}, u32[]{:S(2)}) collective-permute-start(bf16[128,1152]{1,0:T(8,128)(2,1)S(1)} %get-tuple-element.23), channel_id=1, source_target_pairs={{448,0},{464,16},{480,32},{496,48},{0,64},{16,80},{32,96},{48,112}... | collective-permute-start | bytes 884744 | tf_op jit(solution)/shard_map/ppermute | solution.py:641
  100.3 1.9 %collective-permute-start.10 = (bf16[128,1152]{1,0:T(8,128)(2,1)S(1)}, bf16[128,1152]{1,0:T(8,128)(2,1)S(1)}, u32[]{:S(2)}, u32[]{:S(2)}) collective-permute-start(bf16[128,1152]{1,0:T(8,128)(2,1)S(1)} %get-tuple-element.24), channel_id=1, source_target_pairs={{480,0},{496,16},{0,32},{16,48},{32,64},{48,80},{64,96},{80,112},{... | collective-permute-start | bytes 884744 | tf_op jit(solution)/shard_map/ppermute | solution.py:641
  102.3 0.0 collective-permute-done.7.refs_1_
  102.3 10.8 %collective-permute-done.8.refs_2_ = bf16[128,1152]{1,0:T(8,128)(2,1)S(1)} collective-permute-done((bf16[128,1152]{1,0:T(8,128)(2,1)S(1)}, bf16[128,1152]{1,0:T(8,128)(2,1)S(1)}, u32[]{:S(2)}, u32[]{:S(2)}) %collective-permute-start.8) | collective-permute-done | bytes 294944 | tf_op jit(solution)/shard_map/ppermute | solution.py:641
  113.0 0.0 collective-permute-done.9.refs_3_
  113.1 8.5 %collective-permute-done.10.refs_4_ = bf16[128,1152]{1,0:T(8,128)(2,1)S(1)} collective-permute-done((bf16[128,1152]{1,0:T(8,128)(2,1)S(1)}, bf16[128,1152]{1,0:T(8,128)(2,1)S(1)}, u32[]{:S(2)}, u32[]{:S(2)}) %collective-permute-start.10) | collective-permute-done | bytes 294944 | tf_op jit(solution)/shard_map/ppermute | solution.py:641
  121.5 0.1 join.1
  121.6 2.6 %collective-permute-start.11 = (bf16[320,1152]{1,0:T(8,128)(2,1)S(1)}, bf16[320,1152]{1,0:T(8,128)(2,1)S(1)}, u32[]{:S(2)}, u32[]{:S(2)}) collective-permute-start(bf16[320,1152]{1,0:T(8,128)(2,1)S(1)} %join.1), channel_id=1, source_target_pairs={{0,16},{16,0},{32,48},{48,32},{64,80},{80,64},{96,112},{112,96},{1... | collective-permute-start | bytes 2211848 | tf_op jit(solution)/shard_map/ppermute | solution.py:645
  124.1 1.3 reshape.22.q_ref
  125.4 0.4 all-to-all-done.3
  125.9 0.0 copy-done.3
  125.9 5.4 %attend_plane.1 = (f32[4,256,128]{2,1,0:T(8,128)S(1)}, f32[2,256,128]{2,1,0:T(8,128)S(1)}, bf16[2,16384]{1,0:T(2,128)(2,1)}) custom-call(bf16[2,128,576]{2,1,0:T(8,128)(2,1)S(1)} %reshape.22.q_ref, s32[2,32]{1,0:T(2,128)S(1)} %copy-done.3, bf16[384,1152]{1,0:T(8,128)(2,1)} %bitcast.3.after_ref.near_ref, bf16[512,2432]{1,0:T(8,128)(2,1)} %bitcast.5.far_ref), custom_call_target="tpu_custom_call" | custom-call | flops 1660944384 | bytes 4000000 | tf_op jit(solution)/shard_map/attend_plane/pallas_call | solution.py:554
  131.3 0.0 collective-permute-done.11.refs_5_
  131.3 3.0 %attend_column.1 = bf16[2,65536]{1,0:T(2,128)(2,1)} custom-call(bf16[2,128,576]{2,1,0:T(8,128)(2,1)S(1)} %reshape.22.q_ref, s32[2,32]{1,0:T(2,128)S(1)} %copy-done.3, f32[4,256,128]{2,1,0:T(8,128)S(1)} %get-tuple-element.17.before, f32[2,256,128]{2,1,0:T(8,128)S(1)} %get-tuple-element.18.state, bf16[128,1152]{1,0:T(8,128)(2,1)S(1)} %get-tuple-element.20.refs_0_, ...), custom_call_target="tpu_custom_call" | custom-call | flops 754974720 | bytes 3000000 | tf_op jit(solution)/shard_map/attend_column/pallas_call | solution.py:576
  (2 shorter events, 0.0 us)
Async XLA Ops:
  31.5 24.3 %all-to-all-start.1 = ((bf16[16,144,128]{2,1,0:T(8,128)(2,1)}), bf16[16,144,128]{2,1,0:T(8,128)(2,1)S(1)}, u32[]{:S(2)}, u32[]{:S(2)}) async-start(bf16[16,144,128]{2,1,0:T(8,128)(2,1)} %get-tuple-element.15), calls=%async_computation.1 | async-start | bytes 1179648 | tf_op jit(solution)/shard_map/all_to_all | solution.py:670
  38.3 17.6 %collective-permute-start.3 = (bf16[32,2944]{1,0:T(8,128)(2,1)S(1)}, bf16[32,2944]{1,0:T(8,128)(2,1)S(1)}, u32[]{:S(2)}, u32[]{:S(2)}) collective-permute-start(bf16[32,2944]{1,0:T(8,128)(2,1)S(1)} %bitcast.8), channel_id=1, source_target_pairs={{64,0},{464,16},{96,32},{496,48},{128,64},{16,80},{160,96},{48,112... | collective-permute-start | bytes 565256 | tf_op jit(solution)/shard_map/ppermute | solution.py:599
  45.3 10.6 %collective-permute-start.2 = (bf16[32,2944]{1,0:T(8,128)(2,1)S(1)}, bf16[32,2944]{1,0:T(8,128)(2,1)S(1)}, u32[]{:S(2)}, u32[]{:S(2)}) collective-permute-start(bf16[32,2944]{1,0:T(8,128)(2,1)S(1)} %bitcast.9), channel_id=1, source_target_pairs={{480,0},{496,16},{0,32},{16,48},{32,64},{48,80},{64,96},{80,112},{... | collective-permute-start | bytes 565256 | tf_op jit(solution)/shard_map/ppermute | solution.py:641
  47.2 8.7 %collective-permute-start.1 = (bf16[32,2944]{1,0:T(8,128)(2,1)S(1)}, bf16[32,2944]{1,0:T(8,128)(2,1)S(1)}, u32[]{:S(2)}, u32[]{:S(2)}) collective-permute-start(bf16[32,2944]{1,0:T(8,128)(2,1)S(1)} %bitcast.10), channel_id=1, source_target_pairs={{32,0},{48,16},{64,32},{80,48},{96,64},{112,80},{128,96},{144,112}... | collective-permute-start | bytes 565256 | tf_op jit(solution)/shard_map/ppermute | solution.py:641
  51.8 5.1 %collective-permute-start = (bf16[32,2944]{1,0:T(8,128)(2,1)S(1)}, bf16[32,2944]{1,0:T(8,128)(2,1)S(1)}, u32[]{:S(2)}, u32[]{:S(2)}) collective-permute-start(bf16[32,2944]{1,0:T(8,128)(2,1)S(1)} %bitcast.11), channel_id=1, source_target_pairs={{0,16},{16,0},{32,48},{48,32},{64,80},{80,64},{96,112},{112,96},{1... | collective-permute-start | bytes 565256 | tf_op jit(solution)/shard_map/ppermute | solution.py:645
  55.9 20.5 %copy-start.1 = (bf16[32,2944]{1,0:T(8,128)(2,1)}, bf16[32,2944]{1,0:T(8,128)(2,1)S(1)}, u32[]{:S(2)}) copy-start(bf16[32,2944]{1,0:T(8,128)(2,1)S(1)} %collective-permute-done.1.refs_3_.refs_1_.refs_0_) | copy-start | bytes 565252
  58.8 22.0 %all-to-all-start.2 = ((bf16[16,24,1152]{2,1,0:T(8,128)(2,1)}), bf16[16,24,1152]{2,1,0:T(8,128)(2,1)}, u32[]{:S(2)}, u32[]{:S(2)}) async-start(bf16[16,24,1152]{2,1,0:T(8,128)(2,1)} %bitcast.2), calls=%async_computation.2 | async-start | bytes 1769472 | tf_op jit(solution)/shard_map/all_to_all | solution.py:650
  65.8 7.6 %collective-permute-start.6 = (bf16[32,2944]{1,0:T(8,128)(2,1)S(1)}, bf16[32,2944]{1,0:T(8,128)(2,1)S(1)}, u32[]{:S(2)}, u32[]{:S(2)}) collective-permute-start(bf16[32,2944]{1,0:T(8,128)(2,1)S(1)} %collective-permute-done.3.refs_5_.refs_3_.refs_2_), channel_id=1, source_target_pairs={{0,16},{16,0},{32,48},{48,32},{64,80},{80,64},{96,112},{112,96},{1... | collective-permute-start | bytes 565256 | tf_op jit(solution)/shard_map/ppermute | solution.py:645
  69.1 4.4 %collective-permute-start.5 = (bf16[32,2944]{1,0:T(8,128)(2,1)S(1)}, bf16[32,2944]{1,0:T(8,128)(2,1)S(1)}, u32[]{:S(2)}, u32[]{:S(2)}) collective-permute-start(bf16[32,2944]{1,0:T(8,128)(2,1)S(1)} %collective-permute-done.2.refs_4_.refs_2_.refs_1_), channel_id=1, source_target_pairs={{0,16},{16,0},{32,48},{48,32},{64,80},{80,64},{96,112},{112,96},{1... | collective-permute-start | bytes 565256 | tf_op jit(solution)/shard_map/ppermute | solution.py:645
  71.0 3.5 %collective-permute-start.4 = (bf16[32,2944]{1,0:T(8,128)(2,1)S(1)}, bf16[32,2944]{1,0:T(8,128)(2,1)S(1)}, u32[]{:S(2)}, u32[]{:S(2)}) collective-permute-start(bf16[32,2944]{1,0:T(8,128)(2,1)S(1)} %collective-permute-done.1.refs_3_.refs_1_.refs_0_), channel_id=1, source_target_pairs={{0,16},{16,0},{32,48},{48,32},{64,80},{80,64},{96,112},{112,96},{1... | collective-permute-start | bytes 565256 | tf_op jit(solution)/shard_map/ppermute | solution.py:645
  76.4 0.9 copy-start.2
  80.8 7.1 %copy-start = (bf16[512,576]{0,1:T(8,128)(2,1)S(1)}, bf16[512,576]{0,1:T(8,128)(2,1)}, u32[]{:S(2)}) copy-start(bf16[512,576]{0,1:T(8,128)(2,1)} %param.7) | copy-start | bytes 1769476
  80.8 45.0 %all-to-all-start.3 = ((bf16[16,32,2432]{2,1,0:T(8,128)(2,1)}), bf16[16,32,2432]{2,1,0:T(8,128)(2,1)}, u32[]{:S(2)}, u32[]{:S(2)}) async-start(bf16[16,32,2432]{2,1,0:T(8,128)(2,1)} %bitcast.14), calls=%async_computation.3 | async-start | bytes 4980736 | tf_op jit(solution)/shard_map/all_to_all | solution.py:650
  87.9 38.0 %copy-start.3 = (s32[2,32]{1,0:T(2,128)S(1)}, s32[2,32]{1,0:T(2,128)}, u32[]{:S(2)}) copy-start(s32[2,32]{1,0:T(2,128)} %ids_ref.3) | copy-start | bytes 772
  89.2 13.0 %collective-permute-start.7 = (bf16[128,1152]{1,0:T(8,128)(2,1)S(1)}, bf16[128,1152]{1,0:T(8,128)(2,1)S(1)}, u32[]{:S(2)}, u32[]{:S(2)}) collective-permute-start(bf16[128,1152]{1,0:T(8,128)(2,1)S(1)} %get-tuple-element.21), channel_id=1, source_target_pairs={{32,0},{48,16},{64,32},{80,48},{96,64},{112,80},{128,96},{144,112}... | collective-permute-start | bytes 884744 | tf_op jit(solution)/shard_map/ppermute | solution.py:641
  94.1 18.9 %collective-permute-start.8 = (bf16[128,1152]{1,0:T(8,128)(2,1)S(1)}, bf16[128,1152]{1,0:T(8,128)(2,1)S(1)}, u32[]{:S(2)}, u32[]{:S(2)}) collective-permute-start(bf16[128,1152]{1,0:T(8,128)(2,1)S(1)} %get-tuple-element.22), channel_id=1, source_target_pairs={{64,0},{80,16},{96,32},{112,48},{128,64},{144,80},{160,96},{176,11... | collective-permute-start | bytes 884744 | tf_op jit(solution)/shard_map/ppermute | solution.py:641
  96.1 17.0 %collective-permute-start.9 = (bf16[128,1152]{1,0:T(8,128)(2,1)S(1)}, bf16[128,1152]{1,0:T(8,128)(2,1)S(1)}, u32[]{:S(2)}, u32[]{:S(2)}) collective-permute-start(bf16[128,1152]{1,0:T(8,128)(2,1)S(1)} %get-tuple-element.23), channel_id=1, source_target_pairs={{448,0},{464,16},{480,32},{496,48},{0,64},{16,80},{32,96},{48,112}... | collective-permute-start | bytes 884744 | tf_op jit(solution)/shard_map/ppermute | solution.py:641
  100.3 21.2 %collective-permute-start.10 = (bf16[128,1152]{1,0:T(8,128)(2,1)S(1)}, bf16[128,1152]{1,0:T(8,128)(2,1)S(1)}, u32[]{:S(2)}, u32[]{:S(2)}) collective-permute-start(bf16[128,1152]{1,0:T(8,128)(2,1)S(1)} %get-tuple-element.24), channel_id=1, source_target_pairs={{480,0},{496,16},{0,32},{16,48},{32,64},{48,80},{64,96},{80,112},{... | collective-permute-start | bytes 884744 | tf_op jit(solution)/shard_map/ppermute | solution.py:641
  121.6 9.7 %collective-permute-start.11 = (bf16[320,1152]{1,0:T(8,128)(2,1)S(1)}, bf16[320,1152]{1,0:T(8,128)(2,1)S(1)}, u32[]{:S(2)}, u32[]{:S(2)}) collective-permute-start(bf16[320,1152]{1,0:T(8,128)(2,1)S(1)} %join.1), channel_id=1, source_target_pairs={{0,16},{16,0},{32,48},{48,32},{64,80},{80,64},{96,112},{112,96},{1... | collective-permute-start | bytes 2211848 | tf_op jit(solution)/shard_map/ppermute | solution.py:645

commit v6 on v5

--- a/solution.py
+++ b/solution.py
@@ -1,3 +1,5 @@
+import functools
+
 import jax
 import jax.numpy as jnp
 from jax import lax
@@ -411,50 +413,63 @@
     return norm
 
 
-def plane_kernel(q_ref, ids_ref, near_ref, far_ref, total, state, index_ref, scores, turned):
+def plane_kernel(span, q_ref, ids_ref, ref, *refs):
+    if span is NEAR:
+        after_ref, total, state, scores = refs
+    else:
+        before, was, total, state, index_ref, scores, turned = refs
+        far_ref = ref
     ctx, own_block, offsets, padded, sets, tops, keep = attend_start(q_ref, scores)
     ids = ids_ref[...]
     own_row = table_row(own_block)
-    for span, ref, step in ((NEAR, near_ref, 384), (FAR, far_ref, 256)):
-        first, count, slots = span
-        one, two = named_columns(span, [ids[0:1]]), named_columns(span, [ids[1:2]])
-        members = (one[:, 0:1], two[:, 0:1])
-        keys = slot_keys(span, jnp.maximum(one, two))[:, 0:1]
-        halves = 2 if span is NEAR else 1
-        width = PLANE * halves * slots
-        line = iota((count, 128), 0)
-        chosen = keys == (iota((1, width), 1) % slots).astype(f32)
-        limits = []
-        for i in range(2):
-            limit = jnp.where(line[:, 0:1] + first == own_row, offsets[i], 63.0) + 1.0
-            limit = jnp.where(members[i] > 0.5, limit, 0.0)
-            limits.append(jnp.sum(jnp.where(chosen, limit, 0.0), axis=0, keepdims=True))
-        lane = iota((1, width), 1)
-        place = lane // (halves * slots) * PIECE
-        if halves == 2:
-            place = place + lane // slots % 2 * 2
-        for k in range(width // step):
-            rows = slice(k * step, (k + 1) * step)
-            for r in range(PIECE // halves):
-                half, parity = r // 2, r % 2
-                at = half * WIDTH + parity * DL
-                columns = slice(at, at + DL)
-                turn = half * WIDTH + 2 * DL
-                block = product(
-                    padded[parity],
-                    jnp.concatenate([ref[rows, columns], ref[rows, turn : turn + 128]], axis=1),
-                )
-                keep(
-                    block,
-                    (place[:, rows] + r).astype(f32),
-                    [limit[:, rows] for limit in limits],
-                    [(ref, rows, columns)],
-                )
+    step = 384 if span is NEAR else 256
+    first, count, slots = span
+    one, two = named_columns(span, [ids[0:1]]), named_columns(span, [ids[1:2]])
+    members = (one[:, 0:1], two[:, 0:1])
+    keys = slot_keys(span, jnp.maximum(one, two))[:, 0:1]
+    halves = 2 if span is NEAR else 1
+    width = PLANE * halves * slots
+    line = iota((count, 128), 0)
+    chosen = keys == (iota((1, width), 1) % slots).astype(f32)
+    limits = []
+    for i in range(2):
+        limit = jnp.where(line[:, 0:1] + first == own_row, offsets[i], 63.0) + 1.0
+        limit = jnp.where(members[i] > 0.5, limit, 0.0)
+        limits.append(jnp.sum(jnp.where(chosen, limit, 0.0), axis=0, keepdims=True))
+    lane = iota((1, width), 1)
+    place = lane // (halves * slots) * PIECE
+    if halves == 2:
+        place = place + lane // slots % 2 * 2
+    for k in range(width // step):
+        rows = slice(k * step, (k + 1) * step)
+        for r in range(PIECE // halves):
+            half, parity = r // 2, r % 2
+            at = half * WIDTH + parity * DL
+            columns = slice(at, at + DL)
+            turn = half * WIDTH + 2 * DL
+            block = product(
+                padded[parity],
+                jnp.concatenate([ref[rows, columns], ref[rows, turn : turn + 128]], axis=1),
+            )
+            keep(
+                block,
+                (place[:, rows] + r).astype(f32),
+                [limit[:, rows] for limit in limits],
+                [(ref, rows, columns)],
+            )
 
     highest = jnp.max(jnp.concatenate(tops, axis=0), axis=1, keepdims=True)
-    norm = jnp.zeros((2 * HEADS, 128), f32)
+    if span is NEAR:
+        norm = jnp.zeros((2 * HEADS, 128), f32)
+        state[0] = jnp.broadcast_to(highest, (2 * HEADS, 128))
+        state[1] = attend_sum(scores, sets, highest, norm, total, True)
+        return
+    highest = jnp.maximum(highest, was[0][:, 0:1])
+    fade = jnp.exp((was[0] - highest) * score_scale)
+    for k in range(4):
+        total[k] = before[k] * fade
     state[0] = jnp.broadcast_to(highest, (2 * HEADS, 128))
-    state[1] = attend_sum(scores, sets, highest, norm, total, True)
+    state[1] = attend_sum(scores, sets, highest, was[1] * fade, total, False)
 
     tiles = [
         far_ref[p * FAR[2] : p * FAR[2] + 16, KV_COLS:].astype(f32)
@@ -550,26 +565,43 @@
             out_ref[:, at : at + 128] = total[k, pl.ds(h, 2, stride=HEADS), :].astype(bf16)
 
 
-def attend_plane(query, ids, near, far):
-    return pl.pallas_call(
-        plane_kernel,
-        out_shape=(
-            jax.ShapeDtypeStruct((4, 2 * HEADS, 128), f32),
-            jax.ShapeDtypeStruct((2, 2 * HEADS, 128), f32),
-            jax.ShapeDtypeStruct((2, 16384), bf16),
+STATES = (
+    jax.ShapeDtypeStruct((4, 2 * HEADS, 128), f32),
+    jax.ShapeDtypeStruct((2, 2 * HEADS, 128), f32),
+)
+
+
+def attend_near(query, ids, near, after):
+    return pl.pallas_call(
+        functools.partial(plane_kernel, NEAR),
+        out_shape=STATES,
+        in_specs=[whole()] * 3 + [anywhere()],
+        out_specs=(whole(),) * 2,
+        scratch_shapes=[pltpu.VMEM((2 * HEADS, 768), f32)],
+        compiler_params=params(),
+        cost_estimate=pl.CostEstimate(
+            flops=2 * 256 * 768 * 1152, bytes_accessed=2_000_000, transcendentals=256 * 768
         ),
-        in_specs=[whole()] * 4,
+        name="attend_near",
+    )(query, ids, near, after)
+
+
+def attend_far(query, ids, far, before, state):
+    return pl.pallas_call(
+        functools.partial(plane_kernel, FAR),
+        out_shape=STATES + (jax.ShapeDtypeStruct((2, 16384), bf16),),
+        in_specs=[whole()] * 5,
         out_specs=(whole(),) * 3,
         scratch_shapes=[
-            pltpu.VMEM((2 * HEADS, 2816), f32),
+            pltpu.VMEM((2 * HEADS, 2048), f32),
             pltpu.VMEM((256, 128), f32),
         ],
         compiler_params=params(),
         cost_estimate=pl.CostEstimate(
-            flops=2 * 256 * 2816 * 1152, bytes_accessed=4_000_000, transcendentals=256 * 2816
+            flops=2 * 256 * 2048 * 1152, bytes_accessed=4_000_000, transcendentals=256 * 2048
         ),
-        name="attend_plane",
-    )(query, ids, near, far)
+        name="attend_far",
+    )(query, ids, far, before, state)
 
 
 def attend_column(query, ids, before, state, mine, crossed):
@@ -682,7 +714,8 @@
         mine.append(level_from(served[AWAYS.index(-away % LEVELS)], away))
     crossed = swap(join(mine))
     query = q_latent.reshape(2, HEADS, DQK)
-    before, state, scores = attend_plane(query, q_blocks, near, far)
+    before, state = attend_near(query, q_blocks, near, mine[1])
+    before, state, scores = attend_far(query, q_blocks, far, before, state)
     return (attend_column(query, q_blocks, before, state, mine, crossed), scores)
 
 

time: 136 us -> 143 us (1.051)
  local copies, waits for them, and re-layouts: 3.67 us -> 7.22 us
  Pallas kernels: 18 us -> 19.5 us
    unnamed x9 -> x17, local copies, waits for them, and re-layouts: 2.4 us -> 5.94 us
    ppermute x5, starting transfers between devices: 14.2 us -> 17.5 us  [swap(): lax.ppermute(value, 'ctx', [(at, at ^ 1) for at in range(2 * LEVELS)])]
    ppermute x6, waiting for transfers between devices: 19.3 us -> 22 us  [level_from(): return lax.ppermute(value, 'ctx', pairs)]
    ppermute x1, starting transfers between devices: 6.95 us -> 5.01 us  [two_levels_on(): return lax.ppermute(value, 'ctx', pairs)]
    pallas_call x1 -> x2, Pallas kernels: 5.45 us -> 6.97 us  [the longest x1 4.64 us: attend_far(): pl.pallas_call(functools.partial(plane_kernel, FAR), out_shape=STATES + (...]
  transfers between devices with their start and end apart: 15 -> 15, of which waited for: 5 -> 6; matrix products, arithmetic and copies ran while one was open for 2% -> 2% of each run, Pallas kernels for 8% -> 9%
where the time goes in v6:
time: 143 us; the launch traced here: 142 us
  starting transfers between devices  62.6 us (44%)
  blocking collectives  28.5 us (20%)
  waiting for transfers between devices  23.1 us (16%)
  Pallas kernels  19.5 us (14%)
  local copies, waits for them, and re-layouts  7.22 us (5%)
    all_to_all x1, blocking collectives, outer_levels(): lax.all_to_all(chunks, 'ctx', split_axis=0, concat_axis=0, axis_index_gro...  28.5 us
    ppermute x6, waiting for transfers between devices, level_from(): return lax.ppermute(value, 'ctx', pairs)  22 us
    ppermute x6, starting transfers between devices, level_from(): return lax.ppermute(value, 'ctx', pairs)  19.2 us
    ppermute x5, starting transfers between devices, swap(): lax.ppermute(value, 'ctx', [(at, at ^ 1) for at in range(2 * LEVELS)])  17.5 us
    all_to_all x2, starting transfers between devices, exchange(): got = lax.all_to_all(parts, 'pb', split_axis=0, concat_axis=0, tiled=True)  14 us
    all_to_all x1, starting transfers between devices, local(): y = lax.all_to_all(y, 'pb', split_axis=0, concat_axis=0, tiled=True)  6.77 us
    unnamed x17, local copies, waits for them, and re-layouts  5.94 us
    ppermute x1, starting transfers between devices, two_levels_on(): return lax.ppermute(value, 'ctx', pairs)  5.01 us
  transfers between devices with their start and end apart: 15, of which 6 were waited for; matrix products, arithmetic and copies ran while one was open for 2% of the time, Pallas kernels for 9%

profile of v6, /device:TPU:1, one launch (start us, length us, event | category | flops | bytes accessed | tf_op | source)
XLA Modules:
  0.0 141.8 jit_solution(10038888875305128703)
XLA Ops:
  0.6 2.3 %pack.1 = (bf16[4,8,2944]{2,1,0:T(8,128)(2,1)}, bf16[16,144,128]{2,1,0:T(8,128)(2,1)}) custom-call(bf16[576,512]{1,0:T(8,128)(2,1)} %bitcast.6, bf16[32,128]{1,0:T(8,128)(2,1)} %refs_1_.1, bf16[2,8192]{1,0:T(2,128)(2,1)} %refs_2_.1, bf16[2,64]{1,0:T(2,128)(2,1)} %refs_3_.1, s32[2,32]{1,0:T(2,128)} %ids_ref.5), custom_call_target="tpu_custom_call" | custom-call | tf_op jit(solution)/shard_map/pack/pallas_call | solution.py:124
  3.0 28.5 %all_to_all.20 = bf16[4,8,2944]{2,1,0:T(8,128)(2,1)S(1)} all-to-all(bf16[4,8,2944]{2,1,0:T(8,128)(2,1)} %get-tuple-element.16), channel_id=1, replica_groups={{0,128,256,384},{16,144,272,400},{32,160,288,416},{48,176,304,432},{64,..., dimensions={0} | all-to-all | bytes 376832 | tf_op jit(solution)/shard_map/all_to_all | solution.py:692
  31.5 6.8 %all-to-all-start.1 = ((bf16[16,144,128]{2,1,0:T(8,128)(2,1)}), bf16[16,144,128]{2,1,0:T(8,128)(2,1)S(1)}, u32[]{:S(2)}, u32[]{:S(2)}) async-start(bf16[16,144,128]{2,1,0:T(8,128)(2,1)} %get-tuple-element.17), calls=%async_computation.1 | async-start | bytes 1179648 | tf_op jit(solution)/shard_map/all_to_all | solution.py:702
  38.3 6.8 %collective-permute-start.6 = (bf16[32,2944]{1,0:T(8,128)(2,1)S(1)}, bf16[32,2944]{1,0:T(8,128)(2,1)S(1)}, u32[]{:S(2)}, u32[]{:S(2)}) collective-permute-start(bf16[32,2944]{1,0:T(8,128)(2,1)S(1)} %bitcast.8), channel_id=1, source_target_pairs={{0,16},{16,0},{32,48},{48,32},{64,80},{80,64},{96,112},{112,96},{1... | collective-permute-start | bytes 565256 | tf_op jit(solution)/shard_map/ppermute | solution.py:677
  45.1 5.0 %collective-permute-start.2 = (bf16[32,2944]{1,0:T(8,128)(2,1)S(1)}, bf16[32,2944]{1,0:T(8,128)(2,1)S(1)}, u32[]{:S(2)}, u32[]{:S(2)}) collective-permute-start(bf16[32,2944]{1,0:T(8,128)(2,1)S(1)} %bitcast.9), channel_id=1, source_target_pairs={{64,0},{464,16},{96,32},{496,48},{128,64},{16,80},{160,96},{48,112... | collective-permute-start | bytes 565256 | tf_op jit(solution)/shard_map/ppermute | solution.py:631
  50.1 1.9 %collective-permute-start.1 = (bf16[32,2944]{1,0:T(8,128)(2,1)S(1)}, bf16[32,2944]{1,0:T(8,128)(2,1)S(1)}, u32[]{:S(2)}, u32[]{:S(2)}) collective-permute-start(bf16[32,2944]{1,0:T(8,128)(2,1)S(1)} %bitcast.10), channel_id=1, source_target_pairs={{480,0},{496,16},{0,32},{16,48},{32,64},{48,80},{64,96},{80,112},{... | collective-permute-start | bytes 565256 | tf_op jit(solution)/shard_map/ppermute | solution.py:673
  52.1 4.6 %collective-permute-start = (bf16[32,2944]{1,0:T(8,128)(2,1)S(1)}, bf16[32,2944]{1,0:T(8,128)(2,1)S(1)}, u32[]{:S(2)}, u32[]{:S(2)}) collective-permute-start(bf16[32,2944]{1,0:T(8,128)(2,1)S(1)} %bitcast.11), channel_id=1, source_target_pairs={{32,0},{48,16},{64,32},{80,48},{96,64},{112,80},{128,96},{144,112}... | collective-permute-start | bytes 565256 | tf_op jit(solution)/shard_map/ppermute | solution.py:673
  56.6 0.0 all-to-all-done.1.refs_8_.refs_6_.refs_2_
  56.7 0.0 collective-permute-done.6.refs_4_.refs_1_
  56.7 0.0 collective-permute-done.2.refs_3_.refs_2_.refs_5_
  56.7 3.0 %collective-permute-done.1.refs_2_.refs_1_.refs_4_ = bf16[32,2944]{1,0:T(8,128)(2,1)S(1)} collective-permute-done((bf16[32,2944]{1,0:T(8,128)(2,1)S(1)}, bf16[32,2944]{1,0:T(8,128)(2,1)S(1)}, u32[]{:S(2)}, u32[]{:S(2)}) %collective-permute-start.1) | collective-permute-done | bytes 188448 | tf_op jit(solution)/shard_map/ppermute | solution.py:673
  59.7 0.8 collective-permute-done.refs_1_.refs_0_.refs_3_
  60.6 1.9 %near.1 = bf16[384,1152]{1,0:T(8,128)(2,1)} custom-call(bf16[32,2944]{1,0:T(8,128)(2,1)S(1)} %bitcast.12, bf16[32,2944]{1,0:T(8,128)(2,1)S(1)} %collective-permute-done.6.refs_4_.refs_1_, bf16[16,144,128]{2,1,0:T(8,128)(2,1)S(1)} %all-to-all-done.1.refs_8_.refs_6_.refs_2_, bf16[32,2944]{1,0:T(8,128)(2,1)S(1)} %collective-permute-done.refs_1_.refs_0_.refs_3_, ...), custom_call_target="tpu_custom_call" | custom-call | flops 113246208 | bytes 3000000 | tf_op jit(solution)/shard_map/near/pallas_call | solution.py:225
  62.5 7.0 %all-to-all-start.2 = ((bf16[16,24,1152]{2,1,0:T(8,128)(2,1)}), bf16[16,24,1152]{2,1,0:T(8,128)(2,1)}, u32[]{:S(2)}, u32[]{:S(2)}) async-start(bf16[16,24,1152]{2,1,0:T(8,128)(2,1)} %bitcast.2), calls=%async_computation.2 | async-start | bytes 1769472 | tf_op jit(solution)/shard_map/all_to_all | solution.py:682
  69.5 2.7 %collective-permute-start.5 = (bf16[32,2944]{1,0:T(8,128)(2,1)S(1)}, bf16[32,2944]{1,0:T(8,128)(2,1)S(1)}, u32[]{:S(2)}, u32[]{:S(2)}) collective-permute-start(bf16[32,2944]{1,0:T(8,128)(2,1)S(1)} %collective-permute-done.2.refs_3_.refs_2_.refs_5_), channel_id=1, source_target_pairs={{0,16},{16,0},{32,48},{48,32},{64,80},{80,64},{96,112},{112,96},{1... | collective-permute-start | bytes 565256 | tf_op jit(solution)/shard_map/ppermute | solution.py:677
  72.2 1.9 %collective-permute-start.4 = (bf16[32,2944]{1,0:T(8,128)(2,1)S(1)}, bf16[32,2944]{1,0:T(8,128)(2,1)S(1)}, u32[]{:S(2)}, u32[]{:S(2)}) collective-permute-start(bf16[32,2944]{1,0:T(8,128)(2,1)S(1)} %collective-permute-done.1.refs_2_.refs_1_.refs_4_), channel_id=1, source_target_pairs={{0,16},{16,0},{32,48},{48,32},{64,80},{80,64},{96,112},{112,96},{1... | collective-permute-start | bytes 565256 | tf_op jit(solution)/shard_map/ppermute | solution.py:677
  74.1 2.4 %collective-permute-start.3 = (bf16[32,2944]{1,0:T(8,128)(2,1)S(1)}, bf16[32,2944]{1,0:T(8,128)(2,1)S(1)}, u32[]{:S(2)}, u32[]{:S(2)}) collective-permute-start(bf16[32,2944]{1,0:T(8,128)(2,1)S(1)} %collective-permute-done.refs_1_.refs_0_.refs_3_), channel_id=1, source_target_pairs={{0,16},{16,0},{32,48},{48,32},{64,80},{80,64},{96,112},{112,96},{1... | collective-permute-start | bytes 565256 | tf_op jit(solution)/shard_map/ppermute | solution.py:677
  76.6 0.0 collective-permute-done.5.refs_7_.refs_5_
  76.6 0.0 collective-permute-done.4.refs_6_.refs_4_
  76.6 1.0 collective-permute-done.3.refs_5_.refs_3_
  77.6 1.9 %score.1 = (bf16[16,16,128]{2,1,0:T(8,128)(2,1)S(1)}, f32[16,128]{1,0:T(8,128)S(1)}) custom-call(bf16[32,2944]{1,0:T(8,128)(2,1)S(1)} %bitcast.13, bf16[32,2944]{1,0:T(8,128)(2,1)S(1)} %collective-permute-done.refs_1_.refs_0_.refs_3_, bf16[32,2944]{1,0:T(8,128)(2,1)S(1)} %collective-permute-done.1.refs_2_.refs_1_.refs_4_, ...), custom_call_target="tpu_custom_call" | custom-call | flops 536870912 | bytes 2000000 | tf_op jit(solution)/shard_map/score/pallas_call | solution.py:346
  79.6 0.0 copy-start.2
  79.6 0.9 copy-done.2
  80.5 2.0 %far.1.after_ref = bf16[512,2432]{1,0:T(8,128)(2,1)S(1)} custom-call(bf16[32,2944]{1,0:T(8,128)(2,1)S(1)} %copy-done.2, bf16[32,2944]{1,0:T(8,128)(2,1)S(1)} %collective-permute-done.1.refs_2_.refs_1_.refs_4_, bf16[32,2944]{1,0:T(8,128)(2,1)S(1)} %collective-permute-done.2.refs_3_.refs_2_.refs_5_, ...), custom_call_target="tpu_custom_call" | custom-call | flops 905969664 | bytes 3000000 | tf_op jit(solution)/shard_map/far/pallas_call | solution.py:225
  82.5 1.5 %copy.9.value_ref = bf16[512,2432]{1,0:T(8,128)(2,1)} copy(bf16[512,2432]{1,0:T(8,128)(2,1)S(1)} %far.1.after_ref) | data formatting | bytes 4980736
  84.0 0.0 all-to-all-done.2
  84.0 7.1 %all-to-all-start.3 = ((bf16[16,32,2432]{2,1,0:T(8,128)(2,1)}), bf16[16,32,2432]{2,1,0:T(8,128)(2,1)}, u32[]{:S(2)}, u32[]{:S(2)}) async-start(bf16[16,32,2432]{2,1,0:T(8,128)(2,1)} %bitcast.14), calls=%async_computation.3 | async-start | bytes 4980736 | tf_op jit(solution)/shard_map/all_to_all | solution.py:682
  91.1 0.0 copy-start.3
  91.1 1.3 serve.1
  92.4 4.6 %collective-permute-start.7 = (bf16[128,1152]{1,0:T(8,128)(2,1)S(1)}, bf16[128,1152]{1,0:T(8,128)(2,1)S(1)}, u32[]{:S(2)}, u32[]{:S(2)}) collective-permute-start(bf16[128,1152]{1,0:T(8,128)(2,1)S(1)} %get-tuple-element.20), channel_id=1, source_target_pairs={{32,0},{48,16},{64,32},{80,48},{96,64},{112,80},{128,96},{144,112}... | collective-permute-start | bytes 884744 | tf_op jit(solution)/shard_map/ppermute | solution.py:673
  97.0 1.9 %collective-permute-start.8 = (bf16[128,1152]{1,0:T(8,128)(2,1)S(1)}, bf16[128,1152]{1,0:T(8,128)(2,1)S(1)}, u32[]{:S(2)}, u32[]{:S(2)}) collective-permute-start(bf16[128,1152]{1,0:T(8,128)(2,1)S(1)} %get-tuple-element.26), channel_id=1, source_target_pairs={{64,0},{80,16},{96,32},{112,48},{128,64},{144,80},{160,96},{176,11... | collective-permute-start | bytes 884744 | tf_op jit(solution)/shard_map/ppermute | solution.py:673
  99.0 4.3 %collective-permute-start.9 = (bf16[128,1152]{1,0:T(8,128)(2,1)S(1)}, bf16[128,1152]{1,0:T(8,128)(2,1)S(1)}, u32[]{:S(2)}, u32[]{:S(2)}) collective-permute-start(bf16[128,1152]{1,0:T(8,128)(2,1)S(1)} %get-tuple-element.27), channel_id=1, source_target_pairs={{448,0},{464,16},{480,32},{496,48},{0,64},{16,80},{32,96},{48,112}... | collective-permute-start | bytes 884744 | tf_op jit(solution)/shard_map/ppermute | solution.py:673
  103.2 1.9 %collective-permute-start.10 = (bf16[128,1152]{1,0:T(8,128)(2,1)S(1)}, bf16[128,1152]{1,0:T(8,128)(2,1)S(1)}, u32[]{:S(2)}, u32[]{:S(2)}) collective-permute-start(bf16[128,1152]{1,0:T(8,128)(2,1)S(1)} %get-tuple-element.28), channel_id=1, source_target_pairs={{480,0},{496,16},{0,32},{16,48},{32,64},{48,80},{64,96},{80,112},{... | collective-permute-start | bytes 884744 | tf_op jit(solution)/shard_map/ppermute | solution.py:673
  105.2 0.0 collective-permute-done.7.refs_0_.refs_1_
  105.2 10.2 %collective-permute-done.8.refs_2_ = bf16[128,1152]{1,0:T(8,128)(2,1)S(1)} collective-permute-done((bf16[128,1152]{1,0:T(8,128)(2,1)S(1)}, bf16[128,1152]{1,0:T(8,128)(2,1)S(1)}, u32[]{:S(2)}, u32[]{:S(2)}) %collective-permute-start.8) | collective-permute-done | bytes 294944 | tf_op jit(solution)/shard_map/ppermute | solution.py:673
  115.4 2.6 %collective-permute-done.9.refs_3_ = bf16[128,1152]{1,0:T(8,128)(2,1)S(1)} collective-permute-done((bf16[128,1152]{1,0:T(8,128)(2,1)S(1)}, bf16[128,1152]{1,0:T(8,128)(2,1)S(1)}, u32[]{:S(2)}, u32[]{:S(2)}) %collective-permute-start.9) | collective-permute-done | bytes 294944 | tf_op jit(solution)/shard_map/ppermute | solution.py:673
  117.9 5.4 %collective-permute-done.10.refs_4_ = bf16[128,1152]{1,0:T(8,128)(2,1)S(1)} collective-permute-done((bf16[128,1152]{1,0:T(8,128)(2,1)S(1)}, bf16[128,1152]{1,0:T(8,128)(2,1)S(1)}, u32[]{:S(2)}, u32[]{:S(2)}) %collective-permute-start.10) | collective-permute-done | bytes 294944 | tf_op jit(solution)/shard_map/ppermute | solution.py:673
  123.3 0.1 join.1
  123.4 3.7 %collective-permute-start.11 = (bf16[320,1152]{1,0:T(8,128)(2,1)S(1)}, bf16[320,1152]{1,0:T(8,128)(2,1)S(1)}, u32[]{:S(2)}, u32[]{:S(2)}) collective-permute-start(bf16[320,1152]{1,0:T(8,128)(2,1)S(1)} %join.1), channel_id=1, source_target_pairs={{0,16},{16,0},{32,48},{48,32},{64,80},{80,64},{96,112},{112,96},{1... | collective-permute-start | bytes 2211848 | tf_op jit(solution)/shard_map/ppermute | solution.py:677
  127.1 1.3 reshape.22.q_ref
  128.3 2.3 %attend_near.1 = (f32[4,256,128]{2,1,0:T(8,128)S(1)}, f32[2,256,128]{2,1,0:T(8,128)S(1)}) custom-call(bf16[2,128,576]{2,1,0:T(8,128)(2,1)S(1)} %reshape.22.q_ref, s32[2,32]{1,0:T(2,128)S(1)} %copy-done.3, bf16[384,1152]{1,0:T(8,128)(2,1)} %bitcast.3.after_ref.ref, bf16[128,1152]{1,0:T(8,128)(2,1)S(1)} %collective-permute-done.7.refs_0_.refs_1_), custom_call_target="tpu_custom_call" | custom-call | flops 452984832 | bytes 2000000 | tf_op jit(solution)/shard_map/attend_near/pallas_call | solution.py:575
  130.7 0.8 copy-done.4
  131.5 0.7 copy-done.6
  132.2 0.0 all-to-all-done.3
  132.2 1.0 copy-done.5
  133.3 0.9 copy-done.7
  134.2 4.6 %attend_far.1 = (f32[4,256,128]{2,1,0:T(8,128)S(1)}, f32[2,256,128]{2,1,0:T(8,128)S(1)}, bf16[2,16384]{1,0:T(2,128)(2,1)}) custom-call(bf16[2,128,576]{2,1,0:T(8,128)(2,1)S(1)} %reshape.22.q_ref, s32[2,32]{1,0:T(2,128)S(1)} %copy-done.3, bf16[512,2432]{1,0:T(8,128)(2,1)} %bitcast.5.ref, f32[4,256,128]{2,1,0:T(8,128)S(1)} %copy-done.5, ...), custom_call_target="tpu_custom_call" | custom-call | flops 1207959552 | bytes 4000000 | tf_op jit(solution)/shard_map/attend_far/pallas_call | solution.py:590
  138.9 3.0 %attend_column.1 = bf16[2,65536]{1,0:T(2,128)(2,1)} custom-call(bf16[2,128,576]{2,1,0:T(8,128)(2,1)S(1)} %reshape.22.q_ref, s32[2,32]{1,0:T(2,128)S(1)} %copy-done.3, f32[4,256,128]{2,1,0:T(8,128)S(1)} %get-tuple-element.23.before, f32[2,256,128]{2,1,0:T(8,128)S(1)} %get-tuple-element.24.state, bf16[128,1152]{1,0:T(8,128)(2,1)S(1)} %get-tuple-element.25.refs_0_, ...), custom_call_target="tpu_custom_call" | custom-call | flops 754974720 | bytes 3000000 | tf_op jit(solution)/shard_map/attend_column/pallas_call | solution.py:608
  (11 shorter events, 0.0 us)
Async XLA Ops:
  31.5 25.1 %all-to-all-start.1 = ((bf16[16,144,128]{2,1,0:T(8,128)(2,1)}), bf16[16,144,128]{2,1,0:T(8,128)(2,1)S(1)}, u32[]{:S(2)}, u32[]{:S(2)}) async-start(bf16[16,144,128]{2,1,0:T(8,128)(2,1)} %get-tuple-element.17), calls=%async_computation.1 | async-start | bytes 1179648 | tf_op jit(solution)/shard_map/all_to_all | solution.py:702
  38.3 18.4 %collective-permute-start.6 = (bf16[32,2944]{1,0:T(8,128)(2,1)S(1)}, bf16[32,2944]{1,0:T(8,128)(2,1)S(1)}, u32[]{:S(2)}, u32[]{:S(2)}) collective-permute-start(bf16[32,2944]{1,0:T(8,128)(2,1)S(1)} %bitcast.8), channel_id=1, source_target_pairs={{0,16},{16,0},{32,48},{48,32},{64,80},{80,64},{96,112},{112,96},{1... | collective-permute-start | bytes 565256 | tf_op jit(solution)/shard_map/ppermute | solution.py:677
  45.1 11.5 %collective-permute-start.2 = (bf16[32,2944]{1,0:T(8,128)(2,1)S(1)}, bf16[32,2944]{1,0:T(8,128)(2,1)S(1)}, u32[]{:S(2)}, u32[]{:S(2)}) collective-permute-start(bf16[32,2944]{1,0:T(8,128)(2,1)S(1)} %bitcast.9), channel_id=1, source_target_pairs={{64,0},{464,16},{96,32},{496,48},{128,64},{16,80},{160,96},{48,112... | collective-permute-start | bytes 565256 | tf_op jit(solution)/shard_map/ppermute | solution.py:631
  50.1 9.6 %collective-permute-start.1 = (bf16[32,2944]{1,0:T(8,128)(2,1)S(1)}, bf16[32,2944]{1,0:T(8,128)(2,1)S(1)}, u32[]{:S(2)}, u32[]{:S(2)}) collective-permute-start(bf16[32,2944]{1,0:T(8,128)(2,1)S(1)} %bitcast.10), channel_id=1, source_target_pairs={{480,0},{496,16},{0,32},{16,48},{32,64},{48,80},{64,96},{80,112},{... | collective-permute-start | bytes 565256 | tf_op jit(solution)/shard_map/ppermute | solution.py:673
  52.1 8.5 %collective-permute-start = (bf16[32,2944]{1,0:T(8,128)(2,1)S(1)}, bf16[32,2944]{1,0:T(8,128)(2,1)S(1)}, u32[]{:S(2)}, u32[]{:S(2)}) collective-permute-start(bf16[32,2944]{1,0:T(8,128)(2,1)S(1)} %bitcast.11), channel_id=1, source_target_pairs={{32,0},{48,16},{64,32},{80,48},{96,64},{112,80},{128,96},{144,112}... | collective-permute-start | bytes 565256 | tf_op jit(solution)/shard_map/ppermute | solution.py:673
  60.6 19.0 %copy-start.1 = (bf16[32,2944]{1,0:T(8,128)(2,1)}, bf16[32,2944]{1,0:T(8,128)(2,1)S(1)}, u32[]{:S(2)}) copy-start(bf16[32,2944]{1,0:T(8,128)(2,1)S(1)} %collective-permute-done.refs_1_.refs_0_.refs_3_) | copy-start | bytes 565252
  62.5 21.5 %all-to-all-start.2 = ((bf16[16,24,1152]{2,1,0:T(8,128)(2,1)}), bf16[16,24,1152]{2,1,0:T(8,128)(2,1)}, u32[]{:S(2)}, u32[]{:S(2)}) async-start(bf16[16,24,1152]{2,1,0:T(8,128)(2,1)} %bitcast.2), calls=%async_computation.2 | async-start | bytes 1769472 | tf_op jit(solution)/shard_map/all_to_all | solution.py:682
  69.5 7.1 %collective-permute-start.5 = (bf16[32,2944]{1,0:T(8,128)(2,1)S(1)}, bf16[32,2944]{1,0:T(8,128)(2,1)S(1)}, u32[]{:S(2)}, u32[]{:S(2)}) collective-permute-start(bf16[32,2944]{1,0:T(8,128)(2,1)S(1)} %collective-permute-done.2.refs_3_.refs_2_.refs_5_), channel_id=1, source_target_pairs={{0,16},{16,0},{32,48},{48,32},{64,80},{80,64},{96,112},{112,96},{1... | collective-permute-start | bytes 565256 | tf_op jit(solution)/shard_map/ppermute | solution.py:677
  72.2 4.4 %collective-permute-start.4 = (bf16[32,2944]{1,0:T(8,128)(2,1)S(1)}, bf16[32,2944]{1,0:T(8,128)(2,1)S(1)}, u32[]{:S(2)}, u32[]{:S(2)}) collective-permute-start(bf16[32,2944]{1,0:T(8,128)(2,1)S(1)} %collective-permute-done.1.refs_2_.refs_1_.refs_4_), channel_id=1, source_target_pairs={{0,16},{16,0},{32,48},{48,32},{64,80},{80,64},{96,112},{112,96},{1... | collective-permute-start | bytes 565256 | tf_op jit(solution)/shard_map/ppermute | solution.py:677
  74.1 3.5 %collective-permute-start.3 = (bf16[32,2944]{1,0:T(8,128)(2,1)S(1)}, bf16[32,2944]{1,0:T(8,128)(2,1)S(1)}, u32[]{:S(2)}, u32[]{:S(2)}) collective-permute-start(bf16[32,2944]{1,0:T(8,128)(2,1)S(1)} %collective-permute-done.refs_1_.refs_0_.refs_3_), channel_id=1, source_target_pairs={{0,16},{16,0},{32,48},{48,32},{64,80},{80,64},{96,112},{112,96},{1... | collective-permute-start | bytes 565256 | tf_op jit(solution)/shard_map/ppermute | solution.py:677
  79.6 0.9 copy-start.2
  84.0 7.1 %copy-start = (bf16[512,576]{0,1:T(8,128)(2,1)S(1)}, bf16[512,576]{0,1:T(8,128)(2,1)}, u32[]{:S(2)}) copy-start(bf16[512,576]{0,1:T(8,128)(2,1)} %param.7) | copy-start | bytes 1769476
  84.0 48.3 %all-to-all-start.3 = ((bf16[16,32,2432]{2,1,0:T(8,128)(2,1)}), bf16[16,32,2432]{2,1,0:T(8,128)(2,1)}, u32[]{:S(2)}, u32[]{:S(2)}) async-start(bf16[16,32,2432]{2,1,0:T(8,128)(2,1)} %bitcast.14), calls=%async_computation.3 | async-start | bytes 4980736 | tf_op jit(solution)/shard_map/all_to_all | solution.py:682
  91.1 37.3 %copy-start.3 = (s32[2,32]{1,0:T(2,128)S(1)}, s32[2,32]{1,0:T(2,128)}, u32[]{:S(2)}) copy-start(s32[2,32]{1,0:T(2,128)} %ids_ref.5) | copy-start | bytes 772
  92.4 12.8 %collective-permute-start.7 = (bf16[128,1152]{1,0:T(8,128)(2,1)S(1)}, bf16[128,1152]{1,0:T(8,128)(2,1)S(1)}, u32[]{:S(2)}, u32[]{:S(2)}) collective-permute-start(bf16[128,1152]{1,0:T(8,128)(2,1)S(1)} %get-tuple-element.20), channel_id=1, source_target_pairs={{32,0},{48,16},{64,32},{80,48},{96,64},{112,80},{128,96},{144,112}... | collective-permute-start | bytes 884744 | tf_op jit(solution)/shard_map/ppermute | solution.py:673
  97.0 18.3 %collective-permute-start.8 = (bf16[128,1152]{1,0:T(8,128)(2,1)S(1)}, bf16[128,1152]{1,0:T(8,128)(2,1)S(1)}, u32[]{:S(2)}, u32[]{:S(2)}) collective-permute-start(bf16[128,1152]{1,0:T(8,128)(2,1)S(1)} %get-tuple-element.26), channel_id=1, source_target_pairs={{64,0},{80,16},{96,32},{112,48},{128,64},{144,80},{160,96},{176,11... | collective-permute-start | bytes 884744 | tf_op jit(solution)/shard_map/ppermute | solution.py:673
  99.0 19.0 %collective-permute-start.9 = (bf16[128,1152]{1,0:T(8,128)(2,1)S(1)}, bf16[128,1152]{1,0:T(8,128)(2,1)S(1)}, u32[]{:S(2)}, u32[]{:S(2)}) collective-permute-start(bf16[128,1152]{1,0:T(8,128)(2,1)S(1)} %get-tuple-element.27), channel_id=1, source_target_pairs={{448,0},{464,16},{480,32},{496,48},{0,64},{16,80},{32,96},{48,112}... | collective-permute-start | bytes 884744 | tf_op jit(solution)/shard_map/ppermute | solution.py:673
  103.2 20.1 %collective-permute-start.10 = (bf16[128,1152]{1,0:T(8,128)(2,1)S(1)}, bf16[128,1152]{1,0:T(8,128)(2,1)S(1)}, u32[]{:S(2)}, u32[]{:S(2)}) collective-permute-start(bf16[128,1152]{1,0:T(8,128)(2,1)S(1)} %get-tuple-element.28), channel_id=1, source_target_pairs={{480,0},{496,16},{0,32},{16,48},{32,64},{48,80},{64,96},{80,112},{... | collective-permute-start | bytes 884744 | tf_op jit(solution)/shard_map/ppermute | solution.py:673
  123.4 15.5 %collective-permute-start.11 = (bf16[320,1152]{1,0:T(8,128)(2,1)S(1)}, bf16[320,1152]{1,0:T(8,128)(2,1)S(1)}, u32[]{:S(2)}, u32[]{:S(2)}) collective-permute-start(bf16[320,1152]{1,0:T(8,128)(2,1)S(1)} %join.1), channel_id=1, source_target_pairs={{0,16},{16,0},{32,48},{48,32},{64,80},{80,64},{96,112},{112,96},{1... | collective-permute-start | bytes 2211848 | tf_op jit(solution)/shard_map/ppermute | solution.py:677
  130.7 0.8 copy-start.4
  131.5 0.7 copy-start.6
  132.2 1.0 copy-start.5
  133.3 0.9 copy-start.7

commit v7 on v5

--- a/solution.py
+++ b/solution.py
@@ -415,7 +415,7 @@
     ctx, own_block, offsets, padded, sets, tops, keep = attend_start(q_ref, scores)
     ids = ids_ref[...]
     own_row = table_row(own_block)
-    for span, ref, step in ((NEAR, near_ref, 384), (FAR, far_ref, 256)):
+    for span, ref, step in ((NEAR, near_ref, 384), (FAR, far_ref, 512)):
         first, count, slots = span
         one, two = named_columns(span, [ids[0:1]]), named_columns(span, [ids[1:2]])
         members = (one[:, 0:1], two[:, 0:1])
@@ -677,9 +677,10 @@
     sent = gather("far", FAR, others + swapped, y, [], scores)
     served = serve(kv_turned, asked, sent)
     far = exchange(tie(sent, near))
-    mine = [served[0]]
-    for away in AWAYS[1:]:
-        mine.append(level_from(served[AWAYS.index(-away % LEVELS)], away))
+    got = {0: served[0]}
+    for away in (2, 14, 1, 15):
+        got[away] = level_from(served[AWAYS.index(-away % LEVELS)], away)
+    mine = [got[away] for away in AWAYS]
     crossed = swap(join(mine))
     query = q_latent.reshape(2, HEADS, DQK)
     before, state, scores = attend_plane(query, q_blocks, near, far)

time: 136 us -> 136 us (level)
  no operation moved by 1% of the time
where the time goes in v7:
time: 136 us; the launch traced here: 134 us
  starting transfers between devices  61.5 us (45%)
  blocking collectives  28.5 us (21%)
  waiting for transfers between devices  21.7 us (16%)
  Pallas kernels  18 us (13%)
  local copies, waits for them, and re-layouts  3.67 us (3%)
    all_to_all x1, blocking collectives, outer_levels(): lax.all_to_all(chunks, 'ctx', split_axis=0, concat_axis=0, axis_index_gro...  28.5 us
    ppermute x6, starting transfers between devices, level_from(): return lax.ppermute(value, 'ctx', pairs)  19.5 us
    ppermute x6, waiting for transfers between devices, level_from(): return lax.ppermute(value, 'ctx', pairs)  19.3 us
    ppermute x5, starting transfers between devices, swap(): lax.ppermute(value, 'ctx', [(at, at ^ 1) for at in range(2 * LEVELS)])  14.2 us
    all_to_all x2, starting transfers between devices, exchange(): got = lax.all_to_all(parts, 'pb', split_axis=0, concat_axis=0, tiled=True)  14 us
    ppermute x1, starting transfers between devices, two_levels_on(): return lax.ppermute(value, 'ctx', pairs)  6.95 us
    all_to_all x1, starting transfers between devices, local(): y = lax.all_to_all(y, 'pb', split_axis=0, concat_axis=0, tiled=True)  6.77 us
    pallas_call x1, Pallas kernels, attend_plane(): pl.pallas_call(plane_kernel, out_shape=(jax.ShapeDtypeStruct((4, 2 * HEAD...  5.45 us
  transfers between devices with their start and end apart: 15, of which 5 were waited for; matrix products, arithmetic and copies ran while one was open for 2% of the time, Pallas kernels for 8%

profile of v7, /device:TPU:1, one launch (start us, length us, event | category | flops | bytes accessed | tf_op | source)
XLA Modules:
  0.0 134.3 jit_solution(2689518585842601669)
XLA Ops:
  0.6 2.3 %pack.1 = (bf16[4,8,2944]{2,1,0:T(8,128)(2,1)}, bf16[16,144,128]{2,1,0:T(8,128)(2,1)}) custom-call(bf16[576,512]{1,0:T(8,128)(2,1)} %bitcast.6, bf16[32,128]{1,0:T(8,128)(2,1)} %refs_1_.1, bf16[2,8192]{1,0:T(2,128)(2,1)} %refs_2_.1, bf16[2,64]{1,0:T(2,128)(2,1)} %refs_3_.1, s32[2,32]{1,0:T(2,128)} %ids_ref.3), custom_call_target="tpu_custom_call" | custom-call | tf_op jit(solution)/shard_map/pack/pallas_call | solution.py:122
  3.0 28.5 %all_to_all.20 = bf16[4,8,2944]{2,1,0:T(8,128)(2,1)S(1)} all-to-all(bf16[4,8,2944]{2,1,0:T(8,128)(2,1)} %get-tuple-element.14), channel_id=1, replica_groups={{0,128,256,384},{16,144,272,400},{32,160,288,416},{48,176,304,432},{64,..., dimensions={0} | all-to-all | bytes 376832 | tf_op jit(solution)/shard_map/all_to_all | solution.py:660
  31.5 6.8 %all-to-all-start.1 = ((bf16[16,144,128]{2,1,0:T(8,128)(2,1)}), bf16[16,144,128]{2,1,0:T(8,128)(2,1)S(1)}, u32[]{:S(2)}, u32[]{:S(2)}) async-start(bf16[16,144,128]{2,1,0:T(8,128)(2,1)} %get-tuple-element.15), calls=%async_computation.1 | async-start | bytes 1179648 | tf_op jit(solution)/shard_map/all_to_all | solution.py:670
  38.3 7.0 %collective-permute-start.3 = (bf16[32,2944]{1,0:T(8,128)(2,1)S(1)}, bf16[32,2944]{1,0:T(8,128)(2,1)S(1)}, u32[]{:S(2)}, u32[]{:S(2)}) collective-permute-start(bf16[32,2944]{1,0:T(8,128)(2,1)S(1)} %bitcast.8), channel_id=1, source_target_pairs={{64,0},{464,16},{96,32},{496,48},{128,64},{16,80},{160,96},{48,112... | collective-permute-start | bytes 565256 | tf_op jit(solution)/shard_map/ppermute | solution.py:599
  45.3 1.9 %collective-permute-start.2 = (bf16[32,2944]{1,0:T(8,128)(2,1)S(1)}, bf16[32,2944]{1,0:T(8,128)(2,1)S(1)}, u32[]{:S(2)}, u32[]{:S(2)}) collective-permute-start(bf16[32,2944]{1,0:T(8,128)(2,1)S(1)} %bitcast.9), channel_id=1, source_target_pairs={{480,0},{496,16},{0,32},{16,48},{32,64},{48,80},{64,96},{80,112},{... | collective-permute-start | bytes 565256 | tf_op jit(solution)/shard_map/ppermute | solution.py:641
  47.2 4.6 %collective-permute-start.1 = (bf16[32,2944]{1,0:T(8,128)(2,1)S(1)}, bf16[32,2944]{1,0:T(8,128)(2,1)S(1)}, u32[]{:S(2)}, u32[]{:S(2)}) collective-permute-start(bf16[32,2944]{1,0:T(8,128)(2,1)S(1)} %bitcast.10), channel_id=1, source_target_pairs={{32,0},{48,16},{64,32},{80,48},{96,64},{112,80},{128,96},{144,112}... | collective-permute-start | bytes 565256 | tf_op jit(solution)/shard_map/ppermute | solution.py:641
  51.8 4.1 %collective-permute-start = (bf16[32,2944]{1,0:T(8,128)(2,1)S(1)}, bf16[32,2944]{1,0:T(8,128)(2,1)S(1)}, u32[]{:S(2)}, u32[]{:S(2)}) collective-permute-start(bf16[32,2944]{1,0:T(8,128)(2,1)S(1)} %bitcast.11), channel_id=1, source_target_pairs={{0,16},{16,0},{32,48},{48,32},{64,80},{80,64},{96,112},{112,96},{1... | collective-permute-start | bytes 565256 | tf_op jit(solution)/shard_map/ppermute | solution.py:645
  55.8 0.0 all-to-all-done.1.refs_2_.refs_8_.refs_6_
  55.9 0.0 collective-permute-done.3.refs_5_.refs_3_.refs_2_
  55.9 0.0 collective-permute-done.2.refs_4_.refs_2_.refs_1_
  55.9 0.0 collective-permute-done.1.refs_3_.refs_1_.refs_0_
  55.9 0.0 copy-start.1
  55.9 1.0 collective-permute-done.refs_1_.refs_4_
  56.9 1.9 %near.1 = bf16[384,1152]{1,0:T(8,128)(2,1)} custom-call(bf16[32,2944]{1,0:T(8,128)(2,1)S(1)} %bitcast.12, bf16[32,2944]{1,0:T(8,128)(2,1)S(1)} %collective-permute-done.refs_1_.refs_4_, bf16[16,144,128]{2,1,0:T(8,128)(2,1)S(1)} %all-to-all-done.1.refs_2_.refs_8_.refs_6_, bf16[32,2944]{1,0:T(8,128)(2,1)S(1)} %collective-permute-done.1.refs_3_.refs_1_.refs_0_, ...), custom_call_target="tpu_custom_call" | custom-call | flops 113246208 | bytes 3000000 | tf_op jit(solution)/shard_map/near/pallas_call | solution.py:223
  58.8 7.0 %all-to-all-start.2 = ((bf16[16,24,1152]{2,1,0:T(8,128)(2,1)}), bf16[16,24,1152]{2,1,0:T(8,128)(2,1)}, u32[]{:S(2)}, u32[]{:S(2)}) async-start(bf16[16,24,1152]{2,1,0:T(8,128)(2,1)} %bitcast.2), calls=%async_computation.2 | async-start | bytes 1769472 | tf_op jit(solution)/shard_map/all_to_all | solution.py:650
  65.8 3.3 %collective-permute-start.6 = (bf16[32,2944]{1,0:T(8,128)(2,1)S(1)}, bf16[32,2944]{1,0:T(8,128)(2,1)S(1)}, u32[]{:S(2)}, u32[]{:S(2)}) collective-permute-start(bf16[32,2944]{1,0:T(8,128)(2,1)S(1)} %collective-permute-done.3.refs_5_.refs_3_.refs_2_), channel_id=1, source_target_pairs={{0,16},{16,0},{32,48},{48,32},{64,80},{80,64},{96,112},{112,96},{1... | collective-permute-start | bytes 565256 | tf_op jit(solution)/shard_map/ppermute | solution.py:645
  69.1 1.9 %collective-permute-start.5 = (bf16[32,2944]{1,0:T(8,128)(2,1)S(1)}, bf16[32,2944]{1,0:T(8,128)(2,1)S(1)}, u32[]{:S(2)}, u32[]{:S(2)}) collective-permute-start(bf16[32,2944]{1,0:T(8,128)(2,1)S(1)} %collective-permute-done.2.refs_4_.refs_2_.refs_1_), channel_id=1, source_target_pairs={{0,16},{16,0},{32,48},{48,32},{64,80},{80,64},{96,112},{112,96},{1... | collective-permute-start | bytes 565256 | tf_op jit(solution)/shard_map/ppermute | solution.py:645
  71.0 2.4 %collective-permute-start.4 = (bf16[32,2944]{1,0:T(8,128)(2,1)S(1)}, bf16[32,2944]{1,0:T(8,128)(2,1)S(1)}, u32[]{:S(2)}, u32[]{:S(2)}) collective-permute-start(bf16[32,2944]{1,0:T(8,128)(2,1)S(1)} %collective-permute-done.1.refs_3_.refs_1_.refs_0_), channel_id=1, source_target_pairs={{0,16},{16,0},{32,48},{48,32},{64,80},{80,64},{96,112},{112,96},{1... | collective-permute-start | bytes 565256 | tf_op jit(solution)/shard_map/ppermute | solution.py:645
  73.4 0.0 collective-permute-done.6.refs_7_.refs_5_
  73.4 0.0 collective-permute-done.5.refs_6_.refs_4_
  73.4 1.0 collective-permute-done.4.refs_5_.refs_3_
  74.5 1.9 %score.1 = (bf16[16,16,128]{2,1,0:T(8,128)(2,1)S(1)}, f32[16,128]{1,0:T(8,128)S(1)}) custom-call(bf16[32,2944]{1,0:T(8,128)(2,1)S(1)} %bitcast.13, bf16[32,2944]{1,0:T(8,128)(2,1)S(1)} %collective-permute-done.1.refs_3_.refs_1_.refs_0_, bf16[32,2944]{1,0:T(8,128)(2,1)S(1)} %collective-permute-done.2.refs_4_.refs_2_.refs_1_, ...), custom_call_target="tpu_custom_call" | custom-call | flops 536870912 | bytes 2000000 | tf_op jit(solution)/shard_map/score/pallas_call | solution.py:344
  76.4 0.0 copy-done.1
  76.4 0.0 copy-start.2
  76.4 0.9 copy-done.2
  77.4 2.0 %far.1.after_ref = bf16[512,2432]{1,0:T(8,128)(2,1)S(1)} custom-call(bf16[32,2944]{1,0:T(8,128)(2,1)S(1)} %copy-done.2, bf16[32,2944]{1,0:T(8,128)(2,1)S(1)} %collective-permute-done.2.refs_4_.refs_2_.refs_1_, bf16[32,2944]{1,0:T(8,128)(2,1)S(1)} %collective-permute-done.3.refs_5_.refs_3_.refs_2_, ...), custom_call_target="tpu_custom_call" | custom-call | flops 905969664 | bytes 3000000 | tf_op jit(solution)/shard_map/far/pallas_call | solution.py:223
  79.3 1.5 %copy.9.value_ref = bf16[512,2432]{1,0:T(8,128)(2,1)} copy(bf16[512,2432]{1,0:T(8,128)(2,1)S(1)} %far.1.after_ref) | data formatting | bytes 4980736
  80.8 0.0 all-to-all-done.2
  80.8 7.1 %all-to-all-start.3 = ((bf16[16,32,2432]{2,1,0:T(8,128)(2,1)}), bf16[16,32,2432]{2,1,0:T(8,128)(2,1)}, u32[]{:S(2)}, u32[]{:S(2)}) async-start(bf16[16,32,2432]{2,1,0:T(8,128)(2,1)} %bitcast.14), calls=%async_computation.3 | async-start | bytes 4980736 | tf_op jit(solution)/shard_map/all_to_all | solution.py:650
  87.9 0.0 copy-done
  87.9 0.0 copy-start.3
  87.9 1.3 serve.1
  89.2 4.9 %collective-permute-start.7 = (bf16[128,1152]{1,0:T(8,128)(2,1)S(1)}, bf16[128,1152]{1,0:T(8,128)(2,1)S(1)}, u32[]{:S(2)}, u32[]{:S(2)}) collective-permute-start(bf16[128,1152]{1,0:T(8,128)(2,1)S(1)} %get-tuple-element.21), channel_id=1, source_target_pairs={{32,0},{48,16},{64,32},{80,48},{96,64},{112,80},{128,96},{144,112}... | collective-permute-start | bytes 884744 | tf_op jit(solution)/shard_map/ppermute | solution.py:641
  94.1 1.9 %collective-permute-start.8 = (bf16[128,1152]{1,0:T(8,128)(2,1)S(1)}, bf16[128,1152]{1,0:T(8,128)(2,1)S(1)}, u32[]{:S(2)}, u32[]{:S(2)}) collective-permute-start(bf16[128,1152]{1,0:T(8,128)(2,1)S(1)} %get-tuple-element.22), channel_id=1, source_target_pairs={{64,0},{80,16},{96,32},{112,48},{128,64},{144,80},{160,96},{176,11... | collective-permute-start | bytes 884744 | tf_op jit(solution)/shard_map/ppermute | solution.py:641
  96.1 4.3 %collective-permute-start.9 = (bf16[128,1152]{1,0:T(8,128)(2,1)S(1)}, bf16[128,1152]{1,0:T(8,128)(2,1)S(1)}, u32[]{:S(2)}, u32[]{:S(2)}) collective-permute-start(bf16[128,1152]{1,0:T(8,128)(2,1)S(1)} %get-tuple-element.23), channel_id=1, source_target_pairs={{448,0},{464,16},{480,32},{496,48},{0,64},{16,80},{32,96},{48,112}... | collective-permute-start | bytes 884744 | tf_op jit(solution)/shard_map/ppermute | solution.py:641
  100.3 1.9 %collective-permute-start.10 = (bf16[128,1152]{1,0:T(8,128)(2,1)S(1)}, bf16[128,1152]{1,0:T(8,128)(2,1)S(1)}, u32[]{:S(2)}, u32[]{:S(2)}) collective-permute-start(bf16[128,1152]{1,0:T(8,128)(2,1)S(1)} %get-tuple-element.24), channel_id=1, source_target_pairs={{480,0},{496,16},{0,32},{16,48},{32,64},{48,80},{64,96},{80,112},{... | collective-permute-start | bytes 884744 | tf_op jit(solution)/shard_map/ppermute | solution.py:641
  102.3 0.0 collective-permute-done.7.refs_1_
  102.3 10.8 %collective-permute-done.8.refs_2_ = bf16[128,1152]{1,0:T(8,128)(2,1)S(1)} collective-permute-done((bf16[128,1152]{1,0:T(8,128)(2,1)S(1)}, bf16[128,1152]{1,0:T(8,128)(2,1)S(1)}, u32[]{:S(2)}, u32[]{:S(2)}) %collective-permute-start.8) | collective-permute-done | bytes 294944 | tf_op jit(solution)/shard_map/ppermute | solution.py:641
  113.0 0.0 collective-permute-done.9.refs_3_
  113.1 8.5 %collective-permute-done.10.refs_4_ = bf16[128,1152]{1,0:T(8,128)(2,1)S(1)} collective-permute-done((bf16[128,1152]{1,0:T(8,128)(2,1)S(1)}, bf16[128,1152]{1,0:T(8,128)(2,1)S(1)}, u32[]{:S(2)}, u32[]{:S(2)}) %collective-permute-start.10) | collective-permute-done | bytes 294944 | tf_op jit(solution)/shard_map/ppermute | solution.py:641
  121.5 0.1 join.1
  121.6 2.6 %collective-permute-start.11 = (bf16[320,1152]{1,0:T(8,128)(2,1)S(1)}, bf16[320,1152]{1,0:T(8,128)(2,1)S(1)}, u32[]{:S(2)}, u32[]{:S(2)}) collective-permute-start(bf16[320,1152]{1,0:T(8,128)(2,1)S(1)} %join.1), channel_id=1, source_target_pairs={{0,16},{16,0},{32,48},{48,32},{64,80},{80,64},{96,112},{112,96},{1... | collective-permute-start | bytes 2211848 | tf_op jit(solution)/shard_map/ppermute | solution.py:645
  124.1 1.3 reshape.22.q_ref
  125.4 0.4 all-to-all-done.3
  125.9 0.0 copy-done.3
  125.9 5.5 %attend_plane.1 = (f32[4,256,128]{2,1,0:T(8,128)S(1)}, f32[2,256,128]{2,1,0:T(8,128)S(1)}, bf16[2,16384]{1,0:T(2,128)(2,1)}) custom-call(bf16[2,128,576]{2,1,0:T(8,128)(2,1)S(1)} %reshape.22.q_ref, s32[2,32]{1,0:T(2,128)S(1)} %copy-done.3, bf16[384,1152]{1,0:T(8,128)(2,1)} %bitcast.3.after_ref.near_ref, bf16[512,2432]{1,0:T(8,128)(2,1)} %bitcast.5.far_ref), custom_call_target="tpu_custom_call" | custom-call | flops 1660944384 | bytes 4000000 | tf_op jit(solution)/shard_map/attend_plane/pallas_call | solution.py:554
  131.3 0.0 collective-permute-done.11.refs_5_
  131.3 3.0 %attend_column.1 = bf16[2,65536]{1,0:T(2,128)(2,1)} custom-call(bf16[2,128,576]{2,1,0:T(8,128)(2,1)S(1)} %reshape.22.q_ref, s32[2,32]{1,0:T(2,128)S(1)} %copy-done.3, f32[4,256,128]{2,1,0:T(8,128)S(1)} %get-tuple-element.17.before, f32[2,256,128]{2,1,0:T(8,128)S(1)} %get-tuple-element.18.state, bf16[128,1152]{1,0:T(8,128)(2,1)S(1)} %get-tuple-element.20.refs_0_, ...), custom_call_target="tpu_custom_call" | custom-call | flops 754974720 | bytes 3000000 | tf_op jit(solution)/shard_map/attend_column/pallas_call | solution.py:576
  (2 shorter events, 0.0 us)
Async XLA Ops:
  31.5 24.3 %all-to-all-start.1 = ((bf16[16,144,128]{2,1,0:T(8,128)(2,1)}), bf16[16,144,128]{2,1,0:T(8,128)(2,1)S(1)}, u32[]{:S(2)}, u32[]{:S(2)}) async-start(bf16[16,144,128]{2,1,0:T(8,128)(2,1)} %get-tuple-element.15), calls=%async_computation.1 | async-start | bytes 1179648 | tf_op jit(solution)/shard_map/all_to_all | solution.py:670
  38.3 17.6 %collective-permute-start.3 = (bf16[32,2944]{1,0:T(8,128)(2,1)S(1)}, bf16[32,2944]{1,0:T(8,128)(2,1)S(1)}, u32[]{:S(2)}, u32[]{:S(2)}) collective-permute-start(bf16[32,2944]{1,0:T(8,128)(2,1)S(1)} %bitcast.8), channel_id=1, source_target_pairs={{64,0},{464,16},{96,32},{496,48},{128,64},{16,80},{160,96},{48,112... | collective-permute-start | bytes 565256 | tf_op jit(solution)/shard_map/ppermute | solution.py:599
  45.3 10.6 %collective-permute-start.2 = (bf16[32,2944]{1,0:T(8,128)(2,1)S(1)}, bf16[32,2944]{1,0:T(8,128)(2,1)S(1)}, u32[]{:S(2)}, u32[]{:S(2)}) collective-permute-start(bf16[32,2944]{1,0:T(8,128)(2,1)S(1)} %bitcast.9), channel_id=1, source_target_pairs={{480,0},{496,16},{0,32},{16,48},{32,64},{48,80},{64,96},{80,112},{... | collective-permute-start | bytes 565256 | tf_op jit(solution)/shard_map/ppermute | solution.py:641
  47.2 8.7 %collective-permute-start.1 = (bf16[32,2944]{1,0:T(8,128)(2,1)S(1)}, bf16[32,2944]{1,0:T(8,128)(2,1)S(1)}, u32[]{:S(2)}, u32[]{:S(2)}) collective-permute-start(bf16[32,2944]{1,0:T(8,128)(2,1)S(1)} %bitcast.10), channel_id=1, source_target_pairs={{32,0},{48,16},{64,32},{80,48},{96,64},{112,80},{128,96},{144,112}... | collective-permute-start | bytes 565256 | tf_op jit(solution)/shard_map/ppermute | solution.py:641
  51.8 5.1 %collective-permute-start = (bf16[32,2944]{1,0:T(8,128)(2,1)S(1)}, bf16[32,2944]{1,0:T(8,128)(2,1)S(1)}, u32[]{:S(2)}, u32[]{:S(2)}) collective-permute-start(bf16[32,2944]{1,0:T(8,128)(2,1)S(1)} %bitcast.11), channel_id=1, source_target_pairs={{0,16},{16,0},{32,48},{48,32},{64,80},{80,64},{96,112},{112,96},{1... | collective-permute-start | bytes 565256 | tf_op jit(solution)/shard_map/ppermute | solution.py:645
  55.9 20.5 %copy-start.1 = (bf16[32,2944]{1,0:T(8,128)(2,1)}, bf16[32,2944]{1,0:T(8,128)(2,1)S(1)}, u32[]{:S(2)}) copy-start(bf16[32,2944]{1,0:T(8,128)(2,1)S(1)} %collective-permute-done.1.refs_3_.refs_1_.refs_0_) | copy-start | bytes 565252
  58.8 22.0 %all-to-all-start.2 = ((bf16[16,24,1152]{2,1,0:T(8,128)(2,1)}), bf16[16,24,1152]{2,1,0:T(8,128)(2,1)}, u32[]{:S(2)}, u32[]{:S(2)}) async-start(bf16[16,24,1152]{2,1,0:T(8,128)(2,1)} %bitcast.2), calls=%async_computation.2 | async-start | bytes 1769472 | tf_op jit(solution)/shard_map/all_to_all | solution.py:650
  65.8 7.6 %collective-permute-start.6 = (bf16[32,2944]{1,0:T(8,128)(2,1)S(1)}, bf16[32,2944]{1,0:T(8,128)(2,1)S(1)}, u32[]{:S(2)}, u32[]{:S(2)}) collective-permute-start(bf16[32,2944]{1,0:T(8,128)(2,1)S(1)} %collective-permute-done.3.refs_5_.refs_3_.refs_2_), channel_id=1, source_target_pairs={{0,16},{16,0},{32,48},{48,32},{64,80},{80,64},{96,112},{112,96},{1... | collective-permute-start | bytes 565256 | tf_op jit(solution)/shard_map/ppermute | solution.py:645
  69.1 4.4 %collective-permute-start.5 = (bf16[32,2944]{1,0:T(8,128)(2,1)S(1)}, bf16[32,2944]{1,0:T(8,128)(2,1)S(1)}, u32[]{:S(2)}, u32[]{:S(2)}) collective-permute-start(bf16[32,2944]{1,0:T(8,128)(2,1)S(1)} %collective-permute-done.2.refs_4_.refs_2_.refs_1_), channel_id=1, source_target_pairs={{0,16},{16,0},{32,48},{48,32},{64,80},{80,64},{96,112},{112,96},{1... | collective-permute-start | bytes 565256 | tf_op jit(solution)/shard_map/ppermute | solution.py:645
  71.0 3.5 %collective-permute-start.4 = (bf16[32,2944]{1,0:T(8,128)(2,1)S(1)}, bf16[32,2944]{1,0:T(8,128)(2,1)S(1)}, u32[]{:S(2)}, u32[]{:S(2)}) collective-permute-start(bf16[32,2944]{1,0:T(8,128)(2,1)S(1)} %collective-permute-done.1.refs_3_.refs_1_.refs_0_), channel_id=1, source_target_pairs={{0,16},{16,0},{32,48},{48,32},{64,80},{80,64},{96,112},{112,96},{1... | collective-permute-start | bytes 565256 | tf_op jit(solution)/shard_map/ppermute | solution.py:645
  76.4 0.9 copy-start.2
  80.8 7.1 %copy-start = (bf16[512,576]{0,1:T(8,128)(2,1)S(1)}, bf16[512,576]{0,1:T(8,128)(2,1)}, u32[]{:S(2)}) copy-start(bf16[512,576]{0,1:T(8,128)(2,1)} %param.7) | copy-start | bytes 1769476
  80.8 45.0 %all-to-all-start.3 = ((bf16[16,32,2432]{2,1,0:T(8,128)(2,1)}), bf16[16,32,2432]{2,1,0:T(8,128)(2,1)}, u32[]{:S(2)}, u32[]{:S(2)}) async-start(bf16[16,32,2432]{2,1,0:T(8,128)(2,1)} %bitcast.14), calls=%async_computation.3 | async-start | bytes 4980736 | tf_op jit(solution)/shard_map/all_to_all | solution.py:650
  87.9 38.0 %copy-start.3 = (s32[2,32]{1,0:T(2,128)S(1)}, s32[2,32]{1,0:T(2,128)}, u32[]{:S(2)}) copy-start(s32[2,32]{1,0:T(2,128)} %ids_ref.3) | copy-start | bytes 772
  89.2 13.0 %collective-permute-start.7 = (bf16[128,1152]{1,0:T(8,128)(2,1)S(1)}, bf16[128,1152]{1,0:T(8,128)(2,1)S(1)}, u32[]{:S(2)}, u32[]{:S(2)}) collective-permute-start(bf16[128,1152]{1,0:T(8,128)(2,1)S(1)} %get-tuple-element.21), channel_id=1, source_target_pairs={{32,0},{48,16},{64,32},{80,48},{96,64},{112,80},{128,96},{144,112}... | collective-permute-start | bytes 884744 | tf_op jit(solution)/shard_map/ppermute | solution.py:641
  94.1 18.9 %collective-permute-start.8 = (bf16[128,1152]{1,0:T(8,128)(2,1)S(1)}, bf16[128,1152]{1,0:T(8,128)(2,1)S(1)}, u32[]{:S(2)}, u32[]{:S(2)}) collective-permute-start(bf16[128,1152]{1,0:T(8,128)(2,1)S(1)} %get-tuple-element.22), channel_id=1, source_target_pairs={{64,0},{80,16},{96,32},{112,48},{128,64},{144,80},{160,96},{176,11... | collective-permute-start | bytes 884744 | tf_op jit(solution)/shard_map/ppermute | solution.py:641
  96.1 17.0 %collective-permute-start.9 = (bf16[128,1152]{1,0:T(8,128)(2,1)S(1)}, bf16[128,1152]{1,0:T(8,128)(2,1)S(1)}, u32[]{:S(2)}, u32[]{:S(2)}) collective-permute-start(bf16[128,1152]{1,0:T(8,128)(2,1)S(1)} %get-tuple-element.23), channel_id=1, source_target_pairs={{448,0},{464,16},{480,32},{496,48},{0,64},{16,80},{32,96},{48,112}... | collective-permute-start | bytes 884744 | tf_op jit(solution)/shard_map/ppermute | solution.py:641
  100.3 21.2 %collective-permute-start.10 = (bf16[128,1152]{1,0:T(8,128)(2,1)S(1)}, bf16[128,1152]{1,0:T(8,128)(2,1)S(1)}, u32[]{:S(2)}, u32[]{:S(2)}) collective-permute-start(bf16[128,1152]{1,0:T(8,128)(2,1)S(1)} %get-tuple-element.24), channel_id=1, source_target_pairs={{480,0},{496,16},{0,32},{16,48},{32,64},{48,80},{64,96},{80,112},{... | collective-permute-start | bytes 884744 | tf_op jit(solution)/shard_map/ppermute | solution.py:641
  121.6 9.7 %collective-permute-start.11 = (bf16[320,1152]{1,0:T(8,128)(2,1)S(1)}, bf16[320,1152]{1,0:T(8,128)(2,1)S(1)}, u32[]{:S(2)}, u32[]{:S(2)}) collective-permute-start(bf16[320,1152]{1,0:T(8,128)(2,1)S(1)} %join.1), channel_id=1, source_target_pairs={{0,16},{16,0},{32,48},{48,32},{64,80},{80,64},{96,112},{112,96},{1... | collective-permute-start | bytes 2211848 | tf_op jit(solution)/shard_map/ppermute | solution.py:645
